TPU v7x, 32 devices: a whole 2x2x4 slice. The times are simulated.
32 devices in a mesh: batch: 4 (over z), rows: 4 (over y, x), section: 2 (over core).
Axes of the slice: x: 2, y: 2, z: 4, core: 2. Of those that a mesh axis runs over, the one named last changes fastest.
Arguments:
- features: bfloat16 [16, 16, 32, 1536], P('batch', 'rows'), may hold values from -6 to 6, as said below
- dw_kernel: bfloat16 [7, 7, 1536], replicated, may hold values from -0.875 to 0.875
- ln_gain: bfloat16 [1536], replicated, may hold values from 0.25 to 1.75
- widening_pointwise_matrix: bfloat16 [1536, 3072], P(None, 'section'), may hold values from -0.15625 to 0.15625
- w_reduce: bfloat16 [3072, 1536], P('section'), may hold values from -0.109375 to 0.109375
- layer_branch_scale: bfloat16 [1536], replicated, may hold values from 0.5 to 2
- p_expand: bfloat16 [1536, 2048], P(None, 'section'), may hold values from -0.15625 to 0.15625
- p_kernel: bfloat16 [9, 2048, 256], P(None, 'section'), may hold values from -0.046875 to 0.046875
- region_ids: int32 [16, 16, 32], P('batch', 'rows'), may hold values from 0 to 63, as said below
- owner_slot: int32 [4, 256], P('batch'), may hold values from 0 to 255, each once within a row
- partner: int32 [16, 64], P('batch'), may hold values from 0 to 63
- key_embed: bfloat16 [1024, 256], P(('batch', 'rows')), may hold values from -6 to 6
Outputs:
- region_embed: float32 [1024, 256], P(('batch', 'rows'))
- region_loss: float32 [1024], P(('batch', 'rows'))
Inputs may be any that keep to these rules, and one draw needn't show every extreme that they name: `features`: exactly one image other than image 0 has all its entries zero. `region_ids`: each image uses regions 0 to K - 1 for its own K of at least 16, every one of them on some pixel; image 0 uses all 64. `owner_slot`: each row is a permutation of the slots of one batch index.
All inputs are finite; a program needn't handle non-finite values.
Results may differ from a plain program's by a relative error of at most 0.0024.
Values may be sent and summed in bfloat16 or wider, within the bound.
No kernel may reach another device: no remote copies, remote signals or barrier semaphores. Data moves between devices by JAX's collectives and lax.ppermute only.
A program may use at most 128 MiB of HBM per device.

v0:
```python
import functools

import jax
import jax.numpy as jnp
from jax import lax
from jax.experimental import pallas as pl
from jax.experimental.pallas import tpu as pltpu
from jax.sharding import PartitionSpec as P

REG = 64
LANES = 128
STRIP = 4
CHUNKS = 2

sharpness_divisor = 0.1
ln_eps = 1e-06
norm_eps = 1e-06

VMEM = pl.BlockSpec(memory_space=pltpu.VMEM)
SMEM = pl.BlockSpec(memory_space=pltpu.SMEM)
f32 = jnp.float32
bf16 = jnp.bfloat16


def call(kernel, outs, in_specs, scratch, limit, flops, nbytes):
    return pl.pallas_call(
        kernel,
        out_shape=outs,
        in_specs=in_specs,
        out_specs=[VMEM] * len(outs),
        scratch_shapes=scratch,
        compiler_params=pltpu.CompilerParams(vmem_limit_bytes=limit),
        cost_estimate=pl.CostEstimate(flops=flops, bytes_accessed=nbytes, transcendentals=0),
    )


def dot(a, b):
    return jnp.dot(a, b, preferred_element_type=f32)


def dot_nt(a, b):
    return lax.dot_general(a, b, (((1,), (1,)), ((), ())), preferred_element_type=f32)


def split3(x):
    hi = x.astype(bf16)
    rest = x - hi.astype(f32)
    mid = rest.astype(bf16)
    return hi, mid, (rest - mid.astype(f32)).astype(bf16)


def stage_kernel(geo, pos_ref, feat_ref, ids_ref, *refs):
    shards, chunks, parts = geo
    blocks, line = refs[: shards * chunks], refs[shards * chunks]
    row, section = pos_ref[0], pos_ref[3]
    images, pixels, chans = feat_ref.shape
    span = blocks[0].shape[1]
    for c in range(chunks):
        lanes = pl.ds(pl.multiple_of(section * (chans // 2) + c * span, LANES), span)
        for k in range(shards):
            blocks[c * shards + k][0:pixels, :] = feat_ref[(row ^ k) // parts, :, lanes]
    line[...] = jnp.full(line.shape, -1.0, f32)
    shard_rows, width = ids_ref.shape[1:]
    for i in range(images):
        line[i * shard_rows : (i + 1) * shard_rows, 0:width] = ids_ref[i].astype(f32)
    for k in range(shards):
        blocks[(chunks - 1) * shards + k][pixels:, :] = line[...].astype(bf16)


def join_kernel(*refs):
    start = 0
    for ref in refs[:-1]:
        refs[-1][start : start + ref.shape[0], :] = ref[...]
        start += ref.shape[0]


def join(*arrays):
    rows = sum(x.shape[0] for x in arrays)
    shape = jax.ShapeDtypeStruct((rows, arrays[0].shape[1]), arrays[0].dtype)
    joined = call(join_kernel, [shape], [VMEM] * len(arrays), [], 1 << 20, 0, rows * 1024)(*arrays)
    return joined[0]


def add_kernel(a_ref, b_ref, out_ref):
    out_ref[...] = a_ref[...] + b_ref[...]


def conv_kernel(geo, pos_ref, *refs):
    shards, shard_rows, width, out_rows, first_lane = geo
    blocks = refs[:shards]
    w_ref, taps, img_ref, xpad, wide = refs[shards:]
    chunk = taps.shape[1]
    row, first_row, col0 = pos_ref[0], pos_ref[1], pos_ref[2]
    base = pos_ref[3] * (w_ref.shape[2] // 2) + first_lane
    height = shards * shard_rows
    pixels = shard_rows * width
    cols = xpad.shape[1]
    out_pixels = out_rows * width
    step_rows = STRIP

    xpad[0:3] = jnp.zeros((3, cols, LANES), f32)
    xpad[height + 3 : height + 6] = jnp.zeros((3, cols, LANES), f32)
    for y in range(3, height + 3):
        xpad[y, 0:8] = jnp.zeros((8, LANES), f32)
        xpad[y, 8 + width : 16 + width] = jnp.zeros((8, LANES), f32)

    def group(g, carry):
        lanes = pl.ds(pl.multiple_of(g * LANES, LANES), LANES)
        for k in range(shards):
            value = blocks[k][0:pixels, lanes].astype(f32).reshape(shard_rows, width, LANES)
            xpad[pl.ds(3 + (row ^ k) * shard_rows, shard_rows), 8 : 8 + width, :] = value
        for dy in range(7):
            w = w_ref[dy, :, pl.ds(pl.multiple_of(base + g * LANES, LANES), LANES)].astype(f32)
            for dx in range(7):
                wide[dy * 7 + dx] = jnp.broadcast_to(w[dx : dx + 1], (8, LANES))

        def strip(i, carry):
            top = first_row + i * step_rows
            acc = [jnp.zeros((width // 8, 8, LANES), f32) for _ in range(step_rows)]
            for r in range(step_rows + 6):
                for dx in range(7):
                    v = xpad[top + r, pl.ds(col0 + dx, width), :].reshape(width // 8, 8, LANES)
                    for j in range(step_rows):
                        dy = r - j
                        if 0 <= dy < 7:
                            acc[j] = acc[j] + v * wide[dy * 7 + dx][None]
            for j in range(step_rows):
                start = pl.multiple_of((i * step_rows + j) * width, width)
                taps[pl.ds(start, width), lanes] = acc[j].reshape(width, LANES)
            return carry

        return lax.fori_loop(0, out_rows // step_rows, strip, carry)

    lax.fori_loop(0, chunk // LANES, group, 0)

    for k in range(shards):
        start = (row ^ k) * pixels - first_row * width

        @pl.when((start >= 0) & (start < out_pixels))
        def _():
            img_ref[pl.ds(pl.multiple_of(start, pixels), pixels), :] = blocks[k][0:pixels, :]


def block_kernel(geo, pos_ref, *refs):
    first, pixels, chunks = geo
    own, other, img = refs[:chunks], refs[chunks : 2 * chunks], refs[2 * chunks : 3 * chunks]
    gain_ref, scale_ref, w1_ref, w2_ref, z_ref, send_ref, normed, inner = refs[3 * chunks :]
    chans, hid = w1_ref.shape
    half = chans // 2
    width = half // chunks
    section = pos_ref[3]
    rows = slice(first, first + pixels)
    values = [ref[rows, :] for ref in own + other]
    mean = sum(jnp.sum(v, axis=1, keepdims=True) for v in values) * (1.0 / chans)
    values = [v - mean for v in values]
    spread = sum(jnp.sum(v * v, axis=1, keepdims=True) for v in values) * (1.0 / chans)
    inv = lax.rsqrt(spread + ln_eps)
    gains = gain_ref[...].astype(f32).reshape(1, chans)
    scales = scale_ref[...].astype(f32).reshape(1, chans)
    for c in range(chunks):
        lanes = slice(c * width, (c + 1) * width)
        for side, v in ((section, values[c]), (1 - section, values[chunks + c])):
            start = c * width
            gain = jnp.where(side == 0, gains[:, start : start + width], gains[:, half + start : half + start + width])
            normed[pl.ds(side, 1), :, lanes] = (v * inv * gain).astype(bf16)[None]
    step = 256
    for i in range(hid // step):
        cols = slice(i * step, (i + 1) * step)
        h = dot(normed[0], w1_ref[0:half, cols]) + dot(normed[1], w1_ref[half:chans, cols])
        inner[:, cols] = (0.5 * h * (1.0 + lax.erf(h * 0.7071067811865476))).astype(bf16)
    step = width if width % 256 else 256
    for i in range(chans // step):
        cols = slice(i * step, (i + 1) * step)
        side, start = divmod(i * step, half)
        c, start = divmod(start, width)
        keep = jnp.where(section == side, 1.0, 0.0)
        z = dot(inner[...], w2_ref[:, cols]) * scales[:, cols]
        z = z + img[c][rows, start : start + step].astype(f32) * keep
        z_ref[:, cols] = z
        send_ref[:, cols] = z.astype(bf16)


def expand_kernel(z_ref, other_ref, pe_ref, out_ref, block):
    block[...] = (z_ref[...] + other_ref[...].astype(f32)).astype(bf16)
    step = 256
    for i in range(pe_ref.shape[1] // step):
        cols = slice(i * step, (i + 1) * step)
        out_ref[:, cols] = jnp.maximum(dot(block[...], pe_ref[:, cols]), 0.0).astype(bf16)


def prep_kernel(geo, pos_ref, *refs):
    shards, shard_rows, width, out_pixels, images, batches, per_key, parts = geo
    ids = refs[:shards]
    owner_ref, partner_ref, hot_ref, pick_ref, own_ref, flat = refs[shards:]
    row, first_row, batch, first_slot = pos_ref[0], pos_ref[1], pos_ref[4], pos_ref[5]
    pixels = shard_rows * width
    ids = [ref[pixels:, 0:LANES].astype(f32) for ref in ids]
    owned = own_ref.shape[0]
    slots = images * REG
    image = row // parts
    flat[...] = jnp.full(flat.shape, -1.0, f32)
    for k in range(shards):
        start = pl.multiple_of((1 + (row ^ k)) * pixels, LANES)
        number = lax.broadcasted_iota(jnp.int32, ids[k].shape, 0)
        inside = lax.broadcasted_iota(jnp.int32, ids[k].shape, 1) < width
        for y in range(shard_rows):
            keep = inside & (number == image * shard_rows + y)
            mine = jnp.sum(jnp.where(keep, ids[k], 0.0), axis=0, keepdims=True)
            mine = jnp.broadcast_to(mine, (8, LANES))
            mine = pltpu.roll(mine, y * width, 1) if y else mine
            line = mine if y == 0 else line + mine
        flat[0:8, pl.ds(start, pixels)] = line
    total = flat.shape[1]
    whole = jnp.broadcast_to(flat[0:1, :], (8, total))
    lane = lax.broadcasted_iota(jnp.int32, (8, total), 1)
    col = lane % width
    region = lax.broadcasted_iota(jnp.int32, (REG, out_pixels), 0).astype(f32)
    start = pl.multiple_of(pixels + first_row * width, LANES)
    for dy in range(3):
        for dx in range(3):
            off = (dy - 1) * width + dx - 1
            moved = whole if off == 0 else pltpu.roll(whole, off % total, 1)
            if dx == 0:
                moved = jnp.where(col == width - 1, -1.0, moved)
            if dx == 2:
                moved = jnp.where(col == 0, -1.0, moved)
            flat[8:16, :] = moved
            line = flat[8:9, pl.ds(start, out_pixels)]
            tap = dy * 3 + dx
            hot_ref[tap * REG : (tap + 1) * REG, :] = jnp.where(region == line, 1.0, 0.0).astype(bf16)
    slot = lax.broadcasted_iota(jnp.int32, (owned, slots), 1)
    want = lax.broadcasted_iota(jnp.int32, (owned, slots), 0) + first_slot
    pick = owner_ref[...] == want
    pick_ref[...] = jnp.where(pick, 1.0, 0.0).astype(bf16)
    one_region = lax.broadcasted_iota(jnp.int32, (REG, LANES), 0).astype(f32)
    tallies = []
    for i in range(images):
        tally = jnp.zeros((REG, LANES), f32)
        for k in range(shards):
            for y in range(i * shard_rows, (i + 1) * shard_rows):
                tally = tally + jnp.where(one_region == ids[k][y : y + 1, :], 1.0, 0.0)
        tallies.append(tally)
    tally = jnp.concatenate(tallies, axis=0).astype(bf16)
    count = dot_nt(jnp.ones((8, LANES), bf16), tally)[0:1]
    mates = jnp.concatenate([partner_ref[i : i + 1, :] for i in range(images)], axis=1)
    mate = (batch * images + slot // REG) * REG + mates
    block = mate // per_key
    place = ((block % shards) ^ row) * batches + ((block // shards) ^ batch)
    place = place * per_key + mate % per_key
    place = jnp.sum(jnp.where(pick, place, 0).astype(f32), axis=1, keepdims=True)
    number = jnp.sum(jnp.where(pick, count, 0.0), axis=1, keepdims=True)
    side = lax.broadcasted_iota(jnp.int32, (owned, LANES), 1)
    own_ref[...] = jnp.where(side == 0, place, jnp.where(side == 1, number, 0.0))


def project_kernel(z_ref, other_ref, first_ref, pe_ref, pk_ref, hot_ref, out_ref, block, hidden):
    before = first_ref.shape[0]
    pixels = z_ref.shape[0]
    taps = pk_ref.shape[0]
    block[...] = (z_ref[...] + other_ref[...].astype(f32)).astype(bf16)
    step = 256
    acc = jnp.zeros((2 * REG, out_ref.shape[1]), f32)
    for i in range(pe_ref.shape[1] // step):
        cols = slice(i * step, (i + 1) * step)
        hidden[i, 0:before, :] = first_ref[:, cols]
        h = jnp.maximum(dot(block[...], pe_ref[:, cols]), 0.0)
        hidden[i, before : before + pixels, :] = h.astype(bf16)
        sums = dot(hot_ref[...], hidden[i])
        hi = sums.astype(bf16)
        lo = (sums - hi.astype(f32)).astype(bf16)
        for t in range(taps):
            rows = slice(t * REG, (t + 1) * REG)
            both = jnp.concatenate([hi[rows], lo[rows]], axis=0)
            acc = acc + dot(both, pk_ref[t, cols, :])
    out_ref[...] = acc[0:REG] + acc[REG:]


def loss_kernel(geo, *refs):
    shards, parts = geo
    sums, row = refs[1 : shards + 1], refs[0][0]
    pick_ref, own_ref = refs[shards + 1 : shards + 3]
    embed_ref, loss_ref, table = refs[-3:]
    if parts > 1:
        table[...] = jnp.zeros(table.shape, f32)
    for k in range(shards):
        place = pl.ds(pl.multiple_of(((row ^ k) // parts) * REG, REG), REG)
        value = sums[k][...]
        table[place, :] = value if parts == 1 else table[place, :] + value
    pick = pick_ref[...]
    hi, mid, lo = split3(table[...])
    ordered = dot(pick, hi) + dot(pick, mid) + dot(pick, lo)
    unit = ordered * lax.rsqrt(jnp.sum(ordered * ordered, axis=1, keepdims=True) + norm_eps)
    embed_ref[...] = unit
    owned = unit.shape[0]
    keys = jnp.concatenate([ref[...] for ref in refs[shards + 3 : -3]], axis=0)
    wide = keys.astype(f32)
    square = wide * wide
    square_hi = square.astype(bf16)
    square_lo = (square - square_hi.astype(f32)).astype(bf16)
    ones = jnp.ones((16, keys.shape[1]), bf16)
    length = dot_nt(ones, square_hi)[0:1] + dot_nt(ones, square_lo)[0:1]
    three = dot_nt(jnp.concatenate(split3(unit), axis=0), keys)
    logits = three[0:owned] + three[owned : 2 * owned] + three[2 * owned :]
    logits = logits * (lax.rsqrt(length + norm_eps) / sharpness_divisor)
    total = jnp.log(jnp.sum(jnp.exp(logits), axis=1, keepdims=True))
    column = lax.broadcasted_iota(jnp.int32, logits.shape, 1).astype(f32)
    match = jnp.sum(jnp.where(column == own_ref[:, 0:1], logits, 0.0), axis=1, keepdims=True)
    loss = jnp.where(own_ref[:, 1:2] > 0.5, total - match, 0.0)
    line = lax.broadcasted_iota(jnp.int32, (owned, owned), 0)
    other = lax.broadcasted_iota(jnp.int32, (owned, owned), 1)
    loss_ref[...] = jnp.sum(jnp.where(line == other, loss, 0.0), axis=0, keepdims=True)


def swap(x, axis, bit):
    return lax.ppermute(x, axis, [(i, i ^ bit) for i in range(lax.axis_size(axis))])


def body(
    features,
    dw_kernel,
    ln_gain,
    widening_pointwise_matrix,
    w_reduce,
    layer_branch_scale,
    p_expand,
    p_kernel,
    region_ids,
    owner_slot,
    partner,
    key_embed,
):
    images, shard_rows, width, chans = features.shape
    shards = lax.axis_size("rows")
    batches = lax.axis_size("batch")
    row = lax.axis_index("rows")
    batch = lax.axis_index("batch")
    section = lax.axis_index("section")
    half = chans // lax.axis_size("section")
    parts = shards // images
    out_rows = shards * shard_rows // parts
    pixels = shard_rows * width
    out_pixels = out_rows * width
    slots = images * REG
    owned = slots // shards
    out_dim = p_kernel.shape[2]
    mib = 1 << 20
    span = half // CHUNKS

    w1, w2, pe, pk = widening_pointwise_matrix, w_reduce, p_expand, p_kernel
    first_row = (row % parts) * out_rows
    spot = jnp.stack(
        [row, first_row, jnp.int32(5), section, batch, row * owned]
    ).astype(jnp.int32)

    tail = -(-images * shard_rows // 16) * 16
    sizes = [pixels] * (CHUNKS - 1) + [pixels + tail]
    parcels = call(
        functools.partial(stage_kernel, (shards, CHUNKS, parts)),
        [jax.ShapeDtypeStruct((size, span), bf16) for size in sizes for _ in range(shards)],
        [SMEM, VMEM, VMEM],
        [pltpu.VMEM((tail, span), f32)],
        mib,
        0,
        shards * pixels * half * 4,
    )(spot, features.reshape(images, pixels, chans), region_ids)

    pieces = [key_embed]
    steps = []
    for axis, size in (("batch", batches), ("rows", shards)):
        steps += [(axis, 1 << n) for n in range(size.bit_length() - 1)]
    share = -(-len(steps) // 4)

    def key_step():
        for axis, bit in (steps.pop(0) for _ in range(min(share, len(steps)))):
            whole = pieces[0] if len(pieces) == 1 else join(*pieces)
            pieces.append(swap(whole, axis, bit))

    def after(here, *done):
        return lax.optimization_barrier((here, *done))[0]

    got = []
    for c in range(CHUNKS):
        blocks = parcels[c * shards : (c + 1) * shards]
        got.append([blocks[0]] + [swap(blocks[k], "rows", k) for k in range(1, shards)])
    key_step()

    own, other, img = [], [], []
    for c in range(CHUNKS):
        here = after(spot, pieces[-1], *own) if c else spot
        taps, image = call(
            functools.partial(conv_kernel, (shards, shard_rows, width, out_rows, c * span)),
            [
                jax.ShapeDtypeStruct((out_pixels, span), f32),
                jax.ShapeDtypeStruct((out_pixels, span), bf16),
            ],
            [SMEM] + [VMEM] * (shards + 1),
            [
                pltpu.VMEM((shards * shard_rows + 6, width + 16, LANES), f32),
                pltpu.VMEM((49, 8, LANES), f32),
            ],
            3 * mib,
            out_pixels * span * 98 * 100,
            out_pixels * span * 10,
        )(here, *got[c], dw_kernel)
        own.append(taps)
        img.append(image)
        other.append(swap(taps, "section", 1))

    hot, pick, facts = call(
        functools.partial(
            prep_kernel,
            (shards, shard_rows, width, out_pixels, images, batches, key_embed.shape[0], parts),
        ),
        [
            jax.ShapeDtypeStruct((9 * REG, out_pixels), bf16),
            jax.ShapeDtypeStruct((owned, slots), bf16),
            jax.ShapeDtypeStruct((owned, LANES), f32),
        ],
        [SMEM] + [VMEM] * (shards + 2),
        [pltpu.VMEM((16, (shards + 2) * pixels), f32)],
        2 * mib,
        10**8,
        10**6,
    )(spot, *got[-1], owner_slot, partner)

    pieces[-1] = after(pieces[-1], *own)
    key_step()

    hid = w1.shape[1]
    part_pixels = out_pixels // 2
    z, z_other = [], []
    for p in range(2):
        here = after(spot, hot, pieces[-1], *z) if p else after(spot, hot)
        if p:
            key_step()
        mine, send = call(
            functools.partial(block_kernel, (p * part_pixels, part_pixels, CHUNKS)),
            [
                jax.ShapeDtypeStruct((part_pixels, chans), f32),
                jax.ShapeDtypeStruct((part_pixels, chans), bf16),
            ],
            [SMEM] + [VMEM] * (3 * CHUNKS + 4),
            [pltpu.VMEM((2, part_pixels, half), bf16), pltpu.VMEM((part_pixels, hid), bf16)],
            8 * mib,
            4 * part_pixels * hid * chans,
            4 * hid * chans,
        )(here, *own, *other, *img, ln_gain, layer_branch_scale, w1, w2)
        z.append(mine)
        z_other.append(swap(send, "section", 1))
    z[0] = after(z[0], pieces[-1])
    pieces[-1] = after(pieces[-1], z[1])
    key_step()

    hidden = pe.shape[1]
    (hid_a,) = call(
        expand_kernel,
        [jax.ShapeDtypeStruct((part_pixels, hidden), bf16)],
        [VMEM] * 3,
        [pltpu.VMEM((part_pixels, chans), bf16)],
        6 * mib,
        2 * part_pixels * hidden * chans,
        2 * hidden * chans,
    )(z[0], z_other[0], pe)
    (pooled,) = call(
        project_kernel,
        [jax.ShapeDtypeStruct((REG, out_dim), f32)],
        [VMEM] * 6,
        [
            pltpu.VMEM((part_pixels, chans), bf16),
            pltpu.VMEM((hidden // 256, out_pixels, 256), bf16),
        ],
        8 * mib,
        2 * part_pixels * hidden * chans + 4 * 9 * REG * hidden * out_pixels,
        4 * hidden * chans,
    )(z[1], z_other[1], hid_a, pe, pk, hot)
    (pooled,) = call(
        add_kernel,
        [jax.ShapeDtypeStruct((REG, out_dim), f32)],
        [VMEM] * 2,
        [],
        mib,
        10**5,
        10**5,
    )(pooled, swap(pooled, "section", 1))
    sums = [pooled] + [swap(pooled, "rows", k) for k in range(1, shards)]

    embed, loss = call(
        functools.partial(loss_kernel, (shards, parts)),
        [jax.ShapeDtypeStruct((owned, out_dim), f32), jax.ShapeDtypeStruct((1, owned), f32)],
        [SMEM] + [VMEM] * (shards + 2 + len(pieces)),
        [pltpu.VMEM((slots, out_dim), f32)],
        6 * mib,
        10**8,
        10**6,
    )(spot, *sums, pick, facts, *pieces)
    return embed, loss.reshape(owned)


def solution(mesh):
    in_specs = (
        P("batch", "rows", None, None),
        P(),
        P(),
        P(None, "section"),
        P("section", None),
        P(),
        P(None, "section"),
        P(None, "section", None),
        P("batch", "rows", None),
        P("batch", None),
        P("batch", None),
        P(("batch", "rows"), None),
    )
    out_specs = (P(("batch", "rows"), None), P(("batch", "rows")))
    return jax.shard_map(body, mesh=mesh, in_specs=in_specs, out_specs=out_specs, check_vma=False)
```

profile of v0, /device:TPU:0, one launch (start us, length us, event | category | flops | bytes accessed | tf_op | source)
XLA Modules:
  0.0 56.9 jit_solution(17665229054757445377)
XLA Ops:
  0.6 0.1 stack.20.pos_ref.refs_0_
  0.7 1.4 %copy-done.1 = bf16[4,4,32,1536]{3,2,1,0:T(8,128)(2,1)S(1)} copy-done((bf16[4,4,32,1536]{3,2,1,0:T(8,128)(2,1)S(1)}, bf16[4,4,32,1536]{3,2,1,0:T(8,128)(2,1)}, u32[]{:S(2)}) %copy-start.1) | copy-done | bytes 1572888
  2.1 0.7 %copy-done.5 = s32[4,4,32]{2,1,0:T(4,128)S(1)} copy-done((s32[4,4,32]{2,1,0:T(4,128)S(1)}, s32[4,4,32]{2,1,0:T(4,128)}, u32[]{:S(2)}) %copy-start.5) | copy-done | bytes 2072
  2.8 0.6 %shard_map.131 = (bf16[128,384]{1,0:T(8,128)(2,1)S(1)}, bf16[128,384]{1,0:T(8,128)(2,1)S(1)}, bf16[128,384]{1,0:T(8,128)(2,1)S(1)}, bf16[128,384]{1,0:T(8,128)(2...) custom-call(s32[6]{0:T(128)S(1)} %stack.20.pos_ref.refs_0_, ...), custom_call_target="tpu_custom_call" | custom-call | bytes 1572864 | tf_op jit(solution)/shard_map/pallas_call | solution.py:357
  3.5 3.0 %collective-permute-start.4 = (bf16[128,384]{1,0:T(8,128)(2,1)S(1)}, bf16[128,384]{1,0:T(8,128)(2,1)S(1)}, u32[]{:S(2)}, u32[]{:S(2)}) collective-permute-start(bf16[128,384]{1,0:T(8,128)(2,1)S(1)} %get-tuple-element.35), channel_id=1, source_target_pairs={{0,2},{2,0},{4,6},{6,4},{1,3},{3,1},{5,7},{7,5},{8,10},{10,8},{12,... | collective-permute-start | bytes 294920 | tf_op jit(solution)/shard_map/ppermute | solution.py:315
  6.5 1.5 %collective-permute-start.5 = (bf16[128,384]{1,0:T(8,128)(2,1)S(1)}, bf16[128,384]{1,0:T(8,128)(2,1)S(1)}, u32[]{:S(2)}, u32[]{:S(2)}) collective-permute-start(bf16[128,384]{1,0:T(8,128)(2,1)S(1)} %get-tuple-element.36), channel_id=1, source_target_pairs={{0,4},{2,6},{4,0},{6,2},{1,5},{3,7},{5,1},{7,3},{8,12},{10,14},{12... | collective-permute-start | bytes 294920 | tf_op jit(solution)/shard_map/ppermute | solution.py:315
  8.0 0.0 collective-permute-start.6
  8.0 2.0 %collective-permute-start.3 = (bf16[64,256]{1,0:T(8,128)(2,1)}, bf16[64,256]{1,0:T(8,128)(2,1)S(1)}, u32[]{:S(2)}, u32[]{:S(2)}) collective-permute-start(bf16[64,256]{1,0:T(8,128)(2,1)} %refs_7_.5), channel_id=1, source_target_pairs={{0,8},{8,0},{16,24},{24,16},{1,9},{9,1},{17,25},{25,17},{2,10},{10... | collective-permute-start | bytes 98312 | tf_op jit(solution)/shard_map/ppermute | solution.py:315
  10.0 1.5 %collective-permute-start = (bf16[144,384]{1,0:T(8,128)(2,1)S(1)}, bf16[144,384]{1,0:T(8,128)(2,1)S(1)}, u32[]{:S(2)}, u32[]{:S(2)}) collective-permute-start(bf16[144,384]{1,0:T(8,128)(2,1)S(1)} %get-tuple-element.30), channel_id=1, source_target_pairs={{0,2},{2,0},{4,6},{6,4},{1,3},{3,1},{5,7},{7,5},{8,10},{10,8},{12,... | collective-permute-start | bytes 331784 | tf_op jit(solution)/shard_map/ppermute | solution.py:315
  11.5 0.0 collective-permute-done.4.refs_1_
  11.5 1.5 %collective-permute-start.1 = (bf16[144,384]{1,0:T(8,128)(2,1)S(1)}, bf16[144,384]{1,0:T(8,128)(2,1)S(1)}, u32[]{:S(2)}, u32[]{:S(2)}) collective-permute-start(bf16[144,384]{1,0:T(8,128)(2,1)S(1)} %get-tuple-element.31), channel_id=1, source_target_pairs={{0,4},{2,6},{4,0},{6,2},{1,5},{3,7},{5,1},{7,3},{8,12},{10,14},{12... | collective-permute-start | bytes 331784 | tf_op jit(solution)/shard_map/ppermute | solution.py:315
  13.0 0.0 collective-permute-done.5.refs_2_
  13.1 1.6 %collective-permute-start.2 = (bf16[144,384]{1,0:T(8,128)(2,1)S(1)}, bf16[144,384]{1,0:T(8,128)(2,1)S(1)}, u32[]{:S(2)}, u32[]{:S(2)}) collective-permute-start(bf16[144,384]{1,0:T(8,128)(2,1)S(1)} %get-tuple-element.32), channel_id=1, source_target_pairs={{0,6},{2,4},{4,2},{6,0},{1,7},{3,5},{5,3},{7,1},{8,14},{10,12},{12... | collective-permute-start | bytes 331784 | tf_op jit(solution)/shard_map/ppermute | solution.py:315
  14.6 0.0 collective-permute-done.6.refs_3_
  14.6 0.9 %copy-done.8 = bf16[7,7,1536]{2,1,0:T(8,128)(2,1)S(1)} copy-done((bf16[7,7,1536]{2,1,0:T(8,128)(2,1)S(1)}, bf16[7,7,1536]{2,1,0:T(8,128)(2,1)}, u32[]{:S(2)}) %copy-start.8) | copy-done | bytes 150552
  15.6 3.5 %shard_map.133 = (f32[512,384]{1,0:T(8,128)S(1)}, bf16[512,384]{1,0:T(8,128)(2,1)S(1)}) custom-call(s32[6]{0:T(128)S(1)} %stack.20.pos_ref.refs_0_, bf16[128,384]{1,0:T(8,128)(2,1)S(1)} %get-tuple-element.34.refs_0_, bf16[128,384]{1,0:T(8,128)(2,1)S(1)} %collective-permute-done.4.refs_1_, bf16[128,384]{1,0:T(8,128)(2,1)S(1)} %collective-permute-done.5.refs_2_, ...), custom_call_target="tpu_custom_call" | custom-call | flops 1926758400 | bytes 1966080 | tf_op jit(solution)/shard_map/pallas_call | solution.py:390
  19.0 0.1 collective-permute-start.8
  19.1 0.0 collective-permute-done.3.refs_1_.refs_8_
  19.1 0.0 collective-permute-done.refs_1_
  19.1 0.0 collective-permute-done.1.refs_2_
  19.2 0.0 collective-permute-done.2.refs_3_
  19.2 0.0 copy-start.6
  19.2 0.0 copy-start.7
  19.2 0.0 copy-start.2
  19.2 0.0 slice-start.1
  19.2 0.0 copy-start.3
  19.2 0.0 copy-start.4
  19.2 3.5 %shard_map.134 = (f32[512,384]{1,0:T(8,128)S(1)}, bf16[512,384]{1,0:T(8,128)(2,1)S(1)}) custom-call(s32[6]{0:T(128)S(1)} %stack.20.pos_ref.refs_0_, bf16[144,384]{1,0:T(8,128)(2,1)S(1)} %get-tuple-element.29.refs_0_, bf16[144,384]{1,0:T(8,128)(2,1)S(1)} %collective-permute-done.refs_1_, bf16[144,384]{1,0:T(8,128)(2,1)S(1)} %collective-permute-done.1.refs_2_, ...), custom_call_target="tpu_custom_call" | custom-call | flops 1926758400 | bytes 1966080 | tf_op jit(solution)/shard_map/pallas_call | solution.py:390
  22.7 0.5 collective-permute-start.9
  23.3 1.0 %shard_map.132 = (bf16[576,512]{1,0:T(8,128)(2,1)S(1)}, bf16[64,256]{1,0:T(8,128)(2,1)S(1)}, f32[64,128]{1,0:T(8,128)S(1)}) custom-call(s32[6]{0:T(128)S(1)} %stack.20.pos_ref.refs_0_, bf16[144,384]{1,0:T(8,128)(2,1)S(1)} %get-tuple-element.29.refs_0_, bf16[144,384]{1,0:T(8,128)(2,1)S(1)} %collective-permute-done.refs_1_, ...), custom_call_target="tpu_custom_call" | custom-call | flops 100000000 | bytes 1000000 | tf_op jit(solution)/shard_map/pallas_call | solution.py:409
  24.3 0.0 copy-done.2
  24.3 2.7 %collective-permute-start.7 = (bf16[128,256]{1,0:T(8,128)(2,1)S(1)}, bf16[128,256]{1,0:T(8,128)(2,1)S(1)}, u32[]{:S(2)}, u32[]{:S(2)}) collective-permute-start(bf16[128,256]{1,0:T(8,128)(2,1)S(1)} %shard_map.135), channel_id=1, source_target_pairs={{0,16},{8,24},{16,0},{24,8},{1,17},{9,25},{17,1},{25,9},{2,18},{10... | collective-permute-start | bytes 196616 | tf_op jit(solution)/shard_map/ppermute | solution.py:315
  27.0 0.0 collective-permute-done.8.refs_2_
  27.0 0.0 collective-permute-done.9.refs_3_
  27.0 0.0 slice-done
  27.1 0.0 slice-done.3
  27.1 0.0 slice-done.1
  27.1 0.0 copy-done.3
  27.1 0.0 copy-done.4
  27.1 0.0 slice-start.4
  27.1 4.3 %shard_map.136 = (f32[256,1536]{1,0:T(8,128)S(1)}, bf16[256,1536]{1,0:T(8,128)(2,1)S(1)}) custom-call(s32[6]{0:T(128)S(1)} %stack.20.pos_ref.refs_0_, f32[512,384]{1,0:T(8,128)S(1)} %get-tuple-element.38.refs_0_, f32[512,384]{1,0:T(8,128)S(1)} %get-tuple-element.40.refs_1_, f32[512,384]{1,0:T(8,128)S(1)} %collective-permute-done.8.refs_2_, ...), custom_call_target="tpu_custom_call" | custom-call | flops 2415919104 | bytes 9437184 | tf_op jit(solution)/shard_map/pallas_call | solution.py:436
  31.4 0.0 collective-permute-done.7.refs_2_.refs_9_
  31.4 0.0 copy-start
  31.4 0.0 slice-start.5
  31.4 0.1 collective-permute-start.12
  31.5 4.3 %shard_map.137 = (f32[256,1536]{1,0:T(8,128)S(1)}, bf16[256,1536]{1,0:T(8,128)(2,1)S(1)}) custom-call(s32[6]{0:T(128)S(1)} %stack.20.pos_ref.refs_0_, f32[512,384]{1,0:T(8,128)S(1)} %get-tuple-element.38.refs_0_, f32[512,384]{1,0:T(8,128)S(1)} %get-tuple-element.40.refs_1_, f32[512,384]{1,0:T(8,128)S(1)} %collective-permute-done.8.refs_2_, ...), custom_call_target="tpu_custom_call" | custom-call | flops 2415919104 | bytes 9437184 | tf_op jit(solution)/shard_map/pallas_call | solution.py:436
  35.8 0.6 collective-permute-start.10
  36.4 0.6 %collective-permute-start.11 = (bf16[256,256]{1,0:T(8,128)(2,1)S(1)}, bf16[256,256]{1,0:T(8,128)(2,1)S(1)}, u32[]{:S(2)}, u32[]{:S(2)}) collective-permute-start(bf16[256,256]{1,0:T(8,128)(2,1)S(1)} %shard_map.138), channel_id=1, source_target_pairs={{0,2},{2,0},{4,6},{6,4},{1,3},{3,1},{5,7},{7,5},{8,10},{10,8},{12,... | collective-permute-start | bytes 393224 | tf_op jit(solution)/shard_map/ppermute | solution.py:315
  37.0 4.9 %collective-permute-done.11.refs_3_.refs_10_ = bf16[256,256]{1,0:T(8,128)(2,1)S(1)} collective-permute-done((bf16[256,256]{1,0:T(8,128)(2,1)S(1)}, bf16[256,256]{1,0:T(8,128)(2,1)S(1)}, u32[]{:S(2)}, u32[]{:S(2)}) %collective-permute-start.11) | collective-permute-done | bytes 131104 | tf_op jit(solution)/shard_map/ppermute | solution.py:315
  41.9 0.5 collective-permute-start.17
  42.4 0.0 collective-permute-done.12.other_ref
  42.4 1.0 %shard_map.139.first_ref = bf16[256,1024]{1,0:T(8,128)(2,1)S(1)} custom-call(f32[256,1536]{1,0:T(8,128)S(1)} %get-tuple-element.49.z_ref, bf16[256,1536]{1,0:T(8,128)(2,1)S(1)} %collective-permute-done.12.other_ref, bf16[1536,1024]{1,0:T(8,128)(2,1)S(1)} %copy-done), custom_call_target="tpu_custom_call" | custom-call | flops 805306368 | bytes 3145728 | tf_op jit(solution)/shard_map/pallas_call | solution.py:455
  43.4 0.0 collective-permute-done.10.other_ref
  43.5 2.8 %shard_map.140.a_ref = f32[64,256]{1,0:T(8,128)S(1)} custom-call(f32[256,1536]{1,0:T(8,128)S(1)} %get-tuple-element.47.z_ref, bf16[256,1536]{1,0:T(8,128)(2,1)S(1)} %collective-permute-done.10.other_ref, bf16[256,1024]{1,0:T(8,128)(2,1)S(1)} %shard_map.139.first_ref, bf16[1536,1024]{1,0:T(8,128)(2,1)S(1)} %copy-done, bf16[9,1024,256]{2,1,0:T(8,128)(2,1)S(1)} %bitcast.11, ...), custom_call_target="tpu_custom_call" | custom-call | flops 2013265920 | bytes 6291456 | tf_op jit(solution)/shard_map/pallas_call | solution.py:464
  46.3 0.1 collective-permute-start.13
  46.4 1.2 %collective-permute-done.13.b_ref = f32[64,256]{1,0:T(8,128)S(1)} collective-permute-done((f32[64,256]{1,0:T(8,128)S(1)}, f32[64,256]{1,0:T(8,128)S(1)}, u32[]{:S(2)}, u32[]{:S(2)}) %collective-permute-start.13) | collective-permute-done | bytes 65568 | tf_op jit(solution)/shard_map/ppermute | solution.py:315
  47.6 1.5 %collective-permute-start.14 = (f32[64,256]{1,0:T(8,128)S(1)}, f32[64,256]{1,0:T(8,128)S(1)}, u32[]{:S(2)}, u32[]{:S(2)}) collective-permute-start(f32[64,256]{1,0:T(8,128)S(1)} %shard_map.141.refs_1_), channel_id=1, source_target_pairs={{0,2},{2,0},{4,6},{6,4},{1,3},{3,1},{5,7},{7,5},{8,10},{10,8},{12,... | collective-permute-start | bytes 196616 | tf_op jit(solution)/shard_map/ppermute | solution.py:315
  49.1 0.7 %collective-permute-start.15 = (f32[64,256]{1,0:T(8,128)S(1)}, f32[64,256]{1,0:T(8,128)S(1)}, u32[]{:S(2)}, u32[]{:S(2)}) collective-permute-start(f32[64,256]{1,0:T(8,128)S(1)} %shard_map.141.refs_1_), channel_id=1, source_target_pairs={{0,4},{2,6},{4,0},{6,2},{1,5},{3,7},{5,1},{7,3},{8,12},{10,14},{12... | collective-permute-start | bytes 196616 | tf_op jit(solution)/shard_map/ppermute | solution.py:315
  49.8 1.4 %collective-permute-start.16 = (f32[64,256]{1,0:T(8,128)S(1)}, f32[64,256]{1,0:T(8,128)S(1)}, u32[]{:S(2)}, u32[]{:S(2)}) collective-permute-start(f32[64,256]{1,0:T(8,128)S(1)} %shard_map.141.refs_1_), channel_id=1, source_target_pairs={{0,6},{2,4},{4,2},{6,0},{1,7},{3,5},{5,3},{7,1},{8,14},{10,12},{12... | collective-permute-start | bytes 196616 | tf_op jit(solution)/shard_map/ppermute | solution.py:315
  51.2 0.0 collective-permute-done.17.refs_11_
  51.2 0.8 %collective-permute-done.14.refs_2_ = f32[64,256]{1,0:T(8,128)S(1)} collective-permute-done((f32[64,256]{1,0:T(8,128)S(1)}, f32[64,256]{1,0:T(8,128)S(1)}, u32[]{:S(2)}, u32[]{:S(2)}) %collective-permute-start.14) | collective-permute-done | bytes 65568 | tf_op jit(solution)/shard_map/ppermute | solution.py:315
  52.0 2.1 %collective-permute-done.15.refs_3_ = f32[64,256]{1,0:T(8,128)S(1)} collective-permute-done((f32[64,256]{1,0:T(8,128)S(1)}, f32[64,256]{1,0:T(8,128)S(1)}, u32[]{:S(2)}, u32[]{:S(2)}) %collective-permute-start.15) | collective-permute-done | bytes 65568 | tf_op jit(solution)/shard_map/ppermute | solution.py:315
  54.1 0.9 %collective-permute-done.16.refs_4_ = f32[64,256]{1,0:T(8,128)S(1)} collective-permute-done((f32[64,256]{1,0:T(8,128)S(1)}, f32[64,256]{1,0:T(8,128)S(1)}, u32[]{:S(2)}, u32[]{:S(2)}) %collective-permute-start.16) | collective-permute-done | bytes 65568 | tf_op jit(solution)/shard_map/ppermute | solution.py:315
  55.0 1.9 %shard_map.143 = (f32[64,256]{1,0:T(8,128)}, f32[1,64]{1,0:T(1,128)}) custom-call(s32[6]{0:T(128)S(1)} %stack.20.pos_ref.refs_0_, f32[64,256]{1,0:T(8,128)S(1)} %shard_map.141.refs_1_, f32[64,256]{1,0:T(8,128)S(1)} %collective-permute-done.14.refs_2_, f32[64,256]{1,0:T(8,128)S(1)} %collective-permute-done.15.refs_3_, ...), custom_call_target="tpu_custom_call" | custom-call | flops 100000000 | bytes 1000000 | tf_op jit(solution)/shard_map/pallas_call | solution.py:487
  (19 shorter events, 0.1 us)
Async XLA Ops:
  0.7 1.4 %copy-start.1 = (bf16[4,4,32,1536]{3,2,1,0:T(8,128)(2,1)S(1)}, bf16[4,4,32,1536]{3,2,1,0:T(8,128)(2,1)}, u32[]{:S(2)}) copy-start(bf16[4,4,32,1536]{3,2,1,0:T(8,128)(2,1)} %param.12) | copy-start | bytes 4718596
  2.1 0.7 %copy-start.5 = (s32[4,4,32]{2,1,0:T(4,128)S(1)}, s32[4,4,32]{2,1,0:T(4,128)}, u32[]{:S(2)}) copy-start(s32[4,4,32]{2,1,0:T(4,128)} %ids_ref.1) | copy-start | bytes 6148
  2.8 24.2 %slice-start.2 = ((s8[4718592]{0:T(1024)(128)(4,1)}), s8[4194304]{0:T(1024)(128)(4,1)S(1)}, s32[]{:S(2)}) async-start(s8[4718592]{0:T(1024)(128)(4,1)} %bitcast.8), calls=%async_computation.2 | async-start | bytes 8388608
  3.5 8.1 %collective-permute-start.4 = (bf16[128,384]{1,0:T(8,128)(2,1)S(1)}, bf16[128,384]{1,0:T(8,128)(2,1)S(1)}, u32[]{:S(2)}, u32[]{:S(2)}) collective-permute-start(bf16[128,384]{1,0:T(8,128)(2,1)S(1)} %get-tuple-element.35), channel_id=1, source_target_pairs={{0,2},{2,0},{4,6},{6,4},{1,3},{3,1},{5,7},{7,5},{8,10},{10,8},{12,... | collective-permute-start | bytes 294920 | tf_op jit(solution)/shard_map/ppermute | solution.py:315
  6.5 6.6 %collective-permute-start.5 = (bf16[128,384]{1,0:T(8,128)(2,1)S(1)}, bf16[128,384]{1,0:T(8,128)(2,1)S(1)}, u32[]{:S(2)}, u32[]{:S(2)}) collective-permute-start(bf16[128,384]{1,0:T(8,128)(2,1)S(1)} %get-tuple-element.36), channel_id=1, source_target_pairs={{0,4},{2,6},{4,0},{6,2},{1,5},{3,7},{5,1},{7,3},{8,12},{10,14},{12... | collective-permute-start | bytes 294920 | tf_op jit(solution)/shard_map/ppermute | solution.py:315
  8.0 6.7 %collective-permute-start.6 = (bf16[128,384]{1,0:T(8,128)(2,1)S(1)}, bf16[128,384]{1,0:T(8,128)(2,1)S(1)}, u32[]{:S(2)}, u32[]{:S(2)}) collective-permute-start(bf16[128,384]{1,0:T(8,128)(2,1)S(1)} %get-tuple-element.37), channel_id=1, source_target_pairs={{0,6},{2,4},{4,2},{6,0},{1,7},{3,5},{5,3},{7,1},{8,14},{10,12},{12... | collective-permute-start | bytes 294920 | tf_op jit(solution)/shard_map/ppermute | solution.py:315
  8.0 11.1 %collective-permute-start.3 = (bf16[64,256]{1,0:T(8,128)(2,1)}, bf16[64,256]{1,0:T(8,128)(2,1)S(1)}, u32[]{:S(2)}, u32[]{:S(2)}) collective-permute-start(bf16[64,256]{1,0:T(8,128)(2,1)} %refs_7_.5), channel_id=1, source_target_pairs={{0,8},{8,0},{16,24},{24,16},{1,9},{9,1},{17,25},{25,17},{2,10},{10... | collective-permute-start | bytes 98312 | tf_op jit(solution)/shard_map/ppermute | solution.py:315
  10.0 9.1 %collective-permute-start = (bf16[144,384]{1,0:T(8,128)(2,1)S(1)}, bf16[144,384]{1,0:T(8,128)(2,1)S(1)}, u32[]{:S(2)}, u32[]{:S(2)}) collective-permute-start(bf16[144,384]{1,0:T(8,128)(2,1)S(1)} %get-tuple-element.30), channel_id=1, source_target_pairs={{0,2},{2,0},{4,6},{6,4},{1,3},{3,1},{5,7},{7,5},{8,10},{10,8},{12,... | collective-permute-start | bytes 331784 | tf_op jit(solution)/shard_map/ppermute | solution.py:315
  11.5 7.6 %collective-permute-start.1 = (bf16[144,384]{1,0:T(8,128)(2,1)S(1)}, bf16[144,384]{1,0:T(8,128)(2,1)S(1)}, u32[]{:S(2)}, u32[]{:S(2)}) collective-permute-start(bf16[144,384]{1,0:T(8,128)(2,1)S(1)} %get-tuple-element.31), channel_id=1, source_target_pairs={{0,4},{2,6},{4,0},{6,2},{1,5},{3,7},{5,1},{7,3},{8,12},{10,14},{12... | collective-permute-start | bytes 331784 | tf_op jit(solution)/shard_map/ppermute | solution.py:315
  13.1 6.1 %collective-permute-start.2 = (bf16[144,384]{1,0:T(8,128)(2,1)S(1)}, bf16[144,384]{1,0:T(8,128)(2,1)S(1)}, u32[]{:S(2)}, u32[]{:S(2)}) collective-permute-start(bf16[144,384]{1,0:T(8,128)(2,1)S(1)} %get-tuple-element.32), channel_id=1, source_target_pairs={{0,6},{2,4},{4,2},{6,0},{1,7},{3,5},{5,3},{7,1},{8,14},{10,12},{12... | collective-permute-start | bytes 331784 | tf_op jit(solution)/shard_map/ppermute | solution.py:315
  14.6 0.9 %copy-start.8 = (bf16[7,7,1536]{2,1,0:T(8,128)(2,1)S(1)}, bf16[7,7,1536]{2,1,0:T(8,128)(2,1)}, u32[]{:S(2)}) copy-start(bf16[7,7,1536]{2,1,0:T(8,128)(2,1)} %refs_4_.5) | copy-start | bytes 451588
  15.6 11.5 %slice-start = ((s8[4718592]{0:T(1024)(128)(4,1)}), s8[4194304]{0:T(1024)(128)(4,1)S(1)}, s32[]{:S(2)}) async-start(s8[4718592]{0:T(1024)(128)(4,1)} %bitcast.6), calls=%async_computation | async-start | bytes 8388608
  15.6 11.5 %slice-start.3 = ((s8[4718592]{0:T(1024)(128)(4,1)}), s8[524288]{0:T(1024)(128)(4,1)S(1)}, s32[]{:S(2)}) async-start(s8[4718592]{0:T(1024)(128)(4,1)} %bitcast.8), calls=%async_computation.3 | async-start | bytes 1048576
  19.0 8.0 %collective-permute-start.8 = (f32[512,384]{1,0:T(8,128)S(1)}, f32[512,384]{1,0:T(8,128)S(1)}, u32[]{:S(2)}, u32[]{:S(2)}) collective-permute-start(f32[512,384]{1,0:T(8,128)S(1)} %get-tuple-element.38.refs_0_), channel_id=1, source_target_pairs={{0,1},{1,0},{2,3},{3,2},{4,5},{5,4},{6,7},{7,6},{8,9},{9,8},{10,11... | collective-permute-start | bytes 2359304 | tf_op jit(solution)/shard_map/ppermute | solution.py:315
  19.2 4.1 %copy-start.6 = (s32[4,64]{1,0:T(4,128)S(1)}, s32[4,64]{1,0:T(4,128)}, u32[]{:S(2)}) copy-start(s32[4,64]{1,0:T(4,128)} %refs_5_.1) | copy-start | bytes 3076
  19.2 4.1 %copy-start.7 = (s32[1,256]{1,0:T(1,128)S(1)}, s32[1,256]{1,0:T(1,128)}, u32[]{:S(2)}) copy-start(s32[1,256]{1,0:T(1,128)} %refs_4_.3) | copy-start | bytes 3076
  19.2 5.1 %copy-start.2 = (bf16[64,256]{1,0:T(8,128)(2,1)S(1)}, bf16[64,256]{1,0:T(8,128)(2,1)}, u32[]{:S(2)}) copy-start(bf16[64,256]{1,0:T(8,128)(2,1)} %refs_7_.5) | copy-start | bytes 98308
  19.2 7.9 %slice-start.1 = ((s8[4718592]{0:T(1024)(128)(4,1)}), s8[524288]{0:T(1024)(128)(4,1)S(1)}, s32[]{:S(2)}) async-start(s8[4718592]{0:T(1024)(128)(4,1)} %bitcast.6), calls=%async_computation.1 | async-start | bytes 1048576
  19.2 7.9 %copy-start.3 = (bf16[1536]{0:T(1024)(128)(2,1)S(1)}, bf16[1536]{0:T(1024)(128)(2,1)}, u32[]{:S(2)}) copy-start(bf16[1536]{0:T(1024)(128)(2,1)} %refs_6_.3) | copy-start | bytes 9220
  19.2 7.9 %copy-start.4 = (bf16[1536]{0:T(1024)(128)(2,1)S(1)}, bf16[1536]{0:T(1024)(128)(2,1)}, u32[]{:S(2)}) copy-start(bf16[1536]{0:T(1024)(128)(2,1)} %refs_7_.4) | copy-start | bytes 9220
  22.7 4.3 %collective-permute-start.9 = (f32[512,384]{1,0:T(8,128)S(1)}, f32[512,384]{1,0:T(8,128)S(1)}, u32[]{:S(2)}, u32[]{:S(2)}) collective-permute-start(f32[512,384]{1,0:T(8,128)S(1)} %get-tuple-element.40.refs_1_), channel_id=1, source_target_pairs={{0,1},{1,0},{2,3},{3,2},{4,5},{5,4},{6,7},{7,6},{8,9},{9,8},{10,11... | collective-permute-start | bytes 2359304 | tf_op jit(solution)/shard_map/ppermute | solution.py:315
  24.3 7.1 %collective-permute-start.7 = (bf16[128,256]{1,0:T(8,128)(2,1)S(1)}, bf16[128,256]{1,0:T(8,128)(2,1)S(1)}, u32[]{:S(2)}, u32[]{:S(2)}) collective-permute-start(bf16[128,256]{1,0:T(8,128)(2,1)S(1)} %shard_map.135), channel_id=1, source_target_pairs={{0,16},{8,24},{16,0},{24,8},{1,17},{9,25},{17,1},{25,9},{2,18},{10... | collective-permute-start | bytes 196616 | tf_op jit(solution)/shard_map/ppermute | solution.py:315
  27.1 16.3 %slice-start.4 = ((s8[4718592]{0:T(1024)(128)(4,1)}), s8[4194304]{0:T(1024)(128)(4,1)S(1)}, s32[]{:S(2)}) async-start(s8[4718592]{0:T(1024)(128)(4,1)} %bitcast.10), calls=%async_computation.4 | async-start | bytes 8388608
  31.4 11.0 %copy-start = (bf16[1536,1024]{1,0:T(8,128)(2,1)S(1)}, bf16[1536,1024]{1,0:T(8,128)(2,1)}, u32[]{:S(2)}) copy-start(bf16[1536,1024]{1,0:T(8,128)(2,1)} %pe_ref.3) | copy-start | bytes 9437188
  31.4 12.0 %slice-start.5 = ((s8[4718592]{0:T(1024)(128)(4,1)}), s8[524288]{0:T(1024)(128)(4,1)S(1)}, s32[]{:S(2)}) async-start(s8[4718592]{0:T(1024)(128)(4,1)} %bitcast.10), calls=%async_computation.5 | async-start | bytes 1048576
  31.4 11.0 %collective-permute-start.12 = (bf16[256,1536]{1,0:T(8,128)(2,1)S(1)}, bf16[256,1536]{1,0:T(8,128)(2,1)S(1)}, u32[]{:S(2)}, u32[]{:S(2)}) collective-permute-start(bf16[256,1536]{1,0:T(8,128)(2,1)S(1)} %get-tuple-element.50), channel_id=1, source_target_pairs={{0,1},{1,0},{2,3},{3,2},{4,5},{5,4},{6,7},{7,6},{8,9},{9,8},{10,11... | collective-permute-start | bytes 2359304 | tf_op jit(solution)/shard_map/ppermute | solution.py:315
  35.8 7.6 %collective-permute-start.10 = (bf16[256,1536]{1,0:T(8,128)(2,1)S(1)}, bf16[256,1536]{1,0:T(8,128)(2,1)S(1)}, u32[]{:S(2)}, u32[]{:S(2)}) collective-permute-start(bf16[256,1536]{1,0:T(8,128)(2,1)S(1)} %get-tuple-element.48), channel_id=1, source_target_pairs={{0,1},{1,0},{2,3},{3,2},{4,5},{5,4},{6,7},{7,6},{8,9},{9,8},{10,11... | collective-permute-start | bytes 2359304 | tf_op jit(solution)/shard_map/ppermute | solution.py:315
  36.4 5.5 %collective-permute-start.11 = (bf16[256,256]{1,0:T(8,128)(2,1)S(1)}, bf16[256,256]{1,0:T(8,128)(2,1)S(1)}, u32[]{:S(2)}, u32[]{:S(2)}) collective-permute-start(bf16[256,256]{1,0:T(8,128)(2,1)S(1)} %shard_map.138), channel_id=1, source_target_pairs={{0,2},{2,0},{4,6},{6,4},{1,3},{3,1},{5,7},{7,5},{8,10},{10,8},{12,... | collective-permute-start | bytes 393224 | tf_op jit(solution)/shard_map/ppermute | solution.py:315
  41.9 9.3 %collective-permute-start.17 = (bf16[512,256]{1,0:T(8,128)(2,1)S(1)}, bf16[512,256]{1,0:T(8,128)(2,1)S(1)}, u32[]{:S(2)}, u32[]{:S(2)}) collective-permute-start(bf16[512,256]{1,0:T(8,128)(2,1)S(1)} %shard_map.142), channel_id=1, source_target_pairs={{0,4},{2,6},{4,0},{6,2},{1,5},{3,7},{5,1},{7,3},{8,12},{10,14},{12... | collective-permute-start | bytes 786440 | tf_op jit(solution)/shard_map/ppermute | solution.py:315
  46.3 1.3 %collective-permute-start.13 = (f32[64,256]{1,0:T(8,128)S(1)}, f32[64,256]{1,0:T(8,128)S(1)}, u32[]{:S(2)}, u32[]{:S(2)}) collective-permute-start(f32[64,256]{1,0:T(8,128)S(1)} %shard_map.140.a_ref), channel_id=1, source_target_pairs={{0,1},{1,0},{2,3},{3,2},{4,5},{5,4},{6,7},{7,6},{8,9},{9,8},{10,11... | collective-permute-start | bytes 196616 | tf_op jit(solution)/shard_map/ppermute | solution.py:315
  47.6 4.3 %collective-permute-start.14 = (f32[64,256]{1,0:T(8,128)S(1)}, f32[64,256]{1,0:T(8,128)S(1)}, u32[]{:S(2)}, u32[]{:S(2)}) collective-permute-start(f32[64,256]{1,0:T(8,128)S(1)} %shard_map.141.refs_1_), channel_id=1, source_target_pairs={{0,2},{2,0},{4,6},{6,4},{1,3},{3,1},{5,7},{7,5},{8,10},{10,8},{12,... | collective-permute-start | bytes 196616 | tf_op jit(solution)/shard_map/ppermute | solution.py:315
  49.1 5.0 %collective-permute-start.15 = (f32[64,256]{1,0:T(8,128)S(1)}, f32[64,256]{1,0:T(8,128)S(1)}, u32[]{:S(2)}, u32[]{:S(2)}) collective-permute-start(f32[64,256]{1,0:T(8,128)S(1)} %shard_map.141.refs_1_), channel_id=1, source_target_pairs={{0,4},{2,6},{4,0},{6,2},{1,5},{3,7},{5,1},{7,3},{8,12},{10,14},{12... | collective-permute-start | bytes 196616 | tf_op jit(solution)/shard_map/ppermute | solution.py:315
  49.8 5.2 %collective-permute-start.16 = (f32[64,256]{1,0:T(8,128)S(1)}, f32[64,256]{1,0:T(8,128)S(1)}, u32[]{:S(2)}, u32[]{:S(2)}) collective-permute-start(f32[64,256]{1,0:T(8,128)S(1)} %shard_map.141.refs_1_), channel_id=1, source_target_pairs={{0,6},{2,4},{4,2},{6,0},{1,7},{3,5},{5,3},{7,1},{8,14},{10,12},{12... | collective-permute-start | bytes 196616 | tf_op jit(solution)/shard_map/ppermute | solution.py:315
where the time goes:
time: 57.2 us; the launch traced here: 56.9 us
  Pallas kernels  23 us (40%)
  starting transfers between devices  19.8 us (35%)
  waiting for transfers between devices  9.97 us (17%)
  local copies, waits for them, and re-layouts  3.18 us (6%)
  between operations  0.97 us (2%)
    ppermute x18, starting transfers between devices, swap(): lax.ppermute(x, axis, [(i, i ^ bit) for i in range(lax.axis_size(axis))])  19.8 us
    ppermute x18, waiting for transfers between devices, swap(): lax.ppermute(x, axis, [(i, i ^ bit) for i in range(lax.axis_size(axis))])  9.97 us
    pallas_call x2, Pallas kernels, body(): call(functools.partial(block_kernel, (p * part_pixels, part_pixels, CHUNK...  8.56 us
    pallas_call x2, Pallas kernels, body(): call(functools.partial(conv_kernel, (shards, shard_rows, width, out_rows,...  6.96 us
    unnamed x30, local copies, waits for them, and re-layouts  3.1 us
    pallas_call x1, Pallas kernels, body(): call(project_kernel, [jax.ShapeDtypeStruct((REG, out_dim), f32)], [VMEM]...  2.84 us
    pallas_call x1, Pallas kernels, body(): call(functools.partial(loss_kernel, (shards, parts)), [jax.ShapeDtypeStru...  1.95 us
  transfers between devices with their start and end apart: 18, of which 5 were waited for; matrix products, arithmetic and copies ran while one was open for 0% of the time, Pallas kernels for 36%

commit v1 on v0

--- a/solution.py
+++ b/solution.py
@@ -49,22 +49,24 @@
     return hi, mid, (rest - mid.astype(f32)).astype(bf16)
 
 
-def stage_kernel(geo, pos_ref, feat_ref, ids_ref, *refs):
-    shards, chunks, parts = geo
-    blocks, line = refs[: shards * chunks], refs[shards * chunks]
-    row, section = pos_ref[0], pos_ref[3]
-    images, pixels, chans = feat_ref.shape
-    span = blocks[0].shape[1]
-    for c in range(chunks):
-        lanes = pl.ds(pl.multiple_of(section * (chans // 2) + c * span, LANES), span)
-        for k in range(shards):
-            blocks[c * shards + k][0:pixels, :] = feat_ref[(row ^ k) // parts, :, lanes]
+def pack_kernel(count, pos_ref, ids_ref, key_ref, dw_ref, *refs):
+    inputs, blocks = refs[:count], refs[count : 2 * count]
+    w_ref, line = refs[2 * count :]
+    pixels = inputs[0].shape[0]
+    keys, depth = key_ref.shape
+    shard_rows, width = ids_ref.shape[1:]
     line[...] = jnp.full(line.shape, -1.0, f32)
-    shard_rows, width = ids_ref.shape[1:]
-    for i in range(images):
+    for i in range(ids_ref.shape[0]):
         line[i * shard_rows : (i + 1) * shard_rows, 0:width] = ids_ref[i].astype(f32)
-    for k in range(shards):
-        blocks[(chunks - 1) * shards + k][pixels:, :] = line[...].astype(bf16)
+    tail = line[...].astype(bf16)
+    for source, block in zip(inputs, blocks):
+        block[0:pixels, :] = source[...]
+        block[pixels : pixels + keys, 0:depth] = key_ref[...]
+        block[pixels:, depth : depth + LANES] = tail
+    half = w_ref.shape[1]
+    lanes = pl.ds(pl.multiple_of(pos_ref[3] * half, LANES), half)
+    for dy in range(7):
+        w_ref[dy * 7 : dy * 7 + 7, :] = dw_ref[dy, :, lanes].astype(f32)
 
 
 def join_kernel(*refs):
@@ -91,7 +93,6 @@
     w_ref, taps, img_ref, xpad, wide = refs[shards:]
     chunk = taps.shape[1]
     row, first_row, col0 = pos_ref[0], pos_ref[1], pos_ref[2]
-    base = pos_ref[3] * (w_ref.shape[2] // 2) + first_lane
     height = shards * shard_rows
     pixels = shard_rows * width
     cols = xpad.shape[1]
@@ -109,10 +110,9 @@
         for k in range(shards):
             value = blocks[k][0:pixels, lanes].astype(f32).reshape(shard_rows, width, LANES)
             xpad[pl.ds(3 + (row ^ k) * shard_rows, shard_rows), 8 : 8 + width, :] = value
-        for dy in range(7):
-            w = w_ref[dy, :, pl.ds(pl.multiple_of(base + g * LANES, LANES), LANES)].astype(f32)
-            for dx in range(7):
-                wide[dy * 7 + dx] = jnp.broadcast_to(w[dx : dx + 1], (8, LANES))
+        for t in range(49):
+            w = w_ref[t : t + 1, pl.ds(pl.multiple_of(first_lane + g * LANES, LANES), LANES)]
+            wide[t] = jnp.broadcast_to(w, (8, LANES))
 
         def strip(i, carry):
             top = first_row + i * step_rows
@@ -189,12 +189,15 @@
 
 
 def prep_kernel(geo, pos_ref, *refs):
-    shards, shard_rows, width, out_pixels, images, batches, per_key, parts = geo
+    shards, shard_rows, width, out_pixels, images, per_key, parts = geo
     ids = refs[:shards]
-    owner_ref, partner_ref, hot_ref, pick_ref, own_ref, flat = refs[shards:]
+    owner_ref, partner_ref, hot_ref, pick_ref, own_ref, keys_ref, flat = refs[shards:]
     row, first_row, batch, first_slot = pos_ref[0], pos_ref[1], pos_ref[4], pos_ref[5]
     pixels = shard_rows * width
-    ids = [ref[pixels:, 0:LANES].astype(f32) for ref in ids]
+    depth = keys_ref.shape[1]
+    for k in range(shards):
+        keys_ref[k * per_key : (k + 1) * per_key, :] = ids[k][pixels : pixels + per_key, 0:depth]
+    ids = [ref[pixels:, depth : depth + LANES].astype(f32) for ref in ids]
     owned = own_ref.shape[0]
     slots = images * REG
     image = row // parts
@@ -245,7 +248,7 @@
     mates = jnp.concatenate([partner_ref[i : i + 1, :] for i in range(images)], axis=1)
     mate = (batch * images + slot // REG) * REG + mates
     block = mate // per_key
-    place = ((block % shards) ^ row) * batches + ((block // shards) ^ batch)
+    place = ((block // shards) ^ batch) * shards + ((block % shards) ^ row)
     place = place * per_key + mate % per_key
     place = jnp.sum(jnp.where(pick, place, 0).astype(f32), axis=1, keepdims=True)
     number = jnp.sum(jnp.where(pick, count, 0.0), axis=1, keepdims=True)
@@ -352,41 +355,36 @@
         [row, first_row, jnp.int32(5), section, batch, row * owned]
     ).astype(jnp.int32)
 
-    tail = -(-images * shard_rows // 16) * 16
-    sizes = [pixels] * (CHUNKS - 1) + [pixels + tail]
-    parcels = call(
-        functools.partial(stage_kernel, (shards, CHUNKS, parts)),
-        [jax.ShapeDtypeStruct((size, span), bf16) for size in sizes for _ in range(shards)],
-        [SMEM, VMEM, VMEM],
-        [pltpu.VMEM((tail, span), f32)],
+    per_key, depth = key_embed.shape
+    tail = max(-(-images * shard_rows // 16) * 16, per_key)
+    def after(here, *done):
+        return lax.optimization_barrier((here, *done))[0]
+
+    parcels = []
+    for c in range(CHUNKS):
+        blocks = []
+        for k in range(shards):
+            place = ((row ^ k) // parts, 0, 0, section * half + c * span)
+            part = lax.dynamic_slice(features, place, (1, shard_rows, width, span))
+            blocks.append(part.reshape(pixels, span))
+        parcels.append(blocks)
+    *parcels[-1], weights = call(
+        functools.partial(pack_kernel, shards),
+        [jax.ShapeDtypeStruct((pixels + tail, span), bf16)] * shards
+        + [jax.ShapeDtypeStruct((49, half), f32)],
+        [SMEM] + [VMEM] * (3 + shards),
+        [pltpu.VMEM((tail, LANES), f32)],
         mib,
         0,
-        shards * pixels * half * 4,
-    )(spot, features.reshape(images, pixels, chans), region_ids)
-
-    pieces = [key_embed]
-    steps = []
-    for axis, size in (("batch", batches), ("rows", shards)):
-        steps += [(axis, 1 << n) for n in range(size.bit_length() - 1)]
-    share = -(-len(steps) // 4)
-
-    def key_step():
-        for axis, bit in (steps.pop(0) for _ in range(min(share, len(steps)))):
-            whole = pieces[0] if len(pieces) == 1 else join(*pieces)
-            pieces.append(swap(whole, axis, bit))
-
-    def after(here, *done):
-        return lax.optimization_barrier((here, *done))[0]
-
+        10**6,
+    )(spot, region_ids, key_embed, dw_kernel, *parcels[-1])
     got = []
-    for c in range(CHUNKS):
-        blocks = parcels[c * shards : (c + 1) * shards]
+    for blocks in parcels:
         got.append([blocks[0]] + [swap(blocks[k], "rows", k) for k in range(1, shards)])
-    key_step()
 
     own, other, img = [], [], []
     for c in range(CHUNKS):
-        here = after(spot, pieces[-1], *own) if c else spot
+        here = after(spot, *own) if c else spot
         taps, image = call(
             functools.partial(conv_kernel, (shards, shard_rows, width, out_rows, c * span)),
             [
@@ -401,38 +399,35 @@
             3 * mib,
             out_pixels * span * 98 * 100,
             out_pixels * span * 10,
-        )(here, *got[c], dw_kernel)
+        )(here, *got[c], weights)
         own.append(taps)
         img.append(image)
         other.append(swap(taps, "section", 1))
 
-    hot, pick, facts = call(
+    hot, pick, facts, keys = call(
         functools.partial(
             prep_kernel,
-            (shards, shard_rows, width, out_pixels, images, batches, key_embed.shape[0], parts),
+            (shards, shard_rows, width, out_pixels, images, per_key, parts),
         ),
         [
             jax.ShapeDtypeStruct((9 * REG, out_pixels), bf16),
             jax.ShapeDtypeStruct((owned, slots), bf16),
             jax.ShapeDtypeStruct((owned, LANES), f32),
+            jax.ShapeDtypeStruct((shards * per_key, depth), bf16),
         ],
         [SMEM] + [VMEM] * (shards + 2),
         [pltpu.VMEM((16, (shards + 2) * pixels), f32)],
         2 * mib,
         10**8,
         10**6,
-    )(spot, *got[-1], owner_slot, partner)
-
-    pieces[-1] = after(pieces[-1], *own)
-    key_step()
+    )(after(spot, *own), *got[-1], owner_slot, partner)
+    pieces = [keys, swap(keys, "batch", 1)]
 
     hid = w1.shape[1]
     part_pixels = out_pixels // 2
     z, z_other = [], []
     for p in range(2):
-        here = after(spot, hot, pieces[-1], *z) if p else after(spot, hot)
-        if p:
-            key_step()
+        here = after(spot, pieces[-1], *z) if p else after(spot, hot)
         mine, send = call(
             functools.partial(block_kernel, (p * part_pixels, part_pixels, CHUNKS)),
             [
@@ -447,9 +442,10 @@
         )(here, *own, *other, *img, ln_gain, layer_branch_scale, w1, w2)
         z.append(mine)
         z_other.append(swap(send, "section", 1))
-    z[0] = after(z[0], pieces[-1])
-    pieces[-1] = after(pieces[-1], z[1])
-    key_step()
+    bit = 2
+    while bit < batches:
+        pieces.append(swap(join(*pieces), "batch", bit))
+        bit *= 2
 
     hidden = pe.shape[1]
     (hid_a,) = call(

time: 57.2 us -> 52.8 us (0.923)
  starting transfers between devices: 19.8 us -> 16.8 us
  waiting for transfers between devices: 9.97 us -> 7.87 us
  local copies, waits for them, and re-layouts: 3.18 us -> 3.83 us
    ppermute x18 -> x16, starting transfers between devices: 19.8 us -> 16.8 us  [swap(): lax.ppermute(x, axis, [(i, i ^ bit) for i in range(lax.axis_size(axis))])]
    ppermute x18 -> x16, waiting for transfers between devices: 9.97 us -> 7.87 us  [swap(): lax.ppermute(x, axis, [(i, i ^ bit) for i in range(lax.axis_size(axis))])]
    dynamic_slice x0 -> x1, local copies, waits for them, and re-layouts: none -> 1.32 us  [body(): part = lax.dynamic_slice(features, place, (1, shard_rows, width, span))]
    unnamed x30 -> x28, local copies, waits for them, and re-layouts: 3.1 us -> 2.42 us
  transfers between devices with their start and end apart: 18 -> 16, of which waited for: 5 -> 3; matrix products, arithmetic and copies ran while one was open for 0% -> 0% of each run, Pallas kernels for 36% -> 40%
where the time goes in v1:
time: 52.8 us; the launch traced here: 52.5 us
  Pallas kernels  23 us (44%)
  starting transfers between devices  16.8 us (32%)
  waiting for transfers between devices  7.87 us (15%)
  local copies, waits for them, and re-layouts  3.83 us (7%)
  between operations  0.93 us (2%)
    ppermute x16, starting transfers between devices, swap(): lax.ppermute(x, axis, [(i, i ^ bit) for i in range(lax.axis_size(axis))])  16.8 us
    pallas_call x2, Pallas kernels, body(): call(functools.partial(block_kernel, (p * part_pixels, part_pixels, CHUNK...  8.56 us
    ppermute x16, waiting for transfers between devices, swap(): lax.ppermute(x, axis, [(i, i ^ bit) for i in range(lax.axis_size(axis))])  7.87 us
    pallas_call x2, Pallas kernels, body(): call(functools.partial(conv_kernel, (shards, shard_rows, width, out_rows,...  6.97 us
    pallas_call x1, Pallas kernels, body(): call(project_kernel, [jax.ShapeDtypeStruct((REG, out_dim), f32)], [VMEM]...  2.84 us
    unnamed x28, local copies, waits for them, and re-layouts  2.42 us
    pallas_call x1, Pallas kernels, body(): call(functools.partial(loss_kernel, (shards, parts)), [jax.ShapeDtypeStru...  1.95 us
    dynamic_slice x1, local copies, waits for them, and re-layouts, body(): part = lax.dynamic_slice(features, place, (1, shard_rows, width, span))  1.32 us
  transfers between devices with their start and end apart: 16, of which 3 were waited for; matrix products, arithmetic and copies ran while one was open for 0% of the time, Pallas kernels for 40%

profile of v1, /device:TPU:0, one launch (start us, length us, event | category | flops | bytes accessed | tf_op | source)
XLA Modules:
  0.0 52.5 jit_solution(8037055895801602056)
XLA Ops:
  0.7 1.3 %constant_dynamic-slice_fusion = (bf16[1,4,32,384]{3,2,1,0:T(8,128)(2,1)S(1)}, bf16[1,4,32,384]{3,2,1,0:T(8,128)(2,1)S(1)}, bf16[1,4,32,384]{3,2,1,0:T(8,128)(2,...) fusion(bf16[4,4,32,1536]{3,2,1,0:T(8,128)(2,1)} %param.12, ...), kind=kLoop, calls=%fused_computation | loop fusion | bytes 1572888 | tf_op jit(solution)/shard_map/dynamic_slice | solution.py:368
  2.0 3.0 %collective-permute-start = (bf16[128,384]{1,0:T(8,128)(2,1)S(1)}, bf16[128,384]{1,0:T(8,128)(2,1)S(1)}, u32[]{:S(2)}, u32[]{:S(2)}) collective-permute-start(bf16[128,384]{1,0:T(8,128)(2,1)S(1)} %bitcast.26), channel_id=1, source_target_pairs={{0,2},{2,0},{4,6},{6,4},{1,3},{3,1},{5,7},{7,5},{8,10},{10,8},{12,... | collective-permute-start | bytes 294920 | tf_op jit(solution)/shard_map/ppermute | solution.py:318
  5.0 1.5 %collective-permute-start.1 = (bf16[128,384]{1,0:T(8,128)(2,1)S(1)}, bf16[128,384]{1,0:T(8,128)(2,1)S(1)}, u32[]{:S(2)}, u32[]{:S(2)}) collective-permute-start(bf16[128,384]{1,0:T(8,128)(2,1)S(1)} %bitcast.25), channel_id=1, source_target_pairs={{0,4},{2,6},{4,0},{6,2},{1,5},{3,7},{5,1},{7,3},{8,12},{10,14},{12... | collective-permute-start | bytes 294920 | tf_op jit(solution)/shard_map/ppermute | solution.py:318
  6.5 0.0 collective-permute-start.2
  6.5 0.1 stack.20.pos_ref.refs_0_
  6.6 0.0 copy-start.1
  6.6 0.9 %copy-done.1 = bf16[7,7,1536]{2,1,0:T(8,128)(2,1)S(1)} copy-done((bf16[7,7,1536]{2,1,0:T(8,128)(2,1)S(1)}, bf16[7,7,1536]{2,1,0:T(8,128)(2,1)}, u32[]{:S(2)}) %copy-start.1) | copy-done | bytes 150552
  7.5 0.8 %copy-done.2 = bf16[64,256]{1,0:T(8,128)(2,1)S(1)} copy-done((bf16[64,256]{1,0:T(8,128)(2,1)S(1)}, bf16[64,256]{1,0:T(8,128)(2,1)}, u32[]{:S(2)}) %copy-start.2) | copy-done | bytes 32792
  8.3 0.0 copy-start.5
  8.3 0.7 %copy-done.5 = s32[4,4,32]{2,1,0:T(4,128)S(1)} copy-done((s32[4,4,32]{2,1,0:T(4,128)S(1)}, s32[4,4,32]{2,1,0:T(4,128)}, u32[]{:S(2)}) %copy-start.5) | copy-done | bytes 2072
  9.0 0.0 slice-start.2
  9.0 0.6 %shard_map.131 = (bf16[192,384]{1,0:T(8,128)(2,1)S(1)}, bf16[192,384]{1,0:T(8,128)(2,1)S(1)}, bf16[192,384]{1,0:T(8,128)(2,1)S(1)}, bf16[192,384]{1,0:T(8,128)(2,1)S(1)}, f32[49,768]{1,0:T(8,128)S(1)}) custom-call(s32[6]{0:T(128)S(1)} %stack.20.pos_ref.refs_0_, s32[4,4,32]{2,1,0:T(4,128)S(1)} %copy-done.5, bf16[64,256]{1,0:T(8,128)(2,1)S(1)} %copy-done.2, ...), custom_call_target="tpu_custom_call" | custom-call | bytes 1000000 | tf_op jit(solution)/shard_map/pallas_call | solution.py:371
  9.6 2.0 %collective-permute-start.3 = (bf16[192,384]{1,0:T(8,128)(2,1)S(1)}, bf16[192,384]{1,0:T(8,128)(2,1)S(1)}, u32[]{:S(2)}, u32[]{:S(2)}) collective-permute-start(bf16[192,384]{1,0:T(8,128)(2,1)S(1)} %get-tuple-element.29), channel_id=1, source_target_pairs={{0,2},{2,0},{4,6},{6,4},{1,3},{3,1},{5,7},{7,5},{8,10},{10,8},{12,... | collective-permute-start | bytes 442376 | tf_op jit(solution)/shard_map/ppermute | solution.py:318
  11.6 1.5 %collective-permute-start.4 = (bf16[192,384]{1,0:T(8,128)(2,1)S(1)}, bf16[192,384]{1,0:T(8,128)(2,1)S(1)}, u32[]{:S(2)}, u32[]{:S(2)}) collective-permute-start(bf16[192,384]{1,0:T(8,128)(2,1)S(1)} %get-tuple-element.30), channel_id=1, source_target_pairs={{0,4},{2,6},{4,0},{6,2},{1,5},{3,7},{5,1},{7,3},{8,12},{10,14},{12... | collective-permute-start | bytes 442376 | tf_op jit(solution)/shard_map/ppermute | solution.py:318
  13.1 0.0 collective-permute-done.refs_1_
  13.1 0.0 collective-permute-start.5
  13.2 0.0 collective-permute-done.1.refs_2_
  13.2 0.0 collective-permute-done.2.refs_3_
  13.2 0.0 slice-start
  13.2 0.0 slice-start.3
  13.2 3.5 %shard_map.132 = (f32[512,384]{1,0:T(8,128)S(1)}, bf16[512,384]{1,0:T(8,128)(2,1)S(1)}) custom-call(s32[6]{0:T(128)S(1)} %stack.20.pos_ref.refs_0_, bf16[128,384]{1,0:T(8,128)(2,1)S(1)} %bitcast.23, bf16[128,384]{1,0:T(8,128)(2,1)S(1)} %collective-permute-done.refs_1_, bf16[128,384]{1,0:T(8,128)(2,1)S(1)} %collective-permute-done.1.refs_2_, ...), custom_call_target="tpu_custom_call" | custom-call | flops 1926758400 | bytes 1966080 | tf_op jit(solution)/shard_map/pallas_call | solution.py:388
  16.7 0.1 collective-permute-start.7
  16.8 0.0 collective-permute-done.3.refs_1_
  16.8 3.1 %collective-permute-done.4.refs_2_ = bf16[192,384]{1,0:T(8,128)(2,1)S(1)} collective-permute-done((bf16[192,384]{1,0:T(8,128)(2,1)S(1)}, bf16[192,384]{1,0:T(8,128)(2,1)S(1)}, u32[]{:S(2)}, u32[]{:S(2)}) %collective-permute-start.4) | collective-permute-done | bytes 147488 | tf_op jit(solution)/shard_map/ppermute | solution.py:318
  19.8 0.0 collective-permute-done.5.refs_3_
  19.8 0.0 copy-start.3
  19.9 0.0 copy-start.4
  19.9 3.5 %shard_map.133 = (f32[512,384]{1,0:T(8,128)S(1)}, bf16[512,384]{1,0:T(8,128)(2,1)S(1)}) custom-call(s32[6]{0:T(128)S(1)} %stack.20.pos_ref.refs_0_, bf16[192,384]{1,0:T(8,128)(2,1)S(1)} %get-tuple-element.28.refs_0_, bf16[192,384]{1,0:T(8,128)(2,1)S(1)} %collective-permute-done.3.refs_1_, bf16[192,384]{1,0:T(8,128)(2,1)S(1)} %collective-permute-done.4.refs_2_, ...), custom_call_target="tpu_custom_call" | custom-call | flops 1926758400 | bytes 1966080 | tf_op jit(solution)/shard_map/pallas_call | solution.py:388
  23.4 0.1 collective-permute-start.8
  23.4 0.0 copy-done.6
  23.5 0.0 copy-done.7
  23.5 1.1 %shard_map.134 = (bf16[576,512]{1,0:T(8,128)(2,1)S(1)}, bf16[64,256]{1,0:T(8,128)(2,1)S(1)}, f32[64,128]{1,0:T(8,128)S(1)}, bf16[256,256]{1,0:T(8,128)(2,1)S(1)}) custom-call(s32[6]{0:T(128)S(1)} %stack.20.pos_ref.refs_0_, bf16[192,384]{1,0:T(8,128)(2,1)S(1)} %get-tuple-element.28.refs_0_, bf16[192,384]{1,0:T(8,128)(2,1)S(1)} %collective-permute-done.3.refs_1_, ...), custom_call_target="tpu_custom_call" | custom-call | flops 100000000 | bytes 1000000 | tf_op jit(solution)/shard_map/pallas_call | solution.py:407
  24.5 1.6 %collective-permute-start.6 = (bf16[256,256]{1,0:T(8,128)(2,1)S(1)}, bf16[256,256]{1,0:T(8,128)(2,1)S(1)}, u32[]{:S(2)}, u32[]{:S(2)}) collective-permute-start(bf16[256,256]{1,0:T(8,128)(2,1)S(1)} %get-tuple-element.34.refs_0_.refs_7_), channel_id=1, source_target_pairs={{0,8},{8,0},{16,24},{24,16},{1,9},{9,1},{17,25},{25,17},{2,10},{10... | collective-permute-start | bytes 393224 | tf_op jit(solution)/shard_map/ppermute | solution.py:318
  26.2 0.0 collective-permute-done.7.refs_2_
  26.2 0.0 collective-permute-done.8.refs_3_
  26.2 0.0 slice-done.2
  26.2 0.0 slice-done
  26.2 0.0 slice-done.3
  26.2 0.0 slice-done.1
  26.2 0.0 copy-done.3
  26.2 0.0 copy-done.4
  26.3 4.3 %shard_map.135 = (f32[256,1536]{1,0:T(8,128)S(1)}, bf16[256,1536]{1,0:T(8,128)(2,1)S(1)}) custom-call(s32[6]{0:T(128)S(1)} %stack.20.pos_ref.refs_0_, f32[512,384]{1,0:T(8,128)S(1)} %get-tuple-element.26.refs_0_, f32[512,384]{1,0:T(8,128)S(1)} %get-tuple-element.32.refs_1_, f32[512,384]{1,0:T(8,128)S(1)} %collective-permute-done.7.refs_2_, ...), custom_call_target="tpu_custom_call" | custom-call | flops 2415919104 | bytes 9437184 | tf_op jit(solution)/shard_map/pallas_call | solution.py:431
  30.5 0.3 collective-permute-start.10
  30.8 0.0 collective-permute-done.6.refs_1_.refs_8_
  30.8 4.3 %shard_map.136 = (f32[256,1536]{1,0:T(8,128)S(1)}, bf16[256,1536]{1,0:T(8,128)(2,1)S(1)}) custom-call(s32[6]{0:T(128)S(1)} %stack.20.pos_ref.refs_0_, f32[512,384]{1,0:T(8,128)S(1)} %get-tuple-element.26.refs_0_, f32[512,384]{1,0:T(8,128)S(1)} %get-tuple-element.32.refs_1_, f32[512,384]{1,0:T(8,128)S(1)} %collective-permute-done.7.refs_2_, ...), custom_call_target="tpu_custom_call" | custom-call | flops 2415919104 | bytes 9437184 | tf_op jit(solution)/shard_map/pallas_call | solution.py:431
  35.1 0.4 collective-permute-start.9
  35.5 2.7 %collective-permute-start.15 = (bf16[512,256]{1,0:T(8,128)(2,1)S(1)}, bf16[512,256]{1,0:T(8,128)(2,1)S(1)}, u32[]{:S(2)}, u32[]{:S(2)}) collective-permute-start(bf16[512,256]{1,0:T(8,128)(2,1)S(1)} %shard_map.140), channel_id=1, source_target_pairs={{0,16},{8,24},{16,0},{24,8},{1,17},{9,25},{17,1},{25,9},{2,18},{10... | collective-permute-start | bytes 786440 | tf_op jit(solution)/shard_map/ppermute | solution.py:318
  38.2 0.0 collective-permute-done.10.other_ref
  38.2 0.0 copy-done
  38.2 1.0 %shard_map.137.first_ref = bf16[256,1024]{1,0:T(8,128)(2,1)S(1)} custom-call(f32[256,1536]{1,0:T(8,128)S(1)} %get-tuple-element.39.z_ref, bf16[256,1536]{1,0:T(8,128)(2,1)S(1)} %collective-permute-done.10.other_ref, bf16[1536,1024]{1,0:T(8,128)(2,1)S(1)} %copy-done), custom_call_target="tpu_custom_call" | custom-call | flops 805306368 | bytes 3145728 | tf_op jit(solution)/shard_map/pallas_call | solution.py:451
  39.2 0.0 collective-permute-done.9.other_ref
  39.2 0.0 slice-done.4
  39.2 0.0 slice-done.5
  39.2 2.8 %shard_map.138.a_ref = f32[64,256]{1,0:T(8,128)S(1)} custom-call(f32[256,1536]{1,0:T(8,128)S(1)} %get-tuple-element.41.z_ref, bf16[256,1536]{1,0:T(8,128)(2,1)S(1)} %collective-permute-done.9.other_ref, bf16[256,1024]{1,0:T(8,128)(2,1)S(1)} %shard_map.137.first_ref, bf16[1536,1024]{1,0:T(8,128)(2,1)S(1)} %copy-done, bf16[9,1024,256]{2,1,0:T(8,128)(2,1)S(1)} %bitcast.18, ...), custom_call_target="tpu_custom_call" | custom-call | flops 2013265920 | bytes 6291456 | tf_op jit(solution)/shard_map/pallas_call | solution.py:460
  42.1 0.1 collective-permute-start.11
  42.2 1.2 %collective-permute-done.11.b_ref = f32[64,256]{1,0:T(8,128)S(1)} collective-permute-done((f32[64,256]{1,0:T(8,128)S(1)}, f32[64,256]{1,0:T(8,128)S(1)}, u32[]{:S(2)}, u32[]{:S(2)}) %collective-permute-start.11) | collective-permute-done | bytes 65568 | tf_op jit(solution)/shard_map/ppermute | solution.py:318
  43.4 0.7 %collective-permute-start.12 = (f32[64,256]{1,0:T(8,128)S(1)}, f32[64,256]{1,0:T(8,128)S(1)}, u32[]{:S(2)}, u32[]{:S(2)}) collective-permute-start(f32[64,256]{1,0:T(8,128)S(1)} %shard_map.139.refs_1_), channel_id=1, source_target_pairs={{0,2},{2,0},{4,6},{6,4},{1,3},{3,1},{5,7},{7,5},{8,10},{10,8},{12,... | collective-permute-start | bytes 196616 | tf_op jit(solution)/shard_map/ppermute | solution.py:318
  44.1 0.8 %collective-permute-start.13 = (f32[64,256]{1,0:T(8,128)S(1)}, f32[64,256]{1,0:T(8,128)S(1)}, u32[]{:S(2)}, u32[]{:S(2)}) collective-permute-start(f32[64,256]{1,0:T(8,128)S(1)} %shard_map.139.refs_1_), channel_id=1, source_target_pairs={{0,4},{2,6},{4,0},{6,2},{1,5},{3,7},{5,1},{7,3},{8,12},{10,14},{12... | collective-permute-start | bytes 196616 | tf_op jit(solution)/shard_map/ppermute | solution.py:318
  44.9 2.0 %collective-permute-start.14 = (f32[64,256]{1,0:T(8,128)S(1)}, f32[64,256]{1,0:T(8,128)S(1)}, u32[]{:S(2)}, u32[]{:S(2)}) collective-permute-start(f32[64,256]{1,0:T(8,128)S(1)} %shard_map.139.refs_1_), channel_id=1, source_target_pairs={{0,6},{2,4},{4,2},{6,0},{1,7},{3,5},{5,3},{7,1},{8,14},{10,12},{12... | collective-permute-start | bytes 196616 | tf_op jit(solution)/shard_map/ppermute | solution.py:318
  47.0 3.5 %collective-permute-done.15.refs_9_ = bf16[512,256]{1,0:T(8,128)(2,1)S(1)} collective-permute-done((bf16[512,256]{1,0:T(8,128)(2,1)S(1)}, bf16[512,256]{1,0:T(8,128)(2,1)S(1)}, u32[]{:S(2)}, u32[]{:S(2)}) %collective-permute-start.15) | collective-permute-done | bytes 262176 | tf_op jit(solution)/shard_map/ppermute | solution.py:318
  50.5 0.0 collective-permute-done.12.refs_2_
  50.5 0.0 collective-permute-done.13.refs_3_
  50.5 0.0 collective-permute-done.14.refs_4_
  50.5 2.0 %shard_map.141 = (f32[64,256]{1,0:T(8,128)}, f32[1,64]{1,0:T(1,128)}) custom-call(s32[6]{0:T(128)S(1)} %stack.20.pos_ref.refs_0_, f32[64,256]{1,0:T(8,128)S(1)} %shard_map.139.refs_1_, f32[64,256]{1,0:T(8,128)S(1)} %collective-permute-done.12.refs_2_, f32[64,256]{1,0:T(8,128)S(1)} %collective-permute-done.13.refs_3_, ...), custom_call_target="tpu_custom_call" | custom-call | flops 100000000 | bytes 1000000 | tf_op jit(solution)/shard_map/pallas_call | solution.py:483
  (12 shorter events, 0.0 us)
Async XLA Ops:
  2.0 11.2 %collective-permute-start = (bf16[128,384]{1,0:T(8,128)(2,1)S(1)}, bf16[128,384]{1,0:T(8,128)(2,1)S(1)}, u32[]{:S(2)}, u32[]{:S(2)}) collective-permute-start(bf16[128,384]{1,0:T(8,128)(2,1)S(1)} %bitcast.26), channel_id=1, source_target_pairs={{0,2},{2,0},{4,6},{6,4},{1,3},{3,1},{5,7},{7,5},{8,10},{10,8},{12,... | collective-permute-start | bytes 294920 | tf_op jit(solution)/shard_map/ppermute | solution.py:318
  5.0 8.2 %collective-permute-start.1 = (bf16[128,384]{1,0:T(8,128)(2,1)S(1)}, bf16[128,384]{1,0:T(8,128)(2,1)S(1)}, u32[]{:S(2)}, u32[]{:S(2)}) collective-permute-start(bf16[128,384]{1,0:T(8,128)(2,1)S(1)} %bitcast.25), channel_id=1, source_target_pairs={{0,4},{2,6},{4,0},{6,2},{1,5},{3,7},{5,1},{7,3},{8,12},{10,14},{12... | collective-permute-start | bytes 294920 | tf_op jit(solution)/shard_map/ppermute | solution.py:318
  6.5 6.7 %collective-permute-start.2 = (bf16[128,384]{1,0:T(8,128)(2,1)S(1)}, bf16[128,384]{1,0:T(8,128)(2,1)S(1)}, u32[]{:S(2)}, u32[]{:S(2)}) collective-permute-start(bf16[128,384]{1,0:T(8,128)(2,1)S(1)} %bitcast.24), channel_id=1, source_target_pairs={{0,6},{2,4},{4,2},{6,0},{1,7},{3,5},{5,3},{7,1},{8,14},{10,12},{12... | collective-permute-start | bytes 294920 | tf_op jit(solution)/shard_map/ppermute | solution.py:318
  6.6 0.9 %copy-start.1 = (bf16[7,7,1536]{2,1,0:T(8,128)(2,1)S(1)}, bf16[7,7,1536]{2,1,0:T(8,128)(2,1)}, u32[]{:S(2)}) copy-start(bf16[7,7,1536]{2,1,0:T(8,128)(2,1)} %dw_ref.1) | copy-start | bytes 451588
  7.5 0.8 %copy-start.2 = (bf16[64,256]{1,0:T(8,128)(2,1)S(1)}, bf16[64,256]{1,0:T(8,128)(2,1)}, u32[]{:S(2)}) copy-start(bf16[64,256]{1,0:T(8,128)(2,1)} %key_ref.1) | copy-start | bytes 98308
  8.3 0.7 %copy-start.5 = (s32[4,4,32]{2,1,0:T(4,128)S(1)}, s32[4,4,32]{2,1,0:T(4,128)}, u32[]{:S(2)}) copy-start(s32[4,4,32]{2,1,0:T(4,128)} %ids_ref.1) | copy-start | bytes 6148
  9.0 17.2 %slice-start.2 = ((s8[4718592]{0:T(1024)(128)(4,1)}), s8[4194304]{0:T(1024)(128)(4,1)S(1)}, s32[]{:S(2)}) async-start(s8[4718592]{0:T(1024)(128)(4,1)} %bitcast.15), calls=%async_computation.2 | async-start | bytes 8388608
  9.6 7.2 %collective-permute-start.3 = (bf16[192,384]{1,0:T(8,128)(2,1)S(1)}, bf16[192,384]{1,0:T(8,128)(2,1)S(1)}, u32[]{:S(2)}, u32[]{:S(2)}) collective-permute-start(bf16[192,384]{1,0:T(8,128)(2,1)S(1)} %get-tuple-element.29), channel_id=1, source_target_pairs={{0,2},{2,0},{4,6},{6,4},{1,3},{3,1},{5,7},{7,5},{8,10},{10,8},{12,... | collective-permute-start | bytes 442376 | tf_op jit(solution)/shard_map/ppermute | solution.py:318
  11.6 8.2 %collective-permute-start.4 = (bf16[192,384]{1,0:T(8,128)(2,1)S(1)}, bf16[192,384]{1,0:T(8,128)(2,1)S(1)}, u32[]{:S(2)}, u32[]{:S(2)}) collective-permute-start(bf16[192,384]{1,0:T(8,128)(2,1)S(1)} %get-tuple-element.30), channel_id=1, source_target_pairs={{0,4},{2,6},{4,0},{6,2},{1,5},{3,7},{5,1},{7,3},{8,12},{10,14},{12... | collective-permute-start | bytes 442376 | tf_op jit(solution)/shard_map/ppermute | solution.py:318
  13.1 6.7 %collective-permute-start.5 = (bf16[192,384]{1,0:T(8,128)(2,1)S(1)}, bf16[192,384]{1,0:T(8,128)(2,1)S(1)}, u32[]{:S(2)}, u32[]{:S(2)}) collective-permute-start(bf16[192,384]{1,0:T(8,128)(2,1)S(1)} %get-tuple-element.31), channel_id=1, source_target_pairs={{0,6},{2,4},{4,2},{6,0},{1,7},{3,5},{5,3},{7,1},{8,14},{10,12},{12... | collective-permute-start | bytes 442376 | tf_op jit(solution)/shard_map/ppermute | solution.py:318
  13.2 13.0 %slice-start = ((s8[4718592]{0:T(1024)(128)(4,1)}), s8[4194304]{0:T(1024)(128)(4,1)S(1)}, s32[]{:S(2)}) async-start(s8[4718592]{0:T(1024)(128)(4,1)} %bitcast.13), calls=%async_computation | async-start | bytes 8388608
  13.2 13.0 %slice-start.3 = ((s8[4718592]{0:T(1024)(128)(4,1)}), s8[524288]{0:T(1024)(128)(4,1)S(1)}, s32[]{:S(2)}) async-start(s8[4718592]{0:T(1024)(128)(4,1)} %bitcast.15), calls=%async_computation.3 | async-start | bytes 1048576
  16.7 9.5 %collective-permute-start.7 = (f32[512,384]{1,0:T(8,128)S(1)}, f32[512,384]{1,0:T(8,128)S(1)}, u32[]{:S(2)}, u32[]{:S(2)}) collective-permute-start(f32[512,384]{1,0:T(8,128)S(1)} %get-tuple-element.26.refs_0_), channel_id=1, source_target_pairs={{0,1},{1,0},{2,3},{3,2},{4,5},{5,4},{6,7},{7,6},{8,9},{9,8},{10,11... | collective-permute-start | bytes 2359304 | tf_op jit(solution)/shard_map/ppermute | solution.py:318
  19.8 3.6 %copy-start.6 = (s32[4,64]{1,0:T(4,128)S(1)}, s32[4,64]{1,0:T(4,128)}, u32[]{:S(2)}) copy-start(s32[4,64]{1,0:T(4,128)} %refs_5_.1) | copy-start | bytes 3076
  19.8 3.6 %copy-start.7 = (s32[1,256]{1,0:T(1,128)S(1)}, s32[1,256]{1,0:T(1,128)}, u32[]{:S(2)}) copy-start(s32[1,256]{1,0:T(1,128)} %refs_4_.1) | copy-start | bytes 3076
  19.8 6.4 %slice-start.1 = ((s8[4718592]{0:T(1024)(128)(4,1)}), s8[524288]{0:T(1024)(128)(4,1)S(1)}, s32[]{:S(2)}) async-start(s8[4718592]{0:T(1024)(128)(4,1)} %bitcast.13), calls=%async_computation.1 | async-start | bytes 1048576
  19.8 6.4 %copy-start.3 = (bf16[1536]{0:T(1024)(128)(2,1)S(1)}, bf16[1536]{0:T(1024)(128)(2,1)}, u32[]{:S(2)}) copy-start(bf16[1536]{0:T(1024)(128)(2,1)} %refs_6_.3) | copy-start | bytes 9220
  19.9 6.4 %copy-start.4 = (bf16[1536]{0:T(1024)(128)(2,1)S(1)}, bf16[1536]{0:T(1024)(128)(2,1)}, u32[]{:S(2)}) copy-start(bf16[1536]{0:T(1024)(128)(2,1)} %refs_7_.3) | copy-start | bytes 9220
  23.4 2.8 %collective-permute-start.8 = (f32[512,384]{1,0:T(8,128)S(1)}, f32[512,384]{1,0:T(8,128)S(1)}, u32[]{:S(2)}, u32[]{:S(2)}) collective-permute-start(f32[512,384]{1,0:T(8,128)S(1)} %get-tuple-element.32.refs_1_), channel_id=1, source_target_pairs={{0,1},{1,0},{2,3},{3,2},{4,5},{5,4},{6,7},{7,6},{8,9},{9,8},{10,11... | collective-permute-start | bytes 2359304 | tf_op jit(solution)/shard_map/ppermute | solution.py:318
  24.5 6.3 %collective-permute-start.6 = (bf16[256,256]{1,0:T(8,128)(2,1)S(1)}, bf16[256,256]{1,0:T(8,128)(2,1)S(1)}, u32[]{:S(2)}, u32[]{:S(2)}) collective-permute-start(bf16[256,256]{1,0:T(8,128)(2,1)S(1)} %get-tuple-element.34.refs_0_.refs_7_), channel_id=1, source_target_pairs={{0,8},{8,0},{16,24},{24,16},{1,9},{9,1},{17,25},{25,17},{2,10},{10... | collective-permute-start | bytes 393224 | tf_op jit(solution)/shard_map/ppermute | solution.py:318
  30.5 7.6 %collective-permute-start.10 = (bf16[256,1536]{1,0:T(8,128)(2,1)S(1)}, bf16[256,1536]{1,0:T(8,128)(2,1)S(1)}, u32[]{:S(2)}, u32[]{:S(2)}) collective-permute-start(bf16[256,1536]{1,0:T(8,128)(2,1)S(1)} %get-tuple-element.43), channel_id=1, source_target_pairs={{0,1},{1,0},{2,3},{3,2},{4,5},{5,4},{6,7},{7,6},{8,9},{9,8},{10,11... | collective-permute-start | bytes 2359304 | tf_op jit(solution)/shard_map/ppermute | solution.py:318
  30.8 8.4 %slice-start.4 = ((s8[4718592]{0:T(1024)(128)(4,1)}), s8[4194304]{0:T(1024)(128)(4,1)S(1)}, s32[]{:S(2)}) async-start(s8[4718592]{0:T(1024)(128)(4,1)} %bitcast.17), calls=%async_computation.4 | async-start | bytes 8388608
  30.8 7.4 %copy-start = (bf16[1536,1024]{1,0:T(8,128)(2,1)S(1)}, bf16[1536,1024]{1,0:T(8,128)(2,1)}, u32[]{:S(2)}) copy-start(bf16[1536,1024]{1,0:T(8,128)(2,1)} %pe_ref.3) | copy-start | bytes 9437188
  30.8 8.4 %slice-start.5 = ((s8[4718592]{0:T(1024)(128)(4,1)}), s8[524288]{0:T(1024)(128)(4,1)S(1)}, s32[]{:S(2)}) async-start(s8[4718592]{0:T(1024)(128)(4,1)} %bitcast.17), calls=%async_computation.5 | async-start | bytes 1048576
  35.1 4.1 %collective-permute-start.9 = (bf16[256,1536]{1,0:T(8,128)(2,1)S(1)}, bf16[256,1536]{1,0:T(8,128)(2,1)S(1)}, u32[]{:S(2)}, u32[]{:S(2)}) collective-permute-start(bf16[256,1536]{1,0:T(8,128)(2,1)S(1)} %get-tuple-element.42), channel_id=1, source_target_pairs={{0,1},{1,0},{2,3},{3,2},{4,5},{5,4},{6,7},{7,6},{8,9},{9,8},{10,11... | collective-permute-start | bytes 2359304 | tf_op jit(solution)/shard_map/ppermute | solution.py:318
  35.5 15.0 %collective-permute-start.15 = (bf16[512,256]{1,0:T(8,128)(2,1)S(1)}, bf16[512,256]{1,0:T(8,128)(2,1)S(1)}, u32[]{:S(2)}, u32[]{:S(2)}) collective-permute-start(bf16[512,256]{1,0:T(8,128)(2,1)S(1)} %shard_map.140), channel_id=1, source_target_pairs={{0,16},{8,24},{16,0},{24,8},{1,17},{9,25},{17,1},{25,9},{2,18},{10... | collective-permute-start | bytes 786440 | tf_op jit(solution)/shard_map/ppermute | solution.py:318
  42.1 1.3 %collective-permute-start.11 = (f32[64,256]{1,0:T(8,128)S(1)}, f32[64,256]{1,0:T(8,128)S(1)}, u32[]{:S(2)}, u32[]{:S(2)}) collective-permute-start(f32[64,256]{1,0:T(8,128)S(1)} %shard_map.138.a_ref), channel_id=1, source_target_pairs={{0,1},{1,0},{2,3},{3,2},{4,5},{5,4},{6,7},{7,6},{8,9},{9,8},{10,11... | collective-permute-start | bytes 196616 | tf_op jit(solution)/shard_map/ppermute | solution.py:318
  43.4 7.1 %collective-permute-start.12 = (f32[64,256]{1,0:T(8,128)S(1)}, f32[64,256]{1,0:T(8,128)S(1)}, u32[]{:S(2)}, u32[]{:S(2)}) collective-permute-start(f32[64,256]{1,0:T(8,128)S(1)} %shard_map.139.refs_1_), channel_id=1, source_target_pairs={{0,2},{2,0},{4,6},{6,4},{1,3},{3,1},{5,7},{7,5},{8,10},{10,8},{12,... | collective-permute-start | bytes 196616 | tf_op jit(solution)/shard_map/ppermute | solution.py:318
  44.1 6.4 %collective-permute-start.13 = (f32[64,256]{1,0:T(8,128)S(1)}, f32[64,256]{1,0:T(8,128)S(1)}, u32[]{:S(2)}, u32[]{:S(2)}) collective-permute-start(f32[64,256]{1,0:T(8,128)S(1)} %shard_map.139.refs_1_), channel_id=1, source_target_pairs={{0,4},{2,6},{4,0},{6,2},{1,5},{3,7},{5,1},{7,3},{8,12},{10,14},{12... | collective-permute-start | bytes 196616 | tf_op jit(solution)/shard_map/ppermute | solution.py:318
  44.9 5.6 %collective-permute-start.14 = (f32[64,256]{1,0:T(8,128)S(1)}, f32[64,256]{1,0:T(8,128)S(1)}, u32[]{:S(2)}, u32[]{:S(2)}) collective-permute-start(f32[64,256]{1,0:T(8,128)S(1)} %shard_map.139.refs_1_), channel_id=1, source_target_pairs={{0,6},{2,4},{4,2},{6,0},{1,7},{3,5},{5,3},{7,1},{8,14},{10,12},{12... | collective-permute-start | bytes 196616 | tf_op jit(solution)/shard_map/ppermute | solution.py:318

commit v2 on v1

--- a/solution.py
+++ b/solution.py
@@ -49,22 +49,22 @@
     return hi, mid, (rest - mid.astype(f32)).astype(bf16)
 
 
-def pack_kernel(count, pos_ref, ids_ref, key_ref, dw_ref, *refs):
-    inputs, blocks = refs[:count], refs[count : 2 * count]
-    w_ref, line = refs[2 * count :]
-    pixels = inputs[0].shape[0]
+def blank_kernel(out_ref):
+    out_ref[...] = jnp.full(out_ref.shape, -1.0, f32)
+
+
+def pack_kernel(pos_ref, ids_ref, key_ref, dw_ref, blank_ref, tail_ref, w_ref, line):
+    section = pos_ref[3]
     keys, depth = key_ref.shape
     shard_rows, width = ids_ref.shape[1:]
-    line[...] = jnp.full(line.shape, -1.0, f32)
+    line[...] = blank_ref[...]
     for i in range(ids_ref.shape[0]):
         line[i * shard_rows : (i + 1) * shard_rows, 0:width] = ids_ref[i].astype(f32)
-    tail = line[...].astype(bf16)
-    for source, block in zip(inputs, blocks):
-        block[0:pixels, :] = source[...]
-        block[pixels : pixels + keys, 0:depth] = key_ref[...]
-        block[pixels:, depth : depth + LANES] = tail
+    tail_ref[...] = jnp.zeros(tail_ref.shape, bf16)
+    tail_ref[:, depth : depth + LANES] = line[...].astype(bf16)
+    tail_ref[0 : keys // 2, 0:depth] = key_ref[pl.ds(pl.multiple_of(section * (keys // 2), keys // 2), keys // 2), :]
     half = w_ref.shape[1]
-    lanes = pl.ds(pl.multiple_of(pos_ref[3] * half, LANES), half)
+    lanes = pl.ds(pl.multiple_of(section * half, LANES), half)
     for dy in range(7):
         w_ref[dy * 7 : dy * 7 + 7, :] = dw_ref[dy, :, lanes].astype(f32)
 
@@ -189,14 +189,15 @@
 
 
 def prep_kernel(geo, pos_ref, *refs):
-    shards, shard_rows, width, out_pixels, images, per_key, parts = geo
+    shards, shard_rows, width, out_pixels, images, batches, per_key, parts = geo
     ids = refs[:shards]
     owner_ref, partner_ref, hot_ref, pick_ref, own_ref, keys_ref, flat = refs[shards:]
     row, first_row, batch, first_slot = pos_ref[0], pos_ref[1], pos_ref[4], pos_ref[5]
     pixels = shard_rows * width
     depth = keys_ref.shape[1]
     for k in range(shards):
-        keys_ref[k * per_key : (k + 1) * per_key, :] = ids[k][pixels : pixels + per_key, 0:depth]
+        mine = slice(k * per_key // 2, (k + 1) * per_key // 2)
+        keys_ref[mine, :] = ids[k][pixels : pixels + per_key // 2, 0:depth]
     ids = [ref[pixels:, depth : depth + LANES].astype(f32) for ref in ids]
     owned = own_ref.shape[0]
     slots = images * REG
@@ -248,8 +249,10 @@
     mates = jnp.concatenate([partner_ref[i : i + 1, :] for i in range(images)], axis=1)
     mate = (batch * images + slot // REG) * REG + mates
     block = mate // per_key
-    place = ((block // shards) ^ batch) * shards + ((block % shards) ^ row)
-    place = place * per_key + mate % per_key
+    within = mate % per_key
+    core = (within // (per_key // 2)) ^ pos_ref[3]
+    place = (core * batches + ((block // shards) ^ batch)) * shards + ((block % shards) ^ row)
+    place = place * (per_key // 2) + within % (per_key // 2)
     place = jnp.sum(jnp.where(pick, place, 0).astype(f32), axis=1, keepdims=True)
     number = jnp.sum(jnp.where(pick, count, 0.0), axis=1, keepdims=True)
     side = lax.broadcasted_iota(jnp.int32, (owned, LANES), 1)
@@ -356,30 +359,31 @@
     ).astype(jnp.int32)
 
     per_key, depth = key_embed.shape
-    tail = max(-(-images * shard_rows // 16) * 16, per_key)
+    tail = max(-(-images * shard_rows // 16) * 16, per_key // 2)
     def after(here, *done):
         return lax.optimization_barrier((here, *done))[0]
 
-    parcels = []
+    (blank,) = call(
+        blank_kernel, [jax.ShapeDtypeStruct((tail, LANES), f32)], [], [], mib, 10**10, 10**4
+    )()
+    riders, weights = call(
+        pack_kernel,
+        [jax.ShapeDtypeStruct((tail, span), bf16), jax.ShapeDtypeStruct((49, half), f32)],
+        [SMEM] + [VMEM] * 4,
+        [pltpu.VMEM((tail, LANES), f32)],
+        mib,
+        0,
+        10**6,
+    )(spot, region_ids, key_embed, dw_kernel, blank)
+    got = []
     for c in range(CHUNKS):
         blocks = []
         for k in range(shards):
             place = ((row ^ k) // parts, 0, 0, section * half + c * span)
-            part = lax.dynamic_slice(features, place, (1, shard_rows, width, span))
-            blocks.append(part.reshape(pixels, span))
-        parcels.append(blocks)
-    *parcels[-1], weights = call(
-        functools.partial(pack_kernel, shards),
-        [jax.ShapeDtypeStruct((pixels + tail, span), bf16)] * shards
-        + [jax.ShapeDtypeStruct((49, half), f32)],
-        [SMEM] + [VMEM] * (3 + shards),
-        [pltpu.VMEM((tail, LANES), f32)],
-        mib,
-        0,
-        10**6,
-    )(spot, region_ids, key_embed, dw_kernel, *parcels[-1])
-    got = []
-    for blocks in parcels:
+            part = lax.dynamic_slice(features, place, (1, shard_rows, width, span)).reshape(pixels, span)
+            if c == CHUNKS - 1:
+                part = jnp.concatenate([part, riders], axis=0)
+            blocks.append(part)
         got.append([blocks[0]] + [swap(blocks[k], "rows", k) for k in range(1, shards)])
 
     own, other, img = [], [], []
@@ -407,13 +411,13 @@
     hot, pick, facts, keys = call(
         functools.partial(
             prep_kernel,
-            (shards, shard_rows, width, out_pixels, images, per_key, parts),
+            (shards, shard_rows, width, out_pixels, images, batches, per_key, parts),
         ),
         [
             jax.ShapeDtypeStruct((9 * REG, out_pixels), bf16),
             jax.ShapeDtypeStruct((owned, slots), bf16),
             jax.ShapeDtypeStruct((owned, LANES), f32),
-            jax.ShapeDtypeStruct((shards * per_key, depth), bf16),
+            jax.ShapeDtypeStruct((shards * per_key // 2, depth), bf16),
         ],
         [SMEM] + [VMEM] * (shards + 2),
         [pltpu.VMEM((16, (shards + 2) * pixels), f32)],
@@ -446,7 +450,6 @@
     while bit < batches:
         pieces.append(swap(join(*pieces), "batch", bit))
         bit *= 2
-
     hidden = pe.shape[1]
     (hid_a,) = call(
         expand_kernel,
@@ -478,6 +481,8 @@
         10**5,
         10**5,
     )(pooled, swap(pooled, "section", 1))
+    pieces[-1] = after(pieces[-1], pooled)
+    pieces.append(swap(join(*pieces), "section", 1))
     sums = [pooled] + [swap(pooled, "rows", k) for k in range(1, shards)]
 
     embed, loss = call(

time: 52.8 us -> 51.5 us (0.975)
  local copies, waits for them, and re-layouts: 3.83 us -> 2.27 us
    unnamed x28, local copies, waits for them, and re-layouts: 2.42 us -> 0.87 us
    ppermute x16 -> x17, waiting for transfers between devices: 7.87 us -> 8.24 us  [swap(): lax.ppermute(x, axis, [(i, i ^ bit) for i in range(lax.axis_size(axis))])]
    ppermute x16 -> x17, starting transfers between devices: 16.8 us -> 16.9 us  [swap(): lax.ppermute(x, axis, [(i, i ^ bit) for i in range(lax.axis_size(axis))])]
  transfers between devices with their start and end apart: 16 -> 17, of which waited for: 3 -> 7; matrix products, arithmetic and copies ran while one was open for 0% -> 0% of each run, Pallas kernels for 40% -> 41%
where the time goes in v2:
time: 51.5 us; the launch traced here: 51.3 us
  Pallas kernels  23 us (45%)
  starting transfers between devices  16.9 us (33%)
  waiting for transfers between devices  8.24 us (16%)
  local copies, waits for them, and re-layouts  2.27 us (4%)
  between operations  0.95 us (2%)
    ppermute x17, starting transfers between devices, swap(): lax.ppermute(x, axis, [(i, i ^ bit) for i in range(lax.axis_size(axis))])  16.9 us
    pallas_call x2, Pallas kernels, body(): call(functools.partial(block_kernel, (p * part_pixels, part_pixels, CHUNK...  8.56 us
    ppermute x17, waiting for transfers between devices, swap(): lax.ppermute(x, axis, [(i, i ^ bit) for i in range(lax.axis_size(axis))])  8.24 us
    pallas_call x2, Pallas kernels, body(): call(functools.partial(conv_kernel, (shards, shard_rows, width, out_rows,...  6.97 us
    pallas_call x1, Pallas kernels, body(): call(project_kernel, [jax.ShapeDtypeStruct((REG, out_dim), f32)], [VMEM]...  2.84 us
    pallas_call x1, Pallas kernels, body(): call(functools.partial(loss_kernel, (shards, parts)), [jax.ShapeDtypeStru...  1.95 us
    dynamic_slice x1, local copies, waits for them, and re-layouts, body(): lax.dynamic_slice(features, place, (1, shard_rows, width, span))  1.32 us
  transfers between devices with their start and end apart: 17, of which 7 were waited for; matrix products, arithmetic and copies ran while one was open for 0% of the time, Pallas kernels for 41%

profile of v2, /device:TPU:0, one launch (start us, length us, event | category | flops | bytes accessed | tf_op | source)
XLA Modules:
  0.0 51.3 jit_solution(9901758832809401373)
XLA Ops:
  0.7 1.3 %constant_dynamic-slice_fusion = (bf16[1,4,32,384]{3,2,1,0:T(8,128)(2,1)S(1)}, bf16[1,4,32,384]{3,2,1,0:T(8,128)(2,1)S(1)}, bf16[1,4,32,384]{3,2,1,0:T(8,128)(2,...) fusion(bf16[4,4,32,1536]{3,2,1,0:T(8,128)(2,1)} %param.12, ...), kind=kLoop, calls=%fused_computation.4 | loop fusion | bytes 1572888 | tf_op jit(solution)/shard_map/dynamic_slice | solution.py:383
  2.0 3.0 %collective-permute-start = (bf16[128,384]{1,0:T(8,128)(2,1)S(1)}, bf16[128,384]{1,0:T(8,128)(2,1)S(1)}, u32[]{:S(2)}, u32[]{:S(2)}) collective-permute-start(bf16[128,384]{1,0:T(8,128)(2,1)S(1)} %bitcast.26), channel_id=1, source_target_pairs={{0,2},{2,0},{4,6},{6,4},{1,3},{3,1},{5,7},{7,5},{8,10},{10,8},{12,... | collective-permute-start | bytes 294920 | tf_op jit(solution)/shard_map/ppermute | solution.py:321
  5.0 1.5 %collective-permute-start.1 = (bf16[128,384]{1,0:T(8,128)(2,1)S(1)}, bf16[128,384]{1,0:T(8,128)(2,1)S(1)}, u32[]{:S(2)}, u32[]{:S(2)}) collective-permute-start(bf16[128,384]{1,0:T(8,128)(2,1)S(1)} %bitcast.25), channel_id=1, source_target_pairs={{0,4},{2,6},{4,0},{6,2},{1,5},{3,7},{5,1},{7,3},{8,12},{10,14},{12... | collective-permute-start | bytes 294920 | tf_op jit(solution)/shard_map/ppermute | solution.py:321
  6.5 0.0 collective-permute-start.2
  6.5 0.0 copy-start.1
  6.5 0.1 stack.20.pos_ref.refs_0_
  6.6 0.8 %copy-done.1 = bf16[7,7,1536]{2,1,0:T(8,128)(2,1)S(1)} copy-done((bf16[7,7,1536]{2,1,0:T(8,128)(2,1)S(1)}, bf16[7,7,1536]{2,1,0:T(8,128)(2,1)}, u32[]{:S(2)}) %copy-start.1) | copy-done | bytes 150552
  7.4 0.0 copy-done.2
  7.4 0.0 copy-done.5
  7.4 0.6 %shard_map.132 = (bf16[32,384]{1,0:T(8,128)(2,1)S(1)}, f32[49,768]{1,0:T(8,128)S(1)}) custom-call(s32[6]{0:T(128)S(1)} %stack.20.pos_ref.refs_0_, s32[4,4,32]{2,1,0:T(4,128)S(1)} %copy-done.5, bf16[64,256]{1,0:T(8,128)(2,1)S(1)} %copy-done.2, bf16[7,7,1536]{2,1,0:T(8,128)(2,1)S(1)} %copy-done.1, f32[32,128]{1,0:T(8,128)S(1)} %shard_map.131.blank_ref), custom_call_target="tpu_custom_call" | custom-call | bytes 1000000 | tf_op jit(solution)/shard_map/pallas_call | solution.py:369
  8.0 0.0 slice-start.2
  8.0 0.1 pad_maximum_fusion
  8.1 2.0 %collective-permute-start.3 = (bf16[160,384]{1,0:T(8,128)(2,1)S(1)}, bf16[160,384]{1,0:T(8,128)(2,1)S(1)}, u32[]{:S(2)}, u32[]{:S(2)}) collective-permute-start(bf16[160,384]{1,0:T(8,128)(2,1)S(1)} %get-tuple-element.53), channel_id=1, source_target_pairs={{0,2},{2,0},{4,6},{6,4},{1,3},{3,1},{5,7},{7,5},{8,10},{10,8},{12,... | collective-permute-start | bytes 368648 | tf_op jit(solution)/shard_map/ppermute | solution.py:321
  10.1 1.5 %collective-permute-start.4 = (bf16[160,384]{1,0:T(8,128)(2,1)S(1)}, bf16[160,384]{1,0:T(8,128)(2,1)S(1)}, u32[]{:S(2)}, u32[]{:S(2)}) collective-permute-start(bf16[160,384]{1,0:T(8,128)(2,1)S(1)} %get-tuple-element.54), channel_id=1, source_target_pairs={{0,4},{2,6},{4,0},{6,2},{1,5},{3,7},{5,1},{7,3},{8,12},{10,14},{12... | collective-permute-start | bytes 368648 | tf_op jit(solution)/shard_map/ppermute | solution.py:321
  11.6 0.0 collective-permute-done.refs_1_
  11.6 0.0 collective-permute-start.5
  11.6 0.0 collective-permute-done.1.refs_2_
  11.7 1.2 %collective-permute-done.2.refs_3_ = bf16[128,384]{1,0:T(8,128)(2,1)S(1)} collective-permute-done((bf16[128,384]{1,0:T(8,128)(2,1)S(1)}, bf16[128,384]{1,0:T(8,128)(2,1)S(1)}, u32[]{:S(2)}, u32[]{:S(2)}) %collective-permute-start.2) | collective-permute-done | bytes 98336 | tf_op jit(solution)/shard_map/ppermute | solution.py:321
  12.9 3.5 %shard_map.133 = (f32[512,384]{1,0:T(8,128)S(1)}, bf16[512,384]{1,0:T(8,128)(2,1)S(1)}) custom-call(s32[6]{0:T(128)S(1)} %stack.20.pos_ref.refs_0_, bf16[128,384]{1,0:T(8,128)(2,1)S(1)} %bitcast.19, bf16[128,384]{1,0:T(8,128)(2,1)S(1)} %collective-permute-done.refs_1_, bf16[128,384]{1,0:T(8,128)(2,1)S(1)} %collective-permute-done.1.refs_2_, ...), custom_call_target="tpu_custom_call" | custom-call | flops 1926758400 | bytes 1966080 | tf_op jit(solution)/shard_map/pallas_call | solution.py:392
  16.4 0.1 collective-permute-start.7
  16.4 0.0 collective-permute-done.3.refs_1_
  16.5 1.1 %collective-permute-done.4.refs_2_ = bf16[160,384]{1,0:T(8,128)(2,1)S(1)} collective-permute-done((bf16[160,384]{1,0:T(8,128)(2,1)S(1)}, bf16[160,384]{1,0:T(8,128)(2,1)S(1)}, u32[]{:S(2)}, u32[]{:S(2)}) %collective-permute-start.4) | collective-permute-done | bytes 122912 | tf_op jit(solution)/shard_map/ppermute | solution.py:321
  17.6 0.0 collective-permute-done.5.refs_3_
  17.6 0.0 copy-start.3
  17.6 0.0 copy-start.4
  17.6 3.5 %shard_map.134 = (f32[512,384]{1,0:T(8,128)S(1)}, bf16[512,384]{1,0:T(8,128)(2,1)S(1)}) custom-call(s32[6]{0:T(128)S(1)} %stack.20.pos_ref.refs_0_, bf16[160,384]{1,0:T(8,128)(2,1)S(1)} %get-tuple-element.55.refs_0_, bf16[160,384]{1,0:T(8,128)(2,1)S(1)} %collective-permute-done.3.refs_1_, bf16[160,384]{1,0:T(8,128)(2,1)S(1)} %collective-permute-done.4.refs_2_, ...), custom_call_target="tpu_custom_call" | custom-call | flops 1926758400 | bytes 1966080 | tf_op jit(solution)/shard_map/pallas_call | solution.py:392
  21.1 0.1 collective-permute-start.8
  21.2 0.0 copy-done.6
  21.2 0.0 copy-done.7
  21.2 1.0 %shard_map.135 = (bf16[576,512]{1,0:T(8,128)(2,1)S(1)}, bf16[64,256]{1,0:T(8,128)(2,1)S(1)}, f32[64,128]{1,0:T(8,128)S(1)}, bf16[128,256]{1,0:T(8,128)(2,1)S(1)}) custom-call(s32[6]{0:T(128)S(1)} %stack.20.pos_ref.refs_0_, bf16[160,384]{1,0:T(8,128)(2,1)S(1)} %get-tuple-element.55.refs_0_, bf16[160,384]{1,0:T(8,128)(2,1)S(1)} %collective-permute-done.3.refs_1_, ...), custom_call_target="tpu_custom_call" | custom-call | flops 100000000 | bytes 1000000 | tf_op jit(solution)/shard_map/pallas_call | solution.py:411
  22.2 1.6 %collective-permute-start.6 = (bf16[128,256]{1,0:T(8,128)(2,1)S(1)}, bf16[128,256]{1,0:T(8,128)(2,1)S(1)}, u32[]{:S(2)}, u32[]{:S(2)}) collective-permute-start(bf16[128,256]{1,0:T(8,128)(2,1)S(1)} %get-tuple-element.29.refs_0_.refs_7_), channel_id=1, source_target_pairs={{0,8},{8,0},{16,24},{24,16},{1,9},{9,1},{17,25},{25,17},{2,10},{10... | collective-permute-start | bytes 196616 | tf_op jit(solution)/shard_map/ppermute | solution.py:321
  23.9 0.0 collective-permute-done.7.refs_2_
  23.9 0.0 collective-permute-done.8.refs_3_
  23.9 0.0 slice-done.2
  23.9 0.0 slice-done
  23.9 0.0 slice-done.3
  23.9 0.0 slice-done.1
  23.9 0.0 copy-done.3
  23.9 0.0 copy-done.4
  23.9 4.3 %shard_map.136 = (f32[256,1536]{1,0:T(8,128)S(1)}, bf16[256,1536]{1,0:T(8,128)(2,1)S(1)}) custom-call(s32[6]{0:T(128)S(1)} %stack.20.pos_ref.refs_0_, f32[512,384]{1,0:T(8,128)S(1)} %get-tuple-element.24.refs_0_, f32[512,384]{1,0:T(8,128)S(1)} %get-tuple-element.27.refs_1_, f32[512,384]{1,0:T(8,128)S(1)} %collective-permute-done.7.refs_2_, ...), custom_call_target="tpu_custom_call" | custom-call | flops 2415919104 | bytes 9437184 | tf_op jit(solution)/shard_map/pallas_call | solution.py:435
  28.2 0.3 collective-permute-start.10
  28.5 0.0 collective-permute-done.6.refs_1_.refs_8_
  28.5 4.3 %shard_map.137 = (f32[256,1536]{1,0:T(8,128)S(1)}, bf16[256,1536]{1,0:T(8,128)(2,1)S(1)}) custom-call(s32[6]{0:T(128)S(1)} %stack.20.pos_ref.refs_0_, f32[512,384]{1,0:T(8,128)S(1)} %get-tuple-element.24.refs_0_, f32[512,384]{1,0:T(8,128)S(1)} %get-tuple-element.27.refs_1_, f32[512,384]{1,0:T(8,128)S(1)} %collective-permute-done.7.refs_2_, ...), custom_call_target="tpu_custom_call" | custom-call | flops 2415919104 | bytes 9437184 | tf_op jit(solution)/shard_map/pallas_call | solution.py:435
  32.8 0.4 collective-permute-start.9
  33.2 2.7 %collective-permute-start.15 = (bf16[256,256]{1,0:T(8,128)(2,1)S(1)}, bf16[256,256]{1,0:T(8,128)(2,1)S(1)}, u32[]{:S(2)}, u32[]{:S(2)}) collective-permute-start(bf16[256,256]{1,0:T(8,128)(2,1)S(1)} %shard_map.141), channel_id=1, source_target_pairs={{0,16},{8,24},{16,0},{24,8},{1,17},{9,25},{17,1},{25,9},{2,18},{10... | collective-permute-start | bytes 393224 | tf_op jit(solution)/shard_map/ppermute | solution.py:321
  35.8 0.0 collective-permute-done.10.other_ref
  35.8 0.0 copy-done
  35.8 1.0 %shard_map.138.first_ref = bf16[256,1024]{1,0:T(8,128)(2,1)S(1)} custom-call(f32[256,1536]{1,0:T(8,128)S(1)} %get-tuple-element.34.z_ref, bf16[256,1536]{1,0:T(8,128)(2,1)S(1)} %collective-permute-done.10.other_ref, bf16[1536,1024]{1,0:T(8,128)(2,1)S(1)} %copy-done), custom_call_target="tpu_custom_call" | custom-call | flops 805306368 | bytes 3145728 | tf_op jit(solution)/shard_map/pallas_call | solution.py:454
  36.9 0.0 collective-permute-done.9.other_ref
  36.9 0.0 slice-done.4
  36.9 0.0 slice-done.5
  36.9 2.8 %shard_map.139.a_ref = f32[64,256]{1,0:T(8,128)S(1)} custom-call(f32[256,1536]{1,0:T(8,128)S(1)} %get-tuple-element.36.z_ref, bf16[256,1536]{1,0:T(8,128)(2,1)S(1)} %collective-permute-done.9.other_ref, bf16[256,1024]{1,0:T(8,128)(2,1)S(1)} %shard_map.138.first_ref, bf16[1536,1024]{1,0:T(8,128)(2,1)S(1)} %copy-done, bf16[9,1024,256]{2,1,0:T(8,128)(2,1)S(1)} %bitcast.18, ...), custom_call_target="tpu_custom_call" | custom-call | flops 2013265920 | bytes 6291456 | tf_op jit(solution)/shard_map/pallas_call | solution.py:463
  39.7 0.1 collective-permute-start.11
  39.8 1.2 %collective-permute-done.11.b_ref = f32[64,256]{1,0:T(8,128)S(1)} collective-permute-done((f32[64,256]{1,0:T(8,128)S(1)}, f32[64,256]{1,0:T(8,128)S(1)}, u32[]{:S(2)}, u32[]{:S(2)}) %collective-permute-start.11) | collective-permute-done | bytes 65568 | tf_op jit(solution)/shard_map/ppermute | solution.py:321
  41.1 1.5 %collective-permute-done.15.refs_2_.refs_9_ = bf16[256,256]{1,0:T(8,128)(2,1)S(1)} collective-permute-done((bf16[256,256]{1,0:T(8,128)(2,1)S(1)}, bf16[256,256]{1,0:T(8,128)(2,1)S(1)}, u32[]{:S(2)}, u32[]{:S(2)}) %collective-permute-start.15) | collective-permute-done | bytes 131104 | tf_op jit(solution)/shard_map/ppermute | solution.py:321
  42.6 0.1 collective-permute-start.16
  42.7 0.5 %collective-permute-start.12 = (f32[64,256]{1,0:T(8,128)S(1)}, f32[64,256]{1,0:T(8,128)S(1)}, u32[]{:S(2)}, u32[]{:S(2)}) collective-permute-start(f32[64,256]{1,0:T(8,128)S(1)} %shard_map.140.refs_1_), channel_id=1, source_target_pairs={{0,2},{2,0},{4,6},{6,4},{1,3},{3,1},{5,7},{7,5},{8,10},{10,8},{12,... | collective-permute-start | bytes 196616 | tf_op jit(solution)/shard_map/ppermute | solution.py:321
  43.2 1.0 %collective-permute-start.13 = (f32[64,256]{1,0:T(8,128)S(1)}, f32[64,256]{1,0:T(8,128)S(1)}, u32[]{:S(2)}, u32[]{:S(2)}) collective-permute-start(f32[64,256]{1,0:T(8,128)S(1)} %shard_map.140.refs_1_), channel_id=1, source_target_pairs={{0,4},{2,6},{4,0},{6,2},{1,5},{3,7},{5,1},{7,3},{8,12},{10,14},{12... | collective-permute-start | bytes 196616 | tf_op jit(solution)/shard_map/ppermute | solution.py:321
  44.2 2.0 %collective-permute-start.14 = (f32[64,256]{1,0:T(8,128)S(1)}, f32[64,256]{1,0:T(8,128)S(1)}, u32[]{:S(2)}, u32[]{:S(2)}) collective-permute-start(f32[64,256]{1,0:T(8,128)S(1)} %shard_map.140.refs_1_), channel_id=1, source_target_pairs={{0,6},{2,4},{4,2},{6,0},{1,7},{3,5},{5,3},{7,1},{8,14},{10,12},{12... | collective-permute-start | bytes 196616 | tf_op jit(solution)/shard_map/ppermute | solution.py:321
  46.2 1.0 %collective-permute-done.12.refs_2_ = f32[64,256]{1,0:T(8,128)S(1)} collective-permute-done((f32[64,256]{1,0:T(8,128)S(1)}, f32[64,256]{1,0:T(8,128)S(1)}, u32[]{:S(2)}, u32[]{:S(2)}) %collective-permute-start.12) | collective-permute-done | bytes 65568 | tf_op jit(solution)/shard_map/ppermute | solution.py:321
  47.2 0.2 collective-permute-done.13.refs_3_
  47.5 1.9 %collective-permute-done.14.refs_4_ = f32[64,256]{1,0:T(8,128)S(1)} collective-permute-done((f32[64,256]{1,0:T(8,128)S(1)}, f32[64,256]{1,0:T(8,128)S(1)}, u32[]{:S(2)}, u32[]{:S(2)}) %collective-permute-start.14) | collective-permute-done | bytes 65568 | tf_op jit(solution)/shard_map/ppermute | solution.py:321
  49.4 0.0 collective-permute-done.16.refs_10_
  49.4 1.9 %shard_map.143 = (f32[64,256]{1,0:T(8,128)}, f32[1,64]{1,0:T(1,128)}) custom-call(s32[6]{0:T(128)S(1)} %stack.20.pos_ref.refs_0_, f32[64,256]{1,0:T(8,128)S(1)} %shard_map.140.refs_1_, f32[64,256]{1,0:T(8,128)S(1)} %collective-permute-done.12.refs_2_, f32[64,256]{1,0:T(8,128)S(1)} %collective-permute-done.13.refs_3_, ...), custom_call_target="tpu_custom_call" | custom-call | flops 100000000 | bytes 1000000 | tf_op jit(solution)/shard_map/pallas_call | solution.py:488
  (17 shorter events, 0.1 us)
Async XLA Ops:
  2.0 9.7 %collective-permute-start = (bf16[128,384]{1,0:T(8,128)(2,1)S(1)}, bf16[128,384]{1,0:T(8,128)(2,1)S(1)}, u32[]{:S(2)}, u32[]{:S(2)}) collective-permute-start(bf16[128,384]{1,0:T(8,128)(2,1)S(1)} %bitcast.26), channel_id=1, source_target_pairs={{0,2},{2,0},{4,6},{6,4},{1,3},{3,1},{5,7},{7,5},{8,10},{10,8},{12,... | collective-permute-start | bytes 294920 | tf_op jit(solution)/shard_map/ppermute | solution.py:321
  5.0 6.7 %collective-permute-start.1 = (bf16[128,384]{1,0:T(8,128)(2,1)S(1)}, bf16[128,384]{1,0:T(8,128)(2,1)S(1)}, u32[]{:S(2)}, u32[]{:S(2)}) collective-permute-start(bf16[128,384]{1,0:T(8,128)(2,1)S(1)} %bitcast.25), channel_id=1, source_target_pairs={{0,4},{2,6},{4,0},{6,2},{1,5},{3,7},{5,1},{7,3},{8,12},{10,14},{12... | collective-permute-start | bytes 294920 | tf_op jit(solution)/shard_map/ppermute | solution.py:321
  6.5 6.4 %collective-permute-start.2 = (bf16[128,384]{1,0:T(8,128)(2,1)S(1)}, bf16[128,384]{1,0:T(8,128)(2,1)S(1)}, u32[]{:S(2)}, u32[]{:S(2)}) collective-permute-start(bf16[128,384]{1,0:T(8,128)(2,1)S(1)} %bitcast.24), channel_id=1, source_target_pairs={{0,6},{2,4},{4,2},{6,0},{1,7},{3,5},{5,3},{7,1},{8,14},{10,12},{12... | collective-permute-start | bytes 294920 | tf_op jit(solution)/shard_map/ppermute | solution.py:321
  6.5 0.9 %copy-start.1 = (bf16[7,7,1536]{2,1,0:T(8,128)(2,1)S(1)}, bf16[7,7,1536]{2,1,0:T(8,128)(2,1)}, u32[]{:S(2)}) copy-start(bf16[7,7,1536]{2,1,0:T(8,128)(2,1)} %dw_ref.1) | copy-start | bytes 451588
  6.5 0.9 %copy-start.2 = (bf16[64,256]{1,0:T(8,128)(2,1)S(1)}, bf16[64,256]{1,0:T(8,128)(2,1)}, u32[]{:S(2)}) copy-start(bf16[64,256]{1,0:T(8,128)(2,1)} %key_ref.1) | copy-start | bytes 98308
  6.5 0.9 %copy-start.5 = (s32[4,4,32]{2,1,0:T(4,128)S(1)}, s32[4,4,32]{2,1,0:T(4,128)}, u32[]{:S(2)}) copy-start(s32[4,4,32]{2,1,0:T(4,128)} %ids_ref.1) | copy-start | bytes 6148
  8.0 15.9 %slice-start.2 = ((s8[4718592]{0:T(1024)(128)(4,1)}), s8[524288]{0:T(1024)(128)(4,1)S(1)}, s32[]{:S(2)}) async-start(s8[4718592]{0:T(1024)(128)(4,1)} %bitcast.15), calls=%async_computation.2 | async-start | bytes 1048576
  8.1 8.4 %collective-permute-start.3 = (bf16[160,384]{1,0:T(8,128)(2,1)S(1)}, bf16[160,384]{1,0:T(8,128)(2,1)S(1)}, u32[]{:S(2)}, u32[]{:S(2)}) collective-permute-start(bf16[160,384]{1,0:T(8,128)(2,1)S(1)} %get-tuple-element.53), channel_id=1, source_target_pairs={{0,2},{2,0},{4,6},{6,4},{1,3},{3,1},{5,7},{7,5},{8,10},{10,8},{12,... | collective-permute-start | bytes 368648 | tf_op jit(solution)/shard_map/ppermute | solution.py:321
  10.1 7.5 %collective-permute-start.4 = (bf16[160,384]{1,0:T(8,128)(2,1)S(1)}, bf16[160,384]{1,0:T(8,128)(2,1)S(1)}, u32[]{:S(2)}, u32[]{:S(2)}) collective-permute-start(bf16[160,384]{1,0:T(8,128)(2,1)S(1)} %get-tuple-element.54), channel_id=1, source_target_pairs={{0,4},{2,6},{4,0},{6,2},{1,5},{3,7},{5,1},{7,3},{8,12},{10,14},{12... | collective-permute-start | bytes 368648 | tf_op jit(solution)/shard_map/ppermute | solution.py:321
  11.6 5.9 %collective-permute-start.5 = (bf16[160,384]{1,0:T(8,128)(2,1)S(1)}, bf16[160,384]{1,0:T(8,128)(2,1)S(1)}, u32[]{:S(2)}, u32[]{:S(2)}) collective-permute-start(bf16[160,384]{1,0:T(8,128)(2,1)S(1)} %get-tuple-element.52), channel_id=1, source_target_pairs={{0,6},{2,4},{4,2},{6,0},{1,7},{3,5},{5,3},{7,1},{8,14},{10,12},{12... | collective-permute-start | bytes 368648 | tf_op jit(solution)/shard_map/ppermute | solution.py:321
  12.9 11.0 %slice-start = ((s8[4718592]{0:T(1024)(128)(4,1)}), s8[4194304]{0:T(1024)(128)(4,1)S(1)}, s32[]{:S(2)}) async-start(s8[4718592]{0:T(1024)(128)(4,1)} %bitcast.13), calls=%async_computation | async-start | bytes 8388608
  12.9 11.0 %slice-start.3 = ((s8[4718592]{0:T(1024)(128)(4,1)}), s8[4194304]{0:T(1024)(128)(4,1)S(1)}, s32[]{:S(2)}) async-start(s8[4718592]{0:T(1024)(128)(4,1)} %bitcast.15), calls=%async_computation.3 | async-start | bytes 8388608
  16.4 7.5 %collective-permute-start.7 = (f32[512,384]{1,0:T(8,128)S(1)}, f32[512,384]{1,0:T(8,128)S(1)}, u32[]{:S(2)}, u32[]{:S(2)}) collective-permute-start(f32[512,384]{1,0:T(8,128)S(1)} %get-tuple-element.24.refs_0_), channel_id=1, source_target_pairs={{0,1},{1,0},{2,3},{3,2},{4,5},{5,4},{6,7},{7,6},{8,9},{9,8},{10,11... | collective-permute-start | bytes 2359304 | tf_op jit(solution)/shard_map/ppermute | solution.py:321
  17.6 3.6 %copy-start.6 = (s32[4,64]{1,0:T(4,128)S(1)}, s32[4,64]{1,0:T(4,128)}, u32[]{:S(2)}) copy-start(s32[4,64]{1,0:T(4,128)} %refs_5_.1) | copy-start | bytes 3076
  17.6 3.6 %copy-start.7 = (s32[1,256]{1,0:T(1,128)S(1)}, s32[1,256]{1,0:T(1,128)}, u32[]{:S(2)}) copy-start(s32[1,256]{1,0:T(1,128)} %refs_4_.1) | copy-start | bytes 3076
  17.6 6.3 %slice-start.1 = ((s8[4718592]{0:T(1024)(128)(4,1)}), s8[524288]{0:T(1024)(128)(4,1)S(1)}, s32[]{:S(2)}) async-start(s8[4718592]{0:T(1024)(128)(4,1)} %bitcast.13), calls=%async_computation.1 | async-start | bytes 1048576
  17.6 6.3 %copy-start.3 = (bf16[1536]{0:T(1024)(128)(2,1)S(1)}, bf16[1536]{0:T(1024)(128)(2,1)}, u32[]{:S(2)}) copy-start(bf16[1536]{0:T(1024)(128)(2,1)} %refs_6_.3) | copy-start | bytes 9220
  17.6 6.3 %copy-start.4 = (bf16[1536]{0:T(1024)(128)(2,1)S(1)}, bf16[1536]{0:T(1024)(128)(2,1)}, u32[]{:S(2)}) copy-start(bf16[1536]{0:T(1024)(128)(2,1)} %refs_7_.3) | copy-start | bytes 9220
  21.1 2.8 %collective-permute-start.8 = (f32[512,384]{1,0:T(8,128)S(1)}, f32[512,384]{1,0:T(8,128)S(1)}, u32[]{:S(2)}, u32[]{:S(2)}) collective-permute-start(f32[512,384]{1,0:T(8,128)S(1)} %get-tuple-element.27.refs_1_), channel_id=1, source_target_pairs={{0,1},{1,0},{2,3},{3,2},{4,5},{5,4},{6,7},{7,6},{8,9},{9,8},{10,11... | collective-permute-start | bytes 2359304 | tf_op jit(solution)/shard_map/ppermute | solution.py:321
  22.2 6.3 %collective-permute-start.6 = (bf16[128,256]{1,0:T(8,128)(2,1)S(1)}, bf16[128,256]{1,0:T(8,128)(2,1)S(1)}, u32[]{:S(2)}, u32[]{:S(2)}) collective-permute-start(bf16[128,256]{1,0:T(8,128)(2,1)S(1)} %get-tuple-element.29.refs_0_.refs_7_), channel_id=1, source_target_pairs={{0,8},{8,0},{16,24},{24,16},{1,9},{9,1},{17,25},{25,17},{2,10},{10... | collective-permute-start | bytes 196616 | tf_op jit(solution)/shard_map/ppermute | solution.py:321
  28.2 7.6 %collective-permute-start.10 = (bf16[256,1536]{1,0:T(8,128)(2,1)S(1)}, bf16[256,1536]{1,0:T(8,128)(2,1)S(1)}, u32[]{:S(2)}, u32[]{:S(2)}) collective-permute-start(bf16[256,1536]{1,0:T(8,128)(2,1)S(1)} %get-tuple-element.38), channel_id=1, source_target_pairs={{0,1},{1,0},{2,3},{3,2},{4,5},{5,4},{6,7},{7,6},{8,9},{9,8},{10,11... | collective-permute-start | bytes 2359304 | tf_op jit(solution)/shard_map/ppermute | solution.py:321
  28.5 8.4 %slice-start.4 = ((s8[4718592]{0:T(1024)(128)(4,1)}), s8[4194304]{0:T(1024)(128)(4,1)S(1)}, s32[]{:S(2)}) async-start(s8[4718592]{0:T(1024)(128)(4,1)} %bitcast.17), calls=%async_computation.4 | async-start | bytes 8388608
  28.5 7.3 %copy-start = (bf16[1536,1024]{1,0:T(8,128)(2,1)S(1)}, bf16[1536,1024]{1,0:T(8,128)(2,1)}, u32[]{:S(2)}) copy-start(bf16[1536,1024]{1,0:T(8,128)(2,1)} %pe_ref.3) | copy-start | bytes 9437188
  28.5 8.4 %slice-start.5 = ((s8[4718592]{0:T(1024)(128)(4,1)}), s8[524288]{0:T(1024)(128)(4,1)S(1)}, s32[]{:S(2)}) async-start(s8[4718592]{0:T(1024)(128)(4,1)} %bitcast.17), calls=%async_computation.5 | async-start | bytes 1048576
  32.8 4.1 %collective-permute-start.9 = (bf16[256,1536]{1,0:T(8,128)(2,1)S(1)}, bf16[256,1536]{1,0:T(8,128)(2,1)S(1)}, u32[]{:S(2)}, u32[]{:S(2)}) collective-permute-start(bf16[256,1536]{1,0:T(8,128)(2,1)S(1)} %get-tuple-element.37), channel_id=1, source_target_pairs={{0,1},{1,0},{2,3},{3,2},{4,5},{5,4},{6,7},{7,6},{8,9},{9,8},{10,11... | collective-permute-start | bytes 2359304 | tf_op jit(solution)/shard_map/ppermute | solution.py:321
  33.2 9.4 %collective-permute-start.15 = (bf16[256,256]{1,0:T(8,128)(2,1)S(1)}, bf16[256,256]{1,0:T(8,128)(2,1)S(1)}, u32[]{:S(2)}, u32[]{:S(2)}) collective-permute-start(bf16[256,256]{1,0:T(8,128)(2,1)S(1)} %shard_map.141), channel_id=1, source_target_pairs={{0,16},{8,24},{16,0},{24,8},{1,17},{9,25},{17,1},{25,9},{2,18},{10... | collective-permute-start | bytes 393224 | tf_op jit(solution)/shard_map/ppermute | solution.py:321
  39.7 1.3 %collective-permute-start.11 = (f32[64,256]{1,0:T(8,128)S(1)}, f32[64,256]{1,0:T(8,128)S(1)}, u32[]{:S(2)}, u32[]{:S(2)}) collective-permute-start(f32[64,256]{1,0:T(8,128)S(1)} %shard_map.139.a_ref), channel_id=1, source_target_pairs={{0,1},{1,0},{2,3},{3,2},{4,5},{5,4},{6,7},{7,6},{8,9},{9,8},{10,11... | collective-permute-start | bytes 196616 | tf_op jit(solution)/shard_map/ppermute | solution.py:321
  42.6 6.8 %collective-permute-start.16 = (bf16[512,256]{1,0:T(8,128)(2,1)S(1)}, bf16[512,256]{1,0:T(8,128)(2,1)S(1)}, u32[]{:S(2)}, u32[]{:S(2)}) collective-permute-start(bf16[512,256]{1,0:T(8,128)(2,1)S(1)} %shard_map.142), channel_id=1, source_target_pairs={{0,1},{1,0},{2,3},{3,2},{4,5},{5,4},{6,7},{7,6},{8,9},{9,8},{10,11... | collective-permute-start | bytes 786440 | tf_op jit(solution)/shard_map/ppermute | solution.py:321
  42.7 4.6 %collective-permute-start.12 = (f32[64,256]{1,0:T(8,128)S(1)}, f32[64,256]{1,0:T(8,128)S(1)}, u32[]{:S(2)}, u32[]{:S(2)}) collective-permute-start(f32[64,256]{1,0:T(8,128)S(1)} %shard_map.140.refs_1_), channel_id=1, source_target_pairs={{0,2},{2,0},{4,6},{6,4},{1,3},{3,1},{5,7},{7,5},{8,10},{10,8},{12,... | collective-permute-start | bytes 196616 | tf_op jit(solution)/shard_map/ppermute | solution.py:321
  43.2 4.3 %collective-permute-start.13 = (f32[64,256]{1,0:T(8,128)S(1)}, f32[64,256]{1,0:T(8,128)S(1)}, u32[]{:S(2)}, u32[]{:S(2)}) collective-permute-start(f32[64,256]{1,0:T(8,128)S(1)} %shard_map.140.refs_1_), channel_id=1, source_target_pairs={{0,4},{2,6},{4,0},{6,2},{1,5},{3,7},{5,1},{7,3},{8,12},{10,14},{12... | collective-permute-start | bytes 196616 | tf_op jit(solution)/shard_map/ppermute | solution.py:321
  44.2 5.2 %collective-permute-start.14 = (f32[64,256]{1,0:T(8,128)S(1)}, f32[64,256]{1,0:T(8,128)S(1)}, u32[]{:S(2)}, u32[]{:S(2)}) collective-permute-start(f32[64,256]{1,0:T(8,128)S(1)} %shard_map.140.refs_1_), channel_id=1, source_target_pairs={{0,6},{2,4},{4,2},{6,0},{1,7},{3,5},{5,3},{7,1},{8,14},{10,12},{12... | collective-permute-start | bytes 196616 | tf_op jit(solution)/shard_map/ppermute | solution.py:321

commit v3 on v2

--- a/solution.py
+++ b/solution.py
@@ -40,6 +40,10 @@
 
 def dot_nt(a, b):
     return lax.dot_general(a, b, (((1,), (1,)), ((), ())), preferred_element_type=f32)
+
+
+def gelu(x):
+    return 0.5 * x * (1.0 + lax.erf(x * 0.7071067811865476))
 
 
 def split3(x):
@@ -83,8 +87,9 @@
     return joined[0]
 
 
-def add_kernel(a_ref, b_ref, out_ref):
+def add_kernel(a_ref, b_ref, out_ref, send_ref):
     out_ref[...] = a_ref[...] + b_ref[...]
+    send_ref[...] = out_ref[...].astype(bf16)
 
 
 def conv_kernel(geo, pos_ref, *refs):
@@ -144,7 +149,7 @@
 def block_kernel(geo, pos_ref, *refs):
     first, pixels, chunks = geo
     own, other, img = refs[:chunks], refs[chunks : 2 * chunks], refs[2 * chunks : 3 * chunks]
-    gain_ref, scale_ref, w1_ref, w2_ref, z_ref, send_ref, normed, inner = refs[3 * chunks :]
+    gain_ref, scale_ref, w1_ref, w2_ref, z_ref, normed, inner = refs[3 * chunks :]
     chans, hid = w1_ref.shape
     half = chans // 2
     width = half // chunks
@@ -164,24 +169,36 @@
             gain = jnp.where(side == 0, gains[:, start : start + width], gains[:, half + start : half + start + width])
             normed[pl.ds(side, 1), :, lanes] = (v * inv * gain).astype(bf16)[None]
     step = 256
+
+    def widen(i):
+        cols = slice(i * step, (i + 1) * step)
+        return dot(normed[0], w1_ref[0:half, cols]) + dot(normed[1], w1_ref[half:chans, cols])
+
+    ahead = widen(0)
     for i in range(hid // step):
-        cols = slice(i * step, (i + 1) * step)
-        h = dot(normed[0], w1_ref[0:half, cols]) + dot(normed[1], w1_ref[half:chans, cols])
-        inner[:, cols] = (0.5 * h * (1.0 + lax.erf(h * 0.7071067811865476))).astype(bf16)
+        h = ahead
+        if i + 1 < hid // step:
+            ahead = widen(i + 1)
+        inner[:, i * step : (i + 1) * step] = gelu(h).astype(bf16)
     step = width if width % 256 else 256
+
+    def narrow(i):
+        return dot(inner[...], w2_ref[:, i * step : (i + 1) * step])
+
+    ahead = narrow(0)
     for i in range(chans // step):
+        z = ahead
+        if i + 1 < chans // step:
+            ahead = narrow(i + 1)
         cols = slice(i * step, (i + 1) * step)
         side, start = divmod(i * step, half)
         c, start = divmod(start, width)
         keep = jnp.where(section == side, 1.0, 0.0)
-        z = dot(inner[...], w2_ref[:, cols]) * scales[:, cols]
-        z = z + img[c][rows, start : start + step].astype(f32) * keep
-        z_ref[:, cols] = z
-        send_ref[:, cols] = z.astype(bf16)
+        z_ref[:, cols] = z * scales[:, cols] + img[c][rows, start : start + step].astype(f32) * keep
 
 
 def expand_kernel(z_ref, other_ref, pe_ref, out_ref, block):
-    block[...] = (z_ref[...] + other_ref[...].astype(f32)).astype(bf16)
+    block[...] = (z_ref[...] + other_ref[...]).astype(bf16)
     step = 256
     for i in range(pe_ref.shape[1] // step):
         cols = slice(i * step, (i + 1) * step)
@@ -189,18 +206,16 @@
 
 
 def prep_kernel(geo, pos_ref, *refs):
-    shards, shard_rows, width, out_pixels, images, batches, per_key, parts = geo
+    shards, shard_rows, width, out_pixels, per_key, parts = geo
     ids = refs[:shards]
-    owner_ref, partner_ref, hot_ref, pick_ref, own_ref, keys_ref, flat = refs[shards:]
-    row, first_row, batch, first_slot = pos_ref[0], pos_ref[1], pos_ref[4], pos_ref[5]
+    hot_ref, keys_ref, flat = refs[shards:]
+    row, first_row = pos_ref[0], pos_ref[1]
     pixels = shard_rows * width
     depth = keys_ref.shape[1]
     for k in range(shards):
         mine = slice(k * per_key // 2, (k + 1) * per_key // 2)
         keys_ref[mine, :] = ids[k][pixels : pixels + per_key // 2, 0:depth]
     ids = [ref[pixels:, depth : depth + LANES].astype(f32) for ref in ids]
-    owned = own_ref.shape[0]
-    slots = images * REG
     image = row // parts
     flat[...] = jnp.full(flat.shape, -1.0, f32)
     for k in range(shards):
@@ -232,6 +247,16 @@
             line = flat[8:9, pl.ds(start, out_pixels)]
             tap = dy * 3 + dx
             hot_ref[tap * REG : (tap + 1) * REG, :] = jnp.where(region == line, 1.0, 0.0).astype(bf16)
+
+
+def owner_kernel(geo, pos_ref, *refs):
+    shards, shard_rows, pixels, images, batches, per_key = geo
+    ids = refs[:shards]
+    owner_ref, partner_ref, pick_ref, own_ref = refs[shards:]
+    row, batch, first_slot = pos_ref[0], pos_ref[4], pos_ref[5]
+    depth = ids[0].shape[1] - LANES
+    ids = [ref[pixels:, depth : depth + LANES].astype(f32) for ref in ids]
+    owned, slots = pick_ref.shape
     slot = lax.broadcasted_iota(jnp.int32, (owned, slots), 1)
     want = lax.broadcasted_iota(jnp.int32, (owned, slots), 0) + first_slot
     pick = owner_ref[...] == want
@@ -251,7 +276,11 @@
     block = mate // per_key
     within = mate % per_key
     core = (within // (per_key // 2)) ^ pos_ref[3]
-    place = (core * batches + ((block // shards) ^ batch)) * shards + ((block % shards) ^ row)
+    apart = (block // shards) ^ batch
+    turn = core
+    for n in range(batches.bit_length() - 1):
+        turn = turn * 2 + ((apart >> n) & 1)
+    place = turn * shards + ((block % shards) ^ row)
     place = place * (per_key // 2) + within % (per_key // 2)
     place = jnp.sum(jnp.where(pick, place, 0).astype(f32), axis=1, keepdims=True)
     number = jnp.sum(jnp.where(pick, count, 0.0), axis=1, keepdims=True)
@@ -263,7 +292,7 @@
     before = first_ref.shape[0]
     pixels = z_ref.shape[0]
     taps = pk_ref.shape[0]
-    block[...] = (z_ref[...] + other_ref[...].astype(f32)).astype(bf16)
+    block[...] = (z_ref[...] + other_ref[...]).astype(bf16)
     step = 256
     acc = jnp.zeros((2 * REG, out_ref.shape[1]), f32)
     for i in range(pe_ref.shape[1] // step):
@@ -281,16 +310,29 @@
     out_ref[...] = acc[0:REG] + acc[REG:]
 
 
+def keys_kernel(*refs):
+    keys_ref, length_ref = refs[-2:]
+    start = 0
+    for ref in refs[:-2]:
+        keys_ref[start : start + ref.shape[0], :] = ref[...]
+        start += ref.shape[0]
+    keys = keys_ref[...].astype(f32)
+    square = keys * keys
+    hi = square.astype(bf16)
+    lo = (square - hi.astype(f32)).astype(bf16)
+    ones = jnp.ones((16, keys.shape[1]), bf16)
+    length_ref[...] = lax.rsqrt(dot_nt(ones, hi)[0:1] + dot_nt(ones, lo)[0:1] + norm_eps)
+
+
 def loss_kernel(geo, *refs):
     shards, parts = geo
     sums, row = refs[1 : shards + 1], refs[0][0]
-    pick_ref, own_ref = refs[shards + 1 : shards + 3]
-    embed_ref, loss_ref, table = refs[-3:]
+    pick_ref, own_ref, keys_ref, length_ref, embed_ref, loss_ref, table = refs[shards + 1 :]
     if parts > 1:
         table[...] = jnp.zeros(table.shape, f32)
     for k in range(shards):
         place = pl.ds(pl.multiple_of(((row ^ k) // parts) * REG, REG), REG)
-        value = sums[k][...]
+        value = sums[k][...].astype(f32)
         table[place, :] = value if parts == 1 else table[place, :] + value
     pick = pick_ref[...]
     hi, mid, lo = split3(table[...])
@@ -298,16 +340,9 @@
     unit = ordered * lax.rsqrt(jnp.sum(ordered * ordered, axis=1, keepdims=True) + norm_eps)
     embed_ref[...] = unit
     owned = unit.shape[0]
-    keys = jnp.concatenate([ref[...] for ref in refs[shards + 3 : -3]], axis=0)
-    wide = keys.astype(f32)
-    square = wide * wide
-    square_hi = square.astype(bf16)
-    square_lo = (square - square_hi.astype(f32)).astype(bf16)
-    ones = jnp.ones((16, keys.shape[1]), bf16)
-    length = dot_nt(ones, square_hi)[0:1] + dot_nt(ones, square_lo)[0:1]
-    three = dot_nt(jnp.concatenate(split3(unit), axis=0), keys)
+    three = dot_nt(jnp.concatenate(split3(unit), axis=0), keys_ref[...])
     logits = three[0:owned] + three[owned : 2 * owned] + three[2 * owned :]
-    logits = logits * (lax.rsqrt(length + norm_eps) / sharpness_divisor)
+    logits = logits * (length_ref[...] / sharpness_divisor)
     total = jnp.log(jnp.sum(jnp.exp(logits), axis=1, keepdims=True))
     column = lax.broadcasted_iota(jnp.int32, logits.shape, 1).astype(f32)
     match = jnp.sum(jnp.where(column == own_ref[:, 0:1], logits, 0.0), axis=1, keepdims=True)
@@ -408,36 +443,29 @@
         img.append(image)
         other.append(swap(taps, "section", 1))
 
-    hot, pick, facts, keys = call(
-        functools.partial(
-            prep_kernel,
-            (shards, shard_rows, width, out_pixels, images, batches, per_key, parts),
-        ),
+    hot, keys = call(
+        functools.partial(prep_kernel, (shards, shard_rows, width, out_pixels, per_key, parts)),
         [
             jax.ShapeDtypeStruct((9 * REG, out_pixels), bf16),
-            jax.ShapeDtypeStruct((owned, slots), bf16),
-            jax.ShapeDtypeStruct((owned, LANES), f32),
             jax.ShapeDtypeStruct((shards * per_key // 2, depth), bf16),
         ],
-        [SMEM] + [VMEM] * (shards + 2),
+        [SMEM] + [VMEM] * shards,
         [pltpu.VMEM((16, (shards + 2) * pixels), f32)],
         2 * mib,
         10**8,
         10**6,
-    )(after(spot, *own), *got[-1], owner_slot, partner)
-    pieces = [keys, swap(keys, "batch", 1)]
+    )(after(spot, *own), *got[-1])
+    bits = [1 << n for n in reversed(range(batches.bit_length() - 1))]
+    pieces = [keys, swap(keys, "batch", bits[0])]
 
     hid = w1.shape[1]
     part_pixels = out_pixels // 2
     z, z_other = [], []
     for p in range(2):
         here = after(spot, pieces[-1], *z) if p else after(spot, hot)
-        mine, send = call(
+        (mine,) = call(
             functools.partial(block_kernel, (p * part_pixels, part_pixels, CHUNKS)),
-            [
-                jax.ShapeDtypeStruct((part_pixels, chans), f32),
-                jax.ShapeDtypeStruct((part_pixels, chans), bf16),
-            ],
+            [jax.ShapeDtypeStruct((part_pixels, chans), f32)],
             [SMEM] + [VMEM] * (3 * CHUNKS + 4),
             [pltpu.VMEM((2, part_pixels, half), bf16), pltpu.VMEM((part_pixels, hid), bf16)],
             8 * mib,
@@ -445,11 +473,10 @@
             4 * hid * chans,
         )(here, *own, *other, *img, ln_gain, layer_branch_scale, w1, w2)
         z.append(mine)
-        z_other.append(swap(send, "section", 1))
-    bit = 2
-    while bit < batches:
+        z_other.append(swap(mine, "section", 1))
+    for bit in bits[1:]:
         pieces.append(swap(join(*pieces), "batch", bit))
-        bit *= 2
+
     hidden = pe.shape[1]
     (hid_a,) = call(
         expand_kernel,
@@ -472,28 +499,47 @@
         2 * part_pixels * hidden * chans + 4 * 9 * REG * hidden * out_pixels,
         4 * hidden * chans,
     )(z[1], z_other[1], hid_a, pe, pk, hot)
-    (pooled,) = call(
+    pick, facts = call(
+        functools.partial(owner_kernel, (shards, shard_rows, pixels, images, batches, per_key)),
+        [jax.ShapeDtypeStruct((owned, slots), bf16), jax.ShapeDtypeStruct((owned, LANES), f32)],
+        [SMEM] + [VMEM] * (shards + 2),
+        [],
+        2 * mib,
+        10**8,
+        10**6,
+    )(after(spot, pooled), *got[-1], owner_slot, partner)
+    total, send = call(
         add_kernel,
-        [jax.ShapeDtypeStruct((REG, out_dim), f32)],
+        [jax.ShapeDtypeStruct((REG, out_dim), f32), jax.ShapeDtypeStruct((REG, out_dim), bf16)],
         [VMEM] * 2,
         [],
         mib,
         10**5,
         10**5,
     )(pooled, swap(pooled, "section", 1))
+    sums = [total] + [swap(send, "rows", k) for k in range(1, shards)]
     pieces[-1] = after(pieces[-1], pooled)
     pieces.append(swap(join(*pieces), "section", 1))
-    sums = [pooled] + [swap(pooled, "rows", k) for k in range(1, shards)]
+    count = sum(x.shape[0] for x in pieces)
+    keys, length = call(
+        keys_kernel,
+        [jax.ShapeDtypeStruct((count, depth), bf16), jax.ShapeDtypeStruct((1, count), f32)],
+        [VMEM] * len(pieces),
+        [],
+        4 * mib,
+        10**9,
+        10**6,
+    )(*pieces)
 
     embed, loss = call(
         functools.partial(loss_kernel, (shards, parts)),
         [jax.ShapeDtypeStruct((owned, out_dim), f32), jax.ShapeDtypeStruct((1, owned), f32)],
-        [SMEM] + [VMEM] * (shards + 2 + len(pieces)),
+        [SMEM] + [VMEM] * (shards + 4),
         [pltpu.VMEM((slots, out_dim), f32)],
         6 * mib,
         10**8,
         10**6,
-    )(spot, *sums, pick, facts, *pieces)
+    )(spot, *sums, pick, facts, keys, length)
     return embed, loss.reshape(owned)
 
 

time: 51.5 us -> 50.3 us (0.977)
  waiting for transfers between devices: 8.24 us -> 5.42 us
  Pallas kernels: 23 us -> 24.1 us
    ppermute x17, waiting for transfers between devices: 8.24 us -> 5.42 us  [swap(): lax.ppermute(x, axis, [(i, i ^ bit) for i in range(lax.axis_size(axis))])]
    pallas_call x1 -> x3, Pallas kernels: 0.01 us -> 1.4 us  [the longest x1 0.97 us: body(): call(functools.partial(owner_kernel, (shards, shard_rows, pixels, images,...]
  transfers between devices with their start and end apart: 17 -> 17, of which waited for: 7 -> 6; matrix products, arithmetic and copies ran while one was open for 0% -> 0% of each run, Pallas kernels for 41% -> 44%
where the time goes in v3:
time: 50.3 us; the launch traced here: 50.1 us
  Pallas kernels  24.1 us (48%)
  starting transfers between devices  17.3 us (34%)
  waiting for transfers between devices  5.42 us (11%)
  local copies, waits for them, and re-layouts  2.28 us (5%)
  between operations  0.93 us (2%)
    ppermute x17, starting transfers between devices, swap(): lax.ppermute(x, axis, [(i, i ^ bit) for i in range(lax.axis_size(axis))])  17.3 us
    pallas_call x2, Pallas kernels, body(): call(functools.partial(block_kernel, (p * part_pixels, part_pixels, CHUNK...  8.54 us
    pallas_call x2, Pallas kernels, body(): call(functools.partial(conv_kernel, (shards, shard_rows, width, out_rows,...  6.96 us
    ppermute x17, waiting for transfers between devices, swap(): lax.ppermute(x, axis, [(i, i ^ bit) for i in range(lax.axis_size(axis))])  5.42 us
    pallas_call x1, Pallas kernels, body(): call(project_kernel, [jax.ShapeDtypeStruct((REG, out_dim), f32)], [VMEM]...  2.87 us
    pallas_call x1, Pallas kernels, body(): call(functools.partial(loss_kernel, (shards, parts)), [jax.ShapeDtypeStru...  1.91 us
    dynamic_slice x1, local copies, waits for them, and re-layouts, body(): lax.dynamic_slice(features, place, (1, shard_rows, width, span))  1.32 us
  transfers between devices with their start and end apart: 17, of which 6 were waited for; matrix products, arithmetic and copies ran while one was open for 0% of the time, Pallas kernels for 44%

profile of v3, /device:TPU:0, one launch (start us, length us, event | category | flops | bytes accessed | tf_op | source)
XLA Modules:
  0.0 50.1 jit_solution(6230888267751724423)
XLA Ops:
  0.7 1.3 %constant_dynamic-slice_fusion = (bf16[1,4,32,384]{3,2,1,0:T(8,128)(2,1)S(1)}, bf16[1,4,32,384]{3,2,1,0:T(8,128)(2,1)S(1)}, bf16[1,4,32,384]{3,2,1,0:T(8,128)(2,...) fusion(bf16[4,4,32,1536]{3,2,1,0:T(8,128)(2,1)} %param.12, ...), kind=kLoop, calls=%fused_computation.4 | loop fusion | bytes 1572888 | tf_op jit(solution)/shard_map/dynamic_slice | solution.py:418
  2.0 3.0 %collective-permute-start = (bf16[128,384]{1,0:T(8,128)(2,1)S(1)}, bf16[128,384]{1,0:T(8,128)(2,1)S(1)}, u32[]{:S(2)}, u32[]{:S(2)}) collective-permute-start(bf16[128,384]{1,0:T(8,128)(2,1)S(1)} %bitcast.26), channel_id=1, source_target_pairs={{0,2},{2,0},{4,6},{6,4},{1,3},{3,1},{5,7},{7,5},{8,10},{10,8},{12,... | collective-permute-start | bytes 294920 | tf_op jit(solution)/shard_map/ppermute | solution.py:356
  5.0 1.5 %collective-permute-start.1 = (bf16[128,384]{1,0:T(8,128)(2,1)S(1)}, bf16[128,384]{1,0:T(8,128)(2,1)S(1)}, u32[]{:S(2)}, u32[]{:S(2)}) collective-permute-start(bf16[128,384]{1,0:T(8,128)(2,1)S(1)} %bitcast.25), channel_id=1, source_target_pairs={{0,4},{2,6},{4,0},{6,2},{1,5},{3,7},{5,1},{7,3},{8,12},{10,14},{12... | collective-permute-start | bytes 294920 | tf_op jit(solution)/shard_map/ppermute | solution.py:356
  6.5 0.0 collective-permute-start.2
  6.5 0.1 stack.20.pos_ref.refs_0_
  6.6 0.8 %copy-done.1 = bf16[7,7,1536]{2,1,0:T(8,128)(2,1)S(1)} copy-done((bf16[7,7,1536]{2,1,0:T(8,128)(2,1)S(1)}, bf16[7,7,1536]{2,1,0:T(8,128)(2,1)}, u32[]{:S(2)}) %copy-start.1) | copy-done | bytes 150552
  7.4 0.0 copy-done.2
  7.4 0.0 copy-done.5
  7.4 0.6 %shard_map.132 = (bf16[32,384]{1,0:T(8,128)(2,1)S(1)}, f32[49,768]{1,0:T(8,128)S(1)}) custom-call(s32[6]{0:T(128)S(1)} %stack.20.pos_ref.refs_0_, s32[4,4,32]{2,1,0:T(4,128)S(1)} %copy-done.5, bf16[64,256]{1,0:T(8,128)(2,1)S(1)} %copy-done.2, bf16[7,7,1536]{2,1,0:T(8,128)(2,1)S(1)} %copy-done.1, f32[32,128]{1,0:T(8,128)S(1)} %shard_map.131.blank_ref), custom_call_target="tpu_custom_call" | custom-call | bytes 1000000 | tf_op jit(solution)/shard_map/pallas_call | solution.py:404
  8.0 0.0 slice-start.2
  8.0 0.1 pad_maximum_fusion
  8.1 2.0 %collective-permute-start.3 = (bf16[160,384]{1,0:T(8,128)(2,1)S(1)}, bf16[160,384]{1,0:T(8,128)(2,1)S(1)}, u32[]{:S(2)}, u32[]{:S(2)}) collective-permute-start(bf16[160,384]{1,0:T(8,128)(2,1)S(1)} %get-tuple-element.55), channel_id=1, source_target_pairs={{0,2},{2,0},{4,6},{6,4},{1,3},{3,1},{5,7},{7,5},{8,10},{10,8},{12,... | collective-permute-start | bytes 368648 | tf_op jit(solution)/shard_map/ppermute | solution.py:356
  10.1 1.5 %collective-permute-start.4 = (bf16[160,384]{1,0:T(8,128)(2,1)S(1)}, bf16[160,384]{1,0:T(8,128)(2,1)S(1)}, u32[]{:S(2)}, u32[]{:S(2)}) collective-permute-start(bf16[160,384]{1,0:T(8,128)(2,1)S(1)} %get-tuple-element.56), channel_id=1, source_target_pairs={{0,4},{2,6},{4,0},{6,2},{1,5},{3,7},{5,1},{7,3},{8,12},{10,14},{12... | collective-permute-start | bytes 368648 | tf_op jit(solution)/shard_map/ppermute | solution.py:356
  11.6 0.0 collective-permute-done.refs_1_
  11.6 0.0 collective-permute-start.5
  11.6 0.0 collective-permute-done.1.refs_2_
  11.7 1.2 %collective-permute-done.2.refs_3_ = bf16[128,384]{1,0:T(8,128)(2,1)S(1)} collective-permute-done((bf16[128,384]{1,0:T(8,128)(2,1)S(1)}, bf16[128,384]{1,0:T(8,128)(2,1)S(1)}, u32[]{:S(2)}, u32[]{:S(2)}) %collective-permute-start.2) | collective-permute-done | bytes 98336 | tf_op jit(solution)/shard_map/ppermute | solution.py:356
  12.9 3.5 %shard_map.133 = (f32[512,384]{1,0:T(8,128)S(1)}, bf16[512,384]{1,0:T(8,128)(2,1)S(1)}) custom-call(s32[6]{0:T(128)S(1)} %stack.20.pos_ref.refs_0_, bf16[128,384]{1,0:T(8,128)(2,1)S(1)} %bitcast.19, bf16[128,384]{1,0:T(8,128)(2,1)S(1)} %collective-permute-done.refs_1_, bf16[128,384]{1,0:T(8,128)(2,1)S(1)} %collective-permute-done.1.refs_2_, ...), custom_call_target="tpu_custom_call" | custom-call | flops 1926758400 | bytes 1966080 | tf_op jit(solution)/shard_map/pallas_call | solution.py:427
  16.4 0.1 collective-permute-start.7
  16.4 0.0 collective-permute-done.3.refs_1_
  16.5 1.1 %collective-permute-done.4.refs_2_ = bf16[160,384]{1,0:T(8,128)(2,1)S(1)} collective-permute-done((bf16[160,384]{1,0:T(8,128)(2,1)S(1)}, bf16[160,384]{1,0:T(8,128)(2,1)S(1)}, u32[]{:S(2)}, u32[]{:S(2)}) %collective-permute-start.4) | collective-permute-done | bytes 122912 | tf_op jit(solution)/shard_map/ppermute | solution.py:356
  17.6 0.0 collective-permute-done.5.refs_3_
  17.6 3.5 %shard_map.134 = (f32[512,384]{1,0:T(8,128)S(1)}, bf16[512,384]{1,0:T(8,128)(2,1)S(1)}) custom-call(s32[6]{0:T(128)S(1)} %stack.20.pos_ref.refs_0_, bf16[160,384]{1,0:T(8,128)(2,1)S(1)} %get-tuple-element.57.refs_0_, bf16[160,384]{1,0:T(8,128)(2,1)S(1)} %collective-permute-done.3.refs_1_, bf16[160,384]{1,0:T(8,128)(2,1)S(1)} %collective-permute-done.4.refs_2_, ...), custom_call_target="tpu_custom_call" | custom-call | flops 1926758400 | bytes 1966080 | tf_op jit(solution)/shard_map/pallas_call | solution.py:427
  21.1 0.1 collective-permute-start.8
  21.1 0.9 %shard_map.135 = (bf16[576,512]{1,0:T(8,128)(2,1)S(1)}, bf16[128,256]{1,0:T(8,128)(2,1)S(1)}) custom-call(s32[6]{0:T(128)S(1)} %stack.20.pos_ref.refs_0_, bf16[160,384]{1,0:T(8,128)(2,1)S(1)} %get-tuple-element.57.refs_0_, bf16[160,384]{1,0:T(8,128)(2,1)S(1)} %collective-permute-done.3.refs_1_, bf16[160,384]{1,0:T(8,128)(2,1)S(1)} %collective-permute-done.4.refs_2_, ...), custom_call_target="tpu_custom_call" | custom-call | flops 100000000 | bytes 1000000 | tf_op jit(solution)/shard_map/pallas_call | solution.py:446
  22.0 2.7 %collective-permute-start.6 = (bf16[128,256]{1,0:T(8,128)(2,1)S(1)}, bf16[128,256]{1,0:T(8,128)(2,1)S(1)}, u32[]{:S(2)}, u32[]{:S(2)}) collective-permute-start(bf16[128,256]{1,0:T(8,128)(2,1)S(1)} %get-tuple-element.30.refs_0_), channel_id=1, source_target_pairs={{0,16},{8,24},{16,0},{24,8},{1,17},{9,25},{17,1},{25,9},{2,18},{10... | collective-permute-start | bytes 196616 | tf_op jit(solution)/shard_map/ppermute | solution.py:356
  24.7 0.0 collective-permute-done.7.refs_2_
  24.7 0.0 collective-permute-done.8.refs_3_
  24.7 0.0 slice-done.2
  24.7 0.0 slice-done
  24.7 0.0 slice-done.3
  24.7 0.0 slice-done.1
  24.7 0.0 copy-done.3
  24.7 0.0 slice-start.4
  24.8 4.3 %shard_map.136.z_ref = f32[256,1536]{1,0:T(8,128)S(1)} custom-call(s32[6]{0:T(128)S(1)} %stack.20.pos_ref.refs_0_, f32[512,384]{1,0:T(8,128)S(1)} %get-tuple-element.25.refs_0_, f32[512,384]{1,0:T(8,128)S(1)} %get-tuple-element.28.refs_1_, f32[512,384]{1,0:T(8,128)S(1)} %collective-permute-done.7.refs_2_, f32[512,384]{1,0:T(8,128)S(1)} %collective-permute-done.8.refs_3_, ...), custom_call_target="tpu_custom_call" | custom-call | flops 2415919104 | bytes 9437184 | tf_op jit(solution)/shard_map/pallas_call | solution.py:466
  29.0 0.0 slice-start.5
  29.0 0.3 collective-permute-start.10
  29.3 0.0 collective-permute-done.6.refs_1_
  29.3 4.3 %shard_map.137.z_ref = f32[256,1536]{1,0:T(8,128)S(1)} custom-call(s32[6]{0:T(128)S(1)} %stack.20.pos_ref.refs_0_, f32[512,384]{1,0:T(8,128)S(1)} %get-tuple-element.25.refs_0_, f32[512,384]{1,0:T(8,128)S(1)} %get-tuple-element.28.refs_1_, f32[512,384]{1,0:T(8,128)S(1)} %collective-permute-done.7.refs_2_, f32[512,384]{1,0:T(8,128)S(1)} %collective-permute-done.8.refs_3_, ...), custom_call_target="tpu_custom_call" | custom-call | flops 2415919104 | bytes 9437184 | tf_op jit(solution)/shard_map/pallas_call | solution.py:466
  33.6 0.4 collective-permute-start.9
  34.0 1.6 %collective-permute-start.15 = (bf16[256,256]{1,0:T(8,128)(2,1)S(1)}, bf16[256,256]{1,0:T(8,128)(2,1)S(1)}, u32[]{:S(2)}, u32[]{:S(2)}) collective-permute-start(bf16[256,256]{1,0:T(8,128)(2,1)S(1)} %shard_map.142), channel_id=1, source_target_pairs={{0,8},{8,0},{16,24},{24,16},{1,9},{9,1},{17,25},{25,17},{2,10},{10... | collective-permute-start | bytes 393224 | tf_op jit(solution)/shard_map/ppermute | solution.py:356
  35.6 0.0 collective-permute-done.10.other_ref
  35.6 0.0 copy-done
  35.6 1.0 %shard_map.138.first_ref = bf16[256,1024]{1,0:T(8,128)(2,1)S(1)} custom-call(f32[256,1536]{1,0:T(8,128)S(1)} %shard_map.136.z_ref, f32[256,1536]{1,0:T(8,128)S(1)} %collective-permute-done.10.other_ref, bf16[1536,1024]{1,0:T(8,128)(2,1)S(1)} %copy-done), custom_call_target="tpu_custom_call" | custom-call | flops 805306368 | bytes 3145728 | tf_op jit(solution)/shard_map/pallas_call | solution.py:481
  36.6 0.0 copy-start.6
  36.6 0.0 copy-start.7
  36.6 0.4 collective-permute-done.9.other_ref
  37.1 0.0 slice-done.5
  37.1 2.9 %shard_map.139.a_ref = f32[64,256]{1,0:T(8,128)S(1)} custom-call(f32[256,1536]{1,0:T(8,128)S(1)} %shard_map.137.z_ref, f32[256,1536]{1,0:T(8,128)S(1)} %collective-permute-done.9.other_ref, bf16[256,1024]{1,0:T(8,128)(2,1)S(1)} %shard_map.138.first_ref, bf16[1536,1024]{1,0:T(8,128)(2,1)S(1)} %copy-done, bf16[9,1024,256]{2,1,0:T(8,128)(2,1)S(1)} %bitcast.18, ...), custom_call_target="tpu_custom_call" | custom-call | flops 2013265920 | bytes 6291456 | tf_op jit(solution)/shard_map/pallas_call | solution.py:490
  40.0 0.0 collective-permute-done.15.refs_2_
  40.0 0.4 collective-permute-start.16
  40.4 0.2 collective-permute-start.11
  40.6 0.0 copy-done.7
  40.6 1.0 %shard_map.141 = (bf16[64,256]{1,0:T(8,128)(2,1)S(1)}, f32[64,128]{1,0:T(8,128)S(1)}) custom-call(s32[6]{0:T(128)S(1)} %stack.20.pos_ref.refs_0_, bf16[160,384]{1,0:T(8,128)(2,1)S(1)} %get-tuple-element.57.refs_0_, bf16[160,384]{1,0:T(8,128)(2,1)S(1)} %collective-permute-done.3.refs_1_, bf16[160,384]{1,0:T(8,128)(2,1)S(1)} %collective-permute-done.4.refs_2_, ...), custom_call_target="tpu_custom_call" | custom-call | flops 100000000 | bytes 1000000 | tf_op jit(solution)/shard_map/pallas_call | solution.py:502
  41.6 0.1 collective-permute-done.11.b_ref
  41.7 0.5 %collective-permute-start.12 = (bf16[64,256]{1,0:T(8,128)(2,1)S(1)}, bf16[64,256]{1,0:T(8,128)(2,1)S(1)}, u32[]{:S(2)}, u32[]{:S(2)}) collective-permute-start(bf16[64,256]{1,0:T(8,128)(2,1)S(1)} %get-tuple-element.37), channel_id=1, source_target_pairs={{0,2},{2,0},{4,6},{6,4},{1,3},{3,1},{5,7},{7,5},{8,10},{10,8},{12,... | collective-permute-start | bytes 98312 | tf_op jit(solution)/shard_map/ppermute | solution.py:356
  42.2 1.1 %collective-permute-start.13 = (bf16[64,256]{1,0:T(8,128)(2,1)S(1)}, bf16[64,256]{1,0:T(8,128)(2,1)S(1)}, u32[]{:S(2)}, u32[]{:S(2)}) collective-permute-start(bf16[64,256]{1,0:T(8,128)(2,1)S(1)} %get-tuple-element.37), channel_id=1, source_target_pairs={{0,4},{2,6},{4,0},{6,2},{1,5},{3,7},{5,1},{7,3},{8,12},{10,14},{12... | collective-permute-start | bytes 98312 | tf_op jit(solution)/shard_map/ppermute | solution.py:356
  43.4 1.9 %collective-permute-start.14 = (bf16[64,256]{1,0:T(8,128)(2,1)S(1)}, bf16[64,256]{1,0:T(8,128)(2,1)S(1)}, u32[]{:S(2)}, u32[]{:S(2)}) collective-permute-start(bf16[64,256]{1,0:T(8,128)(2,1)S(1)} %get-tuple-element.37), channel_id=1, source_target_pairs={{0,6},{2,4},{4,2},{6,0},{1,7},{3,5},{5,3},{7,1},{8,14},{10,12},{12... | collective-permute-start | bytes 98312 | tf_op jit(solution)/shard_map/ppermute | solution.py:356
  45.3 0.0 collective-permute-done.16.refs_3_
  45.3 0.4 shard_map.144
  45.7 0.0 collective-permute-done.12.refs_2_
  45.7 0.5 collective-permute-done.13.refs_3_
  46.2 2.0 %collective-permute-done.14.refs_4_ = bf16[64,256]{1,0:T(8,128)(2,1)S(1)} collective-permute-done((bf16[64,256]{1,0:T(8,128)(2,1)S(1)}, bf16[64,256]{1,0:T(8,128)(2,1)S(1)}, u32[]{:S(2)}, u32[]{:S(2)}) %collective-permute-start.14) | collective-permute-done | bytes 32800 | tf_op jit(solution)/shard_map/ppermute | solution.py:356
  48.2 1.9 %shard_map.145 = (f32[64,256]{1,0:T(8,128)}, f32[1,64]{1,0:T(1,128)}) custom-call(s32[6]{0:T(128)S(1)} %stack.20.pos_ref.refs_0_, f32[64,256]{1,0:T(8,128)S(1)} %get-tuple-element.36.refs_1_, bf16[64,256]{1,0:T(8,128)(2,1)S(1)} %collective-permute-done.12.refs_2_, bf16[64,256]{1,0:T(8,128)(2,1)S(1)} %collective-permute-done.13.refs_3_, ...), custom_call_target="tpu_custom_call" | custom-call | flops 100000000 | bytes 1000000 | tf_op jit(solution)/shard_map/pallas_call | solution.py:534
  (19 shorter events, 0.1 us)
Async XLA Ops:
  2.0 9.7 %collective-permute-start = (bf16[128,384]{1,0:T(8,128)(2,1)S(1)}, bf16[128,384]{1,0:T(8,128)(2,1)S(1)}, u32[]{:S(2)}, u32[]{:S(2)}) collective-permute-start(bf16[128,384]{1,0:T(8,128)(2,1)S(1)} %bitcast.26), channel_id=1, source_target_pairs={{0,2},{2,0},{4,6},{6,4},{1,3},{3,1},{5,7},{7,5},{8,10},{10,8},{12,... | collective-permute-start | bytes 294920 | tf_op jit(solution)/shard_map/ppermute | solution.py:356
  5.0 6.7 %collective-permute-start.1 = (bf16[128,384]{1,0:T(8,128)(2,1)S(1)}, bf16[128,384]{1,0:T(8,128)(2,1)S(1)}, u32[]{:S(2)}, u32[]{:S(2)}) collective-permute-start(bf16[128,384]{1,0:T(8,128)(2,1)S(1)} %bitcast.25), channel_id=1, source_target_pairs={{0,4},{2,6},{4,0},{6,2},{1,5},{3,7},{5,1},{7,3},{8,12},{10,14},{12... | collective-permute-start | bytes 294920 | tf_op jit(solution)/shard_map/ppermute | solution.py:356
  6.5 6.4 %collective-permute-start.2 = (bf16[128,384]{1,0:T(8,128)(2,1)S(1)}, bf16[128,384]{1,0:T(8,128)(2,1)S(1)}, u32[]{:S(2)}, u32[]{:S(2)}) collective-permute-start(bf16[128,384]{1,0:T(8,128)(2,1)S(1)} %bitcast.24), channel_id=1, source_target_pairs={{0,6},{2,4},{4,2},{6,0},{1,7},{3,5},{5,3},{7,1},{8,14},{10,12},{12... | collective-permute-start | bytes 294920 | tf_op jit(solution)/shard_map/ppermute | solution.py:356
  6.5 0.9 %copy-start.1 = (bf16[7,7,1536]{2,1,0:T(8,128)(2,1)S(1)}, bf16[7,7,1536]{2,1,0:T(8,128)(2,1)}, u32[]{:S(2)}) copy-start(bf16[7,7,1536]{2,1,0:T(8,128)(2,1)} %dw_ref.1) | copy-start | bytes 451588
  6.5 0.9 %copy-start.2 = (bf16[64,256]{1,0:T(8,128)(2,1)S(1)}, bf16[64,256]{1,0:T(8,128)(2,1)}, u32[]{:S(2)}) copy-start(bf16[64,256]{1,0:T(8,128)(2,1)} %key_ref.1) | copy-start | bytes 98308
  6.5 0.9 %copy-start.5 = (s32[4,4,32]{2,1,0:T(4,128)S(1)}, s32[4,4,32]{2,1,0:T(4,128)}, u32[]{:S(2)}) copy-start(s32[4,4,32]{2,1,0:T(4,128)} %ids_ref.1) | copy-start | bytes 6148
  8.0 16.7 %slice-start.2 = ((s8[4718592]{0:T(1024)(128)(4,1)}), s8[524288]{0:T(1024)(128)(4,1)S(1)}, s32[]{:S(2)}) async-start(s8[4718592]{0:T(1024)(128)(4,1)} %bitcast.15), calls=%async_computation.2 | async-start | bytes 1048576
  8.1 8.4 %collective-permute-start.3 = (bf16[160,384]{1,0:T(8,128)(2,1)S(1)}, bf16[160,384]{1,0:T(8,128)(2,1)S(1)}, u32[]{:S(2)}, u32[]{:S(2)}) collective-permute-start(bf16[160,384]{1,0:T(8,128)(2,1)S(1)} %get-tuple-element.55), channel_id=1, source_target_pairs={{0,2},{2,0},{4,6},{6,4},{1,3},{3,1},{5,7},{7,5},{8,10},{10,8},{12,... | collective-permute-start | bytes 368648 | tf_op jit(solution)/shard_map/ppermute | solution.py:356
  10.1 7.5 %collective-permute-start.4 = (bf16[160,384]{1,0:T(8,128)(2,1)S(1)}, bf16[160,384]{1,0:T(8,128)(2,1)S(1)}, u32[]{:S(2)}, u32[]{:S(2)}) collective-permute-start(bf16[160,384]{1,0:T(8,128)(2,1)S(1)} %get-tuple-element.56), channel_id=1, source_target_pairs={{0,4},{2,6},{4,0},{6,2},{1,5},{3,7},{5,1},{7,3},{8,12},{10,14},{12... | collective-permute-start | bytes 368648 | tf_op jit(solution)/shard_map/ppermute | solution.py:356
  11.6 5.9 %collective-permute-start.5 = (bf16[160,384]{1,0:T(8,128)(2,1)S(1)}, bf16[160,384]{1,0:T(8,128)(2,1)S(1)}, u32[]{:S(2)}, u32[]{:S(2)}) collective-permute-start(bf16[160,384]{1,0:T(8,128)(2,1)S(1)} %get-tuple-element.54), channel_id=1, source_target_pairs={{0,6},{2,4},{4,2},{6,0},{1,7},{3,5},{5,3},{7,1},{8,14},{10,12},{12... | collective-permute-start | bytes 368648 | tf_op jit(solution)/shard_map/ppermute | solution.py:356
  12.9 11.8 %slice-start = ((s8[4718592]{0:T(1024)(128)(4,1)}), s8[4194304]{0:T(1024)(128)(4,1)S(1)}, s32[]{:S(2)}) async-start(s8[4718592]{0:T(1024)(128)(4,1)} %bitcast.13), calls=%async_computation | async-start | bytes 8388608
  12.9 11.8 %slice-start.3 = ((s8[4718592]{0:T(1024)(128)(4,1)}), s8[4194304]{0:T(1024)(128)(4,1)S(1)}, s32[]{:S(2)}) async-start(s8[4718592]{0:T(1024)(128)(4,1)} %bitcast.15), calls=%async_computation.3 | async-start | bytes 8388608
  16.4 8.3 %collective-permute-start.7 = (f32[512,384]{1,0:T(8,128)S(1)}, f32[512,384]{1,0:T(8,128)S(1)}, u32[]{:S(2)}, u32[]{:S(2)}) collective-permute-start(f32[512,384]{1,0:T(8,128)S(1)} %get-tuple-element.25.refs_0_), channel_id=1, source_target_pairs={{0,1},{1,0},{2,3},{3,2},{4,5},{5,4},{6,7},{7,6},{8,9},{9,8},{10,11... | collective-permute-start | bytes 2359304 | tf_op jit(solution)/shard_map/ppermute | solution.py:356
  17.6 7.1 %slice-start.1 = ((s8[4718592]{0:T(1024)(128)(4,1)}), s8[524288]{0:T(1024)(128)(4,1)S(1)}, s32[]{:S(2)}) async-start(s8[4718592]{0:T(1024)(128)(4,1)} %bitcast.13), calls=%async_computation.1 | async-start | bytes 1048576
  17.6 7.1 %copy-start.3 = (bf16[1536]{0:T(1024)(128)(2,1)S(1)}, bf16[1536]{0:T(1024)(128)(2,1)}, u32[]{:S(2)}) copy-start(bf16[1536]{0:T(1024)(128)(2,1)} %refs_6_.3) | copy-start | bytes 9220
  17.6 7.1 %copy-start.4 = (bf16[1536]{0:T(1024)(128)(2,1)S(1)}, bf16[1536]{0:T(1024)(128)(2,1)}, u32[]{:S(2)}) copy-start(bf16[1536]{0:T(1024)(128)(2,1)} %refs_7_.3) | copy-start | bytes 9220
  21.1 3.6 %collective-permute-start.8 = (f32[512,384]{1,0:T(8,128)S(1)}, f32[512,384]{1,0:T(8,128)S(1)}, u32[]{:S(2)}, u32[]{:S(2)}) collective-permute-start(f32[512,384]{1,0:T(8,128)S(1)} %get-tuple-element.28.refs_1_), channel_id=1, source_target_pairs={{0,1},{1,0},{2,3},{3,2},{4,5},{5,4},{6,7},{7,6},{8,9},{9,8},{10,11... | collective-permute-start | bytes 2359304 | tf_op jit(solution)/shard_map/ppermute | solution.py:356
  22.0 7.3 %collective-permute-start.6 = (bf16[128,256]{1,0:T(8,128)(2,1)S(1)}, bf16[128,256]{1,0:T(8,128)(2,1)S(1)}, u32[]{:S(2)}, u32[]{:S(2)}) collective-permute-start(bf16[128,256]{1,0:T(8,128)(2,1)S(1)} %get-tuple-element.30.refs_0_), channel_id=1, source_target_pairs={{0,16},{8,24},{16,0},{24,8},{1,17},{9,25},{17,1},{25,9},{2,18},{10... | collective-permute-start | bytes 196616 | tf_op jit(solution)/shard_map/ppermute | solution.py:356
  24.7 12.3 %slice-start.4 = ((s8[4718592]{0:T(1024)(128)(4,1)}), s8[4194304]{0:T(1024)(128)(4,1)S(1)}, s32[]{:S(2)}) async-start(s8[4718592]{0:T(1024)(128)(4,1)} %bitcast.17), calls=%async_computation.4 | async-start | bytes 8388608
  29.0 8.1 %slice-start.5 = ((s8[4718592]{0:T(1024)(128)(4,1)}), s8[524288]{0:T(1024)(128)(4,1)S(1)}, s32[]{:S(2)}) async-start(s8[4718592]{0:T(1024)(128)(4,1)} %bitcast.17), calls=%async_computation.5 | async-start | bytes 1048576
  29.0 6.6 %collective-permute-start.10 = (f32[256,1536]{1,0:T(8,128)S(1)}, f32[256,1536]{1,0:T(8,128)S(1)}, u32[]{:S(2)}, u32[]{:S(2)}) collective-permute-start(f32[256,1536]{1,0:T(8,128)S(1)} %shard_map.136.z_ref), channel_id=1, source_target_pairs={{0,1},{1,0},{2,3},{3,2},{4,5},{5,4},{6,7},{7,6},{8,9},{9,8},{10,11... | collective-permute-start | bytes 4718600 | tf_op jit(solution)/shard_map/ppermute | solution.py:356
  29.3 6.3 %copy-start = (bf16[1536,1024]{1,0:T(8,128)(2,1)S(1)}, bf16[1536,1024]{1,0:T(8,128)(2,1)}, u32[]{:S(2)}) copy-start(bf16[1536,1024]{1,0:T(8,128)(2,1)} %pe_ref.3) | copy-start | bytes 9437188
  33.6 3.5 %collective-permute-start.9 = (f32[256,1536]{1,0:T(8,128)S(1)}, f32[256,1536]{1,0:T(8,128)S(1)}, u32[]{:S(2)}, u32[]{:S(2)}) collective-permute-start(f32[256,1536]{1,0:T(8,128)S(1)} %shard_map.137.z_ref), channel_id=1, source_target_pairs={{0,1},{1,0},{2,3},{3,2},{4,5},{5,4},{6,7},{7,6},{8,9},{9,8},{10,11... | collective-permute-start | bytes 4718600 | tf_op jit(solution)/shard_map/ppermute | solution.py:356
  34.0 6.0 %collective-permute-start.15 = (bf16[256,256]{1,0:T(8,128)(2,1)S(1)}, bf16[256,256]{1,0:T(8,128)(2,1)S(1)}, u32[]{:S(2)}, u32[]{:S(2)}) collective-permute-start(bf16[256,256]{1,0:T(8,128)(2,1)S(1)} %shard_map.142), channel_id=1, source_target_pairs={{0,8},{8,0},{16,24},{24,16},{1,9},{9,1},{17,25},{25,17},{2,10},{10... | collective-permute-start | bytes 393224 | tf_op jit(solution)/shard_map/ppermute | solution.py:356
  36.6 4.0 %copy-start.6 = (s32[4,64]{1,0:T(4,128)S(1)}, s32[4,64]{1,0:T(4,128)}, u32[]{:S(2)}) copy-start(s32[4,64]{1,0:T(4,128)} %refs_5_.1) | copy-start | bytes 3076
  36.6 4.0 %copy-start.7 = (s32[1,256]{1,0:T(1,128)S(1)}, s32[1,256]{1,0:T(1,128)}, u32[]{:S(2)}) copy-start(s32[1,256]{1,0:T(1,128)} %refs_4_.1) | copy-start | bytes 3076
  40.0 5.3 %collective-permute-start.16 = (bf16[512,256]{1,0:T(8,128)(2,1)S(1)}, bf16[512,256]{1,0:T(8,128)(2,1)S(1)}, u32[]{:S(2)}, u32[]{:S(2)}) collective-permute-start(bf16[512,256]{1,0:T(8,128)(2,1)S(1)} %shard_map.143), channel_id=1, source_target_pairs={{0,1},{1,0},{2,3},{3,2},{4,5},{5,4},{6,7},{7,6},{8,9},{9,8},{10,11... | collective-permute-start | bytes 786440 | tf_op jit(solution)/shard_map/ppermute | solution.py:356
  40.4 1.3 %collective-permute-start.11 = (f32[64,256]{1,0:T(8,128)S(1)}, f32[64,256]{1,0:T(8,128)S(1)}, u32[]{:S(2)}, u32[]{:S(2)}) collective-permute-start(f32[64,256]{1,0:T(8,128)S(1)} %shard_map.139.a_ref), channel_id=1, source_target_pairs={{0,1},{1,0},{2,3},{3,2},{4,5},{5,4},{6,7},{7,6},{8,9},{9,8},{10,11... | collective-permute-start | bytes 196616 | tf_op jit(solution)/shard_map/ppermute | solution.py:356
  41.7 4.0 %collective-permute-start.12 = (bf16[64,256]{1,0:T(8,128)(2,1)S(1)}, bf16[64,256]{1,0:T(8,128)(2,1)S(1)}, u32[]{:S(2)}, u32[]{:S(2)}) collective-permute-start(bf16[64,256]{1,0:T(8,128)(2,1)S(1)} %get-tuple-element.37), channel_id=1, source_target_pairs={{0,2},{2,0},{4,6},{6,4},{1,3},{3,1},{5,7},{7,5},{8,10},{10,8},{12,... | collective-permute-start | bytes 98312 | tf_op jit(solution)/shard_map/ppermute | solution.py:356
  42.2 3.9 %collective-permute-start.13 = (bf16[64,256]{1,0:T(8,128)(2,1)S(1)}, bf16[64,256]{1,0:T(8,128)(2,1)S(1)}, u32[]{:S(2)}, u32[]{:S(2)}) collective-permute-start(bf16[64,256]{1,0:T(8,128)(2,1)S(1)} %get-tuple-element.37), channel_id=1, source_target_pairs={{0,4},{2,6},{4,0},{6,2},{1,5},{3,7},{5,1},{7,3},{8,12},{10,14},{12... | collective-permute-start | bytes 98312 | tf_op jit(solution)/shard_map/ppermute | solution.py:356
  43.4 4.8 %collective-permute-start.14 = (bf16[64,256]{1,0:T(8,128)(2,1)S(1)}, bf16[64,256]{1,0:T(8,128)(2,1)S(1)}, u32[]{:S(2)}, u32[]{:S(2)}) collective-permute-start(bf16[64,256]{1,0:T(8,128)(2,1)S(1)} %get-tuple-element.37), channel_id=1, source_target_pairs={{0,6},{2,4},{4,2},{6,0},{1,7},{3,5},{5,3},{7,1},{8,14},{10,12},{12... | collective-permute-start | bytes 98312 | tf_op jit(solution)/shard_map/ppermute | solution.py:356

commit v4 on v3

--- a/solution.py
+++ b/solution.py
@@ -46,18 +46,16 @@
     return 0.5 * x * (1.0 + lax.erf(x * 0.7071067811865476))
 
 
-def split3(x):
+def split(x):
     hi = x.astype(bf16)
-    rest = x - hi.astype(f32)
-    mid = rest.astype(bf16)
-    return hi, mid, (rest - mid.astype(f32)).astype(bf16)
-
-
-def blank_kernel(out_ref):
+    return hi, (x - hi.astype(f32)).astype(bf16)
+
+
+def blank_kernel(pos_ref, out_ref):
     out_ref[...] = jnp.full(out_ref.shape, -1.0, f32)
 
 
-def pack_kernel(pos_ref, ids_ref, key_ref, dw_ref, blank_ref, tail_ref, w_ref, line):
+def pack_kernel(pos_ref, ids_ref, key_ref, blank_ref, tail_ref, line):
     section = pos_ref[3]
     keys, depth = key_ref.shape
     shard_rows, width = ids_ref.shape[1:]
@@ -67,10 +65,6 @@
     tail_ref[...] = jnp.zeros(tail_ref.shape, bf16)
     tail_ref[:, depth : depth + LANES] = line[...].astype(bf16)
     tail_ref[0 : keys // 2, 0:depth] = key_ref[pl.ds(pl.multiple_of(section * (keys // 2), keys // 2), keys // 2), :]
-    half = w_ref.shape[1]
-    lanes = pl.ds(pl.multiple_of(section * half, LANES), half)
-    for dy in range(7):
-        w_ref[dy * 7 : dy * 7 + 7, :] = dw_ref[dy, :, lanes].astype(f32)
 
 
 def join_kernel(*refs):
@@ -93,8 +87,9 @@
 
 
 def conv_kernel(geo, pos_ref, *refs):
-    shards, shard_rows, width, out_rows, first_lane = geo
-    blocks = refs[:shards]
+    order, shard_rows, width, out_rows, first_lane = geo
+    shards = len(order)
+    blocks = dict(zip(order, refs[:shards]))
     w_ref, taps, img_ref, xpad, wide = refs[shards:]
     chunk = taps.shape[1]
     row, first_row, col0 = pos_ref[0], pos_ref[1], pos_ref[2]
@@ -115,9 +110,11 @@
         for k in range(shards):
             value = blocks[k][0:pixels, lanes].astype(f32).reshape(shard_rows, width, LANES)
             xpad[pl.ds(3 + (row ^ k) * shard_rows, shard_rows), 8 : 8 + width, :] = value
-        for t in range(49):
-            w = w_ref[t : t + 1, pl.ds(pl.multiple_of(first_lane + g * LANES, LANES), LANES)]
-            wide[t] = jnp.broadcast_to(w, (8, LANES))
+        start = pos_ref[3] * (w_ref.shape[2] // 2) + first_lane + g * LANES
+        for dy in range(7):
+            w = w_ref[dy, :, pl.ds(pl.multiple_of(start, LANES), LANES)].astype(f32)
+            for dx in range(7):
+                wide[dy * 7 + dx] = jnp.broadcast_to(w[dx : dx + 1], (8, LANES))
 
         def strip(i, carry):
             top = first_row + i * step_rows
@@ -155,19 +152,25 @@
     width = half // chunks
     section = pos_ref[3]
     rows = slice(first, first + pixels)
-    values = [ref[rows, :] for ref in own + other]
-    mean = sum(jnp.sum(v, axis=1, keepdims=True) for v in values) * (1.0 / chans)
-    values = [v - mean for v in values]
-    spread = sum(jnp.sum(v * v, axis=1, keepdims=True) for v in values) * (1.0 / chans)
-    inv = lax.rsqrt(spread + ln_eps)
     gains = gain_ref[...].astype(f32).reshape(1, chans)
     scales = scale_ref[...].astype(f32).reshape(1, chans)
-    for c in range(chunks):
-        lanes = slice(c * width, (c + 1) * width)
-        for side, v in ((section, values[c]), (1 - section, values[chunks + c])):
-            start = c * width
-            gain = jnp.where(side == 0, gains[:, start : start + width], gains[:, half + start : half + start + width])
-            normed[pl.ds(side, 1), :, lanes] = (v * inv * gain).astype(bf16)[None]
+    gains = [gains[:, n * width : (n + 1) * width] for n in range(2 * chunks)]
+    gains_own = [jnp.where(section == 0, gains[c], gains[chunks + c]) for c in range(chunks)]
+    gains_other = [jnp.where(section == 0, gains[chunks + c], gains[c]) for c in range(chunks)]
+    block = 32
+    for r in range(pixels // block):
+        part = slice(first + r * block, first + (r + 1) * block)
+        values = [ref[part, :] for ref in own + other]
+        mean = sum(jnp.sum(v, axis=1, keepdims=True) for v in values) * (1.0 / chans)
+        values = [v - mean for v in values]
+        spread = sum(jnp.sum(v * v, axis=1, keepdims=True) for v in values) * (1.0 / chans)
+        inv = lax.rsqrt(spread + ln_eps)
+        values = [(v * inv * g).astype(bf16) for v, g in zip(values, gains_own + gains_other)]
+        to = slice(r * block, (r + 1) * block)
+        for c in range(chunks):
+            lanes = slice(c * width, (c + 1) * width)
+            normed[pl.ds(section, 1), to, lanes] = values[c][None]
+            normed[pl.ds(1 - section, 1), to, lanes] = values[chunks + c][None]
     step = 256
 
     def widen(i):
@@ -206,15 +209,13 @@
 
 
 def prep_kernel(geo, pos_ref, *refs):
-    shards, shard_rows, width, out_pixels, per_key, parts = geo
-    ids = refs[:shards]
-    hot_ref, keys_ref, flat = refs[shards:]
+    order, shard_rows, width, out_pixels, parts = geo
+    shards = len(order)
+    ids = [refs[order.index(k)] for k in range(shards)]
+    hot_ref, flat = refs[shards:]
     row, first_row = pos_ref[0], pos_ref[1]
     pixels = shard_rows * width
-    depth = keys_ref.shape[1]
-    for k in range(shards):
-        mine = slice(k * per_key // 2, (k + 1) * per_key // 2)
-        keys_ref[mine, :] = ids[k][pixels : pixels + per_key // 2, 0:depth]
+    depth = ids[0].shape[1] - LANES
     ids = [ref[pixels:, depth : depth + LANES].astype(f32) for ref in ids]
     image = row // parts
     flat[...] = jnp.full(flat.shape, -1.0, f32)
@@ -249,9 +250,18 @@
             hot_ref[tap * REG : (tap + 1) * REG, :] = jnp.where(region == line, 1.0, 0.0).astype(bf16)
 
 
+def unpack_kernel(geo, *refs):
+    order, pixels = geo
+    keys_ref = refs[-1]
+    count = keys_ref.shape[0] // len(order)
+    for k, ref in zip(order, refs):
+        keys_ref[k * count : (k + 1) * count, :] = ref[pixels : pixels + count, 0 : keys_ref.shape[1]]
+
+
 def owner_kernel(geo, pos_ref, *refs):
-    shards, shard_rows, pixels, images, batches, per_key = geo
-    ids = refs[:shards]
+    order, shard_rows, pixels, images, batches, per_key = geo
+    shards = len(order)
+    ids = [refs[order.index(k)] for k in range(shards)]
     owner_ref, partner_ref, pick_ref, own_ref = refs[shards:]
     row, batch, first_slot = pos_ref[0], pos_ref[4], pos_ref[5]
     depth = ids[0].shape[1] - LANES
@@ -312,21 +322,15 @@
 
 def keys_kernel(*refs):
     keys_ref, length_ref = refs[-2:]
-    start = 0
-    for ref in refs[:-2]:
-        keys_ref[start : start + ref.shape[0], :] = ref[...]
-        start += ref.shape[0]
-    keys = keys_ref[...].astype(f32)
-    square = keys * keys
-    hi = square.astype(bf16)
-    lo = (square - hi.astype(f32)).astype(bf16)
-    ones = jnp.ones((16, keys.shape[1]), bf16)
-    length_ref[...] = lax.rsqrt(dot_nt(ones, hi)[0:1] + dot_nt(ones, lo)[0:1] + norm_eps)
+    keys = jnp.concatenate([ref[...] for ref in refs[:-2]], axis=0).astype(f32).T
+    keys_ref[...] = keys.astype(bf16)
+    length_ref[...] = lax.rsqrt(jnp.sum(keys * keys, axis=0, keepdims=True) + norm_eps)
 
 
 def loss_kernel(geo, *refs):
-    shards, parts = geo
-    sums, row = refs[1 : shards + 1], refs[0][0]
+    order, parts = geo
+    shards = len(order)
+    sums, row = dict(zip(order, refs[1 : shards + 1])), refs[0][0]
     pick_ref, own_ref, keys_ref, length_ref, embed_ref, loss_ref, table = refs[shards + 1 :]
     if parts > 1:
         table[...] = jnp.zeros(table.shape, f32)
@@ -335,13 +339,13 @@
         value = sums[k][...].astype(f32)
         table[place, :] = value if parts == 1 else table[place, :] + value
     pick = pick_ref[...]
-    hi, mid, lo = split3(table[...])
-    ordered = dot(pick, hi) + dot(pick, mid) + dot(pick, lo)
+    hi, lo = split(table[...])
+    ordered = dot(pick, hi) + dot(pick, lo)
     unit = ordered * lax.rsqrt(jnp.sum(ordered * ordered, axis=1, keepdims=True) + norm_eps)
     embed_ref[...] = unit
     owned = unit.shape[0]
-    three = dot_nt(jnp.concatenate(split3(unit), axis=0), keys_ref[...])
-    logits = three[0:owned] + three[owned : 2 * owned] + three[2 * owned :]
+    both = dot(jnp.concatenate(split(unit), axis=0), keys_ref[...])
+    logits = both[0:owned] + both[owned:]
     logits = logits * (length_ref[...] / sharpness_divisor)
     total = jnp.log(jnp.sum(jnp.exp(logits), axis=1, keepdims=True))
     column = lax.broadcasted_iota(jnp.int32, logits.shape, 1).astype(f32)
@@ -398,34 +402,39 @@
     def after(here, *done):
         return lax.optimization_barrier((here, *done))[0]
 
-    (blank,) = call(
-        blank_kernel, [jax.ShapeDtypeStruct((tail, LANES), f32)], [], [], mib, 10**10, 10**4
-    )()
-    riders, weights = call(
-        pack_kernel,
-        [jax.ShapeDtypeStruct((tail, span), bf16), jax.ShapeDtypeStruct((49, half), f32)],
-        [SMEM] + [VMEM] * 4,
-        [pltpu.VMEM((tail, LANES), f32)],
-        mib,
-        0,
-        10**6,
-    )(spot, region_ids, key_embed, dw_kernel, blank)
-    got = []
+    parcels = []
     for c in range(CHUNKS):
         blocks = []
         for k in range(shards):
             place = ((row ^ k) // parts, 0, 0, section * half + c * span)
-            part = lax.dynamic_slice(features, place, (1, shard_rows, width, span)).reshape(pixels, span)
-            if c == CHUNKS - 1:
-                part = jnp.concatenate([part, riders], axis=0)
-            blocks.append(part)
-        got.append([blocks[0]] + [swap(blocks[k], "rows", k) for k in range(1, shards)])
+            part = lax.dynamic_slice(features, place, (1, shard_rows, width, span))
+            blocks.append(part.reshape(pixels, span))
+        parcels.append(blocks)
+    (blank,) = call(
+        blank_kernel, [jax.ShapeDtypeStruct((tail, LANES), f32)], [SMEM], [], mib, 10**10, 10**4
+    )(after(spot, *parcels[0]))
+    parcels[0] = after(parcels[0], blank)
+    (riders,) = call(
+        pack_kernel,
+        [jax.ShapeDtypeStruct((tail, span), bf16)],
+        [SMEM] + [VMEM] * 3,
+        [pltpu.VMEM((tail, LANES), f32)],
+        mib,
+        0,
+        10**6,
+    )(spot, region_ids, key_embed, blank)
+    parcels[-1] = [jnp.concatenate([part, riders], axis=0) for part in parcels[-1]]
+    got = [
+        [blocks[0]] + [swap(blocks[k], "rows", k) for k in range(1, shards)] for blocks in parcels
+    ]
+    order = sorted(range(shards), key=lambda k: (k > 0, -k.bit_count()))
+    last = [got[-1][k] for k in order]
 
     own, other, img = [], [], []
     for c in range(CHUNKS):
         here = after(spot, *own) if c else spot
         taps, image = call(
-            functools.partial(conv_kernel, (shards, shard_rows, width, out_rows, c * span)),
+            functools.partial(conv_kernel, (order, shard_rows, width, out_rows, c * span)),
             [
                 jax.ShapeDtypeStruct((out_pixels, span), f32),
                 jax.ShapeDtypeStruct((out_pixels, span), bf16),
@@ -438,23 +447,20 @@
             3 * mib,
             out_pixels * span * 98 * 100,
             out_pixels * span * 10,
-        )(here, *got[c], weights)
+        )(here, *[got[c][k] for k in order], dw_kernel)
         own.append(taps)
         img.append(image)
         other.append(swap(taps, "section", 1))
 
-    hot, keys = call(
-        functools.partial(prep_kernel, (shards, shard_rows, width, out_pixels, per_key, parts)),
-        [
-            jax.ShapeDtypeStruct((9 * REG, out_pixels), bf16),
-            jax.ShapeDtypeStruct((shards * per_key // 2, depth), bf16),
-        ],
-        [SMEM] + [VMEM] * shards,
-        [pltpu.VMEM((16, (shards + 2) * pixels), f32)],
-        2 * mib,
-        10**8,
-        10**6,
-    )(after(spot, *own), *got[-1])
+    (keys,) = call(
+        functools.partial(unpack_kernel, (order, pixels)),
+        [jax.ShapeDtypeStruct((shards * per_key // 2, depth), bf16)],
+        [VMEM] * shards,
+        [],
+        mib,
+        10**6,
+        10**6,
+    )(*after(last, *own))
     bits = [1 << n for n in reversed(range(batches.bit_length() - 1))]
     pieces = [keys, swap(keys, "batch", bits[0])]
 
@@ -462,7 +468,7 @@
     part_pixels = out_pixels // 2
     z, z_other = [], []
     for p in range(2):
-        here = after(spot, pieces[-1], *z) if p else after(spot, hot)
+        here = after(spot, pieces[-1], *z) if p else after(spot, keys)
         (mine,) = call(
             functools.partial(block_kernel, (p * part_pixels, part_pixels, CHUNKS)),
             [jax.ShapeDtypeStruct((part_pixels, chans), f32)],
@@ -487,6 +493,15 @@
         2 * part_pixels * hidden * chans,
         2 * hidden * chans,
     )(z[0], z_other[0], pe)
+    (hot,) = call(
+        functools.partial(prep_kernel, (order, shard_rows, width, out_pixels, parts)),
+        [jax.ShapeDtypeStruct((9 * REG, out_pixels), bf16)],
+        [SMEM] + [VMEM] * shards,
+        [pltpu.VMEM((16, (shards + 2) * pixels), f32)],
+        2 * mib,
+        10**8,
+        10**6,
+    )(after(spot, hid_a), *last)
     (pooled,) = call(
         project_kernel,
         [jax.ShapeDtypeStruct((REG, out_dim), f32)],
@@ -500,14 +515,14 @@
         4 * hidden * chans,
     )(z[1], z_other[1], hid_a, pe, pk, hot)
     pick, facts = call(
-        functools.partial(owner_kernel, (shards, shard_rows, pixels, images, batches, per_key)),
+        functools.partial(owner_kernel, (order, shard_rows, pixels, images, batches, per_key)),
         [jax.ShapeDtypeStruct((owned, slots), bf16), jax.ShapeDtypeStruct((owned, LANES), f32)],
         [SMEM] + [VMEM] * (shards + 2),
         [],
         2 * mib,
         10**8,
         10**6,
-    )(after(spot, pooled), *got[-1], owner_slot, partner)
+    )(after(spot, pooled), *last, owner_slot, partner)
     total, send = call(
         add_kernel,
         [jax.ShapeDtypeStruct((REG, out_dim), f32), jax.ShapeDtypeStruct((REG, out_dim), bf16)],
@@ -517,13 +532,13 @@
         10**5,
         10**5,
     )(pooled, swap(pooled, "section", 1))
-    sums = [total] + [swap(send, "rows", k) for k in range(1, shards)]
+    sums = [swap(send, "rows", k) if k else total for k in order]
     pieces[-1] = after(pieces[-1], pooled)
     pieces.append(swap(join(*pieces), "section", 1))
     count = sum(x.shape[0] for x in pieces)
     keys, length = call(
         keys_kernel,
-        [jax.ShapeDtypeStruct((count, depth), bf16), jax.ShapeDtypeStruct((1, count), f32)],
+        [jax.ShapeDtypeStruct((depth, count), bf16), jax.ShapeDtypeStruct((1, count), f32)],
         [VMEM] * len(pieces),
         [],
         4 * mib,
@@ -532,7 +547,7 @@
     )(*pieces)
 
     embed, loss = call(
-        functools.partial(loss_kernel, (shards, parts)),
+        functools.partial(loss_kernel, (order, parts)),
         [jax.ShapeDtypeStruct((owned, out_dim), f32), jax.ShapeDtypeStruct((1, owned), f32)],
         [SMEM] + [VMEM] * (shards + 4),
         [pltpu.VMEM((slots, out_dim), f32)],

time: 50.3 us -> 50.6 us (level)
  starting transfers between devices: 17.3 us -> 18.7 us
  local copies, waits for them, and re-layouts: 2.28 us -> 1.48 us
    ppermute x17, starting transfers between devices: 17.3 us -> 18.7 us  [swap(): lax.ppermute(x, axis, [(i, i ^ bit) for i in range(lax.axis_size(axis))])]
    unnamed x28, local copies, waits for them, and re-layouts: 0.88 us -> 0.09 us
    pallas_call x8 -> x9, Pallas kernels: 11.7 us -> 11.9 us  [the longest x2 6.96 us: body(): call(functools.partial(conv_kernel, (order, shard_rows, width, out_rows,...]
  transfers between devices with their start and end apart: 17 -> 17, of which waited for: 6 -> 6; matrix products, arithmetic and copies ran while one was open for 0% -> 0% of each run, Pallas kernels for 44% -> 43%
where the time goes in v4:
time: 50.6 us; the launch traced here: 50.4 us
  Pallas kernels  24.1 us (48%)
  starting transfers between devices  18.7 us (37%)
  waiting for transfers between devices  5.1 us (10%)
  local copies, waits for them, and re-layouts  1.48 us (3%)
  between operations  1.02 us (2%)
    ppermute x17, starting transfers between devices, swap(): lax.ppermute(x, axis, [(i, i ^ bit) for i in range(lax.axis_size(axis))])  18.7 us
    pallas_call x2, Pallas kernels, body(): call(functools.partial(block_kernel, (p * part_pixels, part_pixels, CHUNK...  8.29 us
    pallas_call x2, Pallas kernels, body(): call(functools.partial(conv_kernel, (order, shard_rows, width, out_rows,...  6.96 us
    ppermute x17, waiting for transfers between devices, swap(): lax.ppermute(x, axis, [(i, i ^ bit) for i in range(lax.axis_size(axis))])  5.1 us
    pallas_call x1, Pallas kernels, body(): call(project_kernel, [jax.ShapeDtypeStruct((REG, out_dim), f32)], [VMEM]...  2.86 us
    pallas_call x1, Pallas kernels, body(): call(functools.partial(loss_kernel, (order, parts)), [jax.ShapeDtypeStruc...  1.78 us
    dynamic_slice x1, local copies, waits for them, and re-layouts, body(): part = lax.dynamic_slice(features, place, (1, shard_rows, width, span))  1.3 us
  transfers between devices with their start and end apart: 17, of which 6 were waited for; matrix products, arithmetic and copies ran while one was open for 0% of the time, Pallas kernels for 43%

profile of v4, /device:TPU:0, one launch (start us, length us, event | category | flops | bytes accessed | tf_op | source)
XLA Modules:
  0.0 50.4 jit_solution(5545723560469039248)
XLA Ops:
  0.7 0.1 stack.20.pos_ref.refs_0_
  0.7 1.3 %constant_dynamic-slice_fusion = (bf16[1,4,32,384]{3,2,1,0:T(8,128)(2,1)S(1)}, bf16[1,4,32,384]{3,2,1,0:T(8,128)(2,1)S(1)}, bf16[1,4,32,384]{3,2,1,0:T(8,128)(2,...) fusion(bf16[4,4,32,1536]{3,2,1,0:T(8,128)(2,1)} %param.12, ...), kind=kLoop, calls=%fused_computation.4 | loop fusion | bytes 1572888 | tf_op jit(solution)/shard_map/dynamic_slice | solution.py:410
  2.1 0.0 copy-start.1
  2.1 0.0 copy-start.4
  2.1 0.0 copy-start.7
  2.1 0.5 %shard_map.131.blank_ref = f32[32,128]{1,0:T(8,128)S(1)} custom-call(s32[6]{0:T(128)S(1)} %stack.20.pos_ref.refs_0_), custom_call_target="tpu_custom_call" | custom-call | flops 10000000000 | bytes 10000 | tf_op jit(solution)/shard_map/pallas_call | solution.py:413
  2.6 4.0 %collective-permute-start.3 = (bf16[128,384]{1,0:T(8,128)(2,1)S(1)}, bf16[128,384]{1,0:T(8,128)(2,1)S(1)}, u32[]{:S(2)}, u32[]{:S(2)}) collective-permute-start(bf16[128,384]{1,0:T(8,128)(2,1)S(1)} %bitcast.26), channel_id=1, source_target_pairs={{0,6},{2,4},{4,2},{6,0},{1,7},{3,5},{5,3},{7,1},{8,14},{10,12},{12... | collective-permute-start | bytes 294920 | tf_op jit(solution)/shard_map/ppermute | solution.py:360
  6.6 0.5 %collective-permute-start.4 = (bf16[128,384]{1,0:T(8,128)(2,1)S(1)}, bf16[128,384]{1,0:T(8,128)(2,1)S(1)}, u32[]{:S(2)}, u32[]{:S(2)}) collective-permute-start(bf16[128,384]{1,0:T(8,128)(2,1)S(1)} %bitcast.25), channel_id=1, source_target_pairs={{0,2},{2,0},{4,6},{6,4},{1,3},{3,1},{5,7},{7,5},{8,10},{10,8},{12,... | collective-permute-start | bytes 294920 | tf_op jit(solution)/shard_map/ppermute | solution.py:360
  7.1 0.1 collective-permute-start.5
  7.2 0.6 %shard_map.132 = bf16[32,384]{1,0:T(8,128)(2,1)S(1)} custom-call(s32[6]{0:T(128)S(1)} %stack.20.pos_ref.refs_0_, s32[4,4,32]{2,1,0:T(4,128)S(1)} %copy-done.4, bf16[64,256]{1,0:T(8,128)(2,1)S(1)} %copy-done.1, f32[32,128]{1,0:T(8,128)S(1)} %shard_map.131.blank_ref), custom_call_target="tpu_custom_call" | custom-call | bytes 1000000 | tf_op jit(solution)/shard_map/pallas_call | solution.py:417
  7.8 0.0 slice-start.2
  7.8 0.1 pad_maximum_fusion
  7.9 2.9 %collective-permute-start = (bf16[160,384]{1,0:T(8,128)(2,1)S(1)}, bf16[160,384]{1,0:T(8,128)(2,1)S(1)}, u32[]{:S(2)}, u32[]{:S(2)}) collective-permute-start(bf16[160,384]{1,0:T(8,128)(2,1)S(1)} %get-tuple-element.65), channel_id=1, source_target_pairs={{0,6},{2,4},{4,2},{6,0},{1,7},{3,5},{5,3},{7,1},{8,14},{10,12},{12... | collective-permute-start | bytes 368648 | tf_op jit(solution)/shard_map/ppermute | solution.py:360
  10.8 0.5 %collective-permute-start.1 = (bf16[160,384]{1,0:T(8,128)(2,1)S(1)}, bf16[160,384]{1,0:T(8,128)(2,1)S(1)}, u32[]{:S(2)}, u32[]{:S(2)}) collective-permute-start(bf16[160,384]{1,0:T(8,128)(2,1)S(1)} %get-tuple-element.66), channel_id=1, source_target_pairs={{0,2},{2,0},{4,6},{6,4},{1,3},{3,1},{5,7},{7,5},{8,10},{10,8},{12,... | collective-permute-start | bytes 368648 | tf_op jit(solution)/shard_map/ppermute | solution.py:360
  11.3 0.0 collective-permute-done.3.refs_1_
  11.3 0.8 %collective-permute-start.2 = (bf16[160,384]{1,0:T(8,128)(2,1)S(1)}, bf16[160,384]{1,0:T(8,128)(2,1)S(1)}, u32[]{:S(2)}, u32[]{:S(2)}) collective-permute-start(bf16[160,384]{1,0:T(8,128)(2,1)S(1)} %get-tuple-element.64), channel_id=1, source_target_pairs={{0,4},{2,6},{4,0},{6,2},{1,5},{3,7},{5,1},{7,3},{8,12},{10,14},{12... | collective-permute-start | bytes 368648 | tf_op jit(solution)/shard_map/ppermute | solution.py:360
  12.2 0.5 %collective-permute-done.4.refs_2_ = bf16[128,384]{1,0:T(8,128)(2,1)S(1)} collective-permute-done((bf16[128,384]{1,0:T(8,128)(2,1)S(1)}, bf16[128,384]{1,0:T(8,128)(2,1)S(1)}, u32[]{:S(2)}, u32[]{:S(2)}) %collective-permute-start.4) | collective-permute-done | bytes 98336 | tf_op jit(solution)/shard_map/ppermute | solution.py:360
  12.7 1.2 %collective-permute-done.5.refs_3_ = bf16[128,384]{1,0:T(8,128)(2,1)S(1)} collective-permute-done((bf16[128,384]{1,0:T(8,128)(2,1)S(1)}, bf16[128,384]{1,0:T(8,128)(2,1)S(1)}, u32[]{:S(2)}, u32[]{:S(2)}) %collective-permute-start.5) | collective-permute-done | bytes 98336 | tf_op jit(solution)/shard_map/ppermute | solution.py:360
  13.9 0.0 copy-done.7
  13.9 3.5 %shard_map.133 = (f32[512,384]{1,0:T(8,128)S(1)}, bf16[512,384]{1,0:T(8,128)(2,1)S(1)}) custom-call(s32[6]{0:T(128)S(1)} %stack.20.pos_ref.refs_0_, bf16[128,384]{1,0:T(8,128)(2,1)S(1)} %bitcast.19, bf16[128,384]{1,0:T(8,128)(2,1)S(1)} %collective-permute-done.3.refs_1_, bf16[128,384]{1,0:T(8,128)(2,1)S(1)} %collective-permute-done.4.refs_2_, ...), custom_call_target="tpu_custom_call" | custom-call | flops 1926758400 | bytes 1966080 | tf_op jit(solution)/shard_map/pallas_call | solution.py:436
  17.4 0.1 collective-permute-start.7
  17.4 0.0 collective-permute-done.refs_1_
  17.5 0.0 collective-permute-done.1.refs_2_
  17.5 0.0 collective-permute-done.2.refs_3_
  17.5 0.0 slice-start.1
  17.5 0.0 copy-start.2
  17.5 0.0 copy-start.3
  17.5 3.5 %shard_map.134 = (f32[512,384]{1,0:T(8,128)S(1)}, bf16[512,384]{1,0:T(8,128)(2,1)S(1)}) custom-call(s32[6]{0:T(128)S(1)} %stack.20.pos_ref.refs_0_, bf16[160,384]{1,0:T(8,128)(2,1)S(1)} %get-tuple-element.37.refs_0_, bf16[160,384]{1,0:T(8,128)(2,1)S(1)} %collective-permute-done.refs_1_, bf16[160,384]{1,0:T(8,128)(2,1)S(1)} %collective-permute-done.1.refs_2_, ...), custom_call_target="tpu_custom_call" | custom-call | flops 1926758400 | bytes 1966080 | tf_op jit(solution)/shard_map/pallas_call | solution.py:436
  21.0 0.5 %collective-permute-start.8 = (f32[512,384]{1,0:T(8,128)S(1)}, f32[512,384]{1,0:T(8,128)S(1)}, u32[]{:S(2)}, u32[]{:S(2)}) collective-permute-start(f32[512,384]{1,0:T(8,128)S(1)} %get-tuple-element.36.refs_1_), channel_id=1, source_target_pairs={{0,1},{1,0},{2,3},{3,2},{4,5},{5,4},{6,7},{7,6},{8,9},{9,8},{10,11... | collective-permute-start | bytes 2359304 | tf_op jit(solution)/shard_map/ppermute | solution.py:360
  21.5 2.8 %collective-permute-start.6 = (bf16[128,256]{1,0:T(8,128)(2,1)S(1)}, bf16[128,256]{1,0:T(8,128)(2,1)S(1)}, u32[]{:S(2)}, u32[]{:S(2)}) collective-permute-start(bf16[128,256]{1,0:T(8,128)(2,1)S(1)} %shard_map.135.refs_0_), channel_id=1, source_target_pairs={{0,16},{8,24},{16,0},{24,8},{1,17},{9,25},{17,1},{25,9},{2,18},{10... | collective-permute-start | bytes 196616 | tf_op jit(solution)/shard_map/ppermute | solution.py:360
  24.4 0.0 collective-permute-done.7.refs_2_
  24.4 0.0 collective-permute-done.8.refs_3_
  24.4 0.0 slice-done.2
  24.4 0.0 slice-start.4
  24.5 4.1 %shard_map.136.z_ref = f32[256,1536]{1,0:T(8,128)S(1)} custom-call(s32[6]{0:T(128)S(1)} %stack.20.pos_ref.refs_0_, f32[512,384]{1,0:T(8,128)S(1)} %get-tuple-element.34.refs_0_, f32[512,384]{1,0:T(8,128)S(1)} %get-tuple-element.36.refs_1_, f32[512,384]{1,0:T(8,128)S(1)} %collective-permute-done.7.refs_2_, f32[512,384]{1,0:T(8,128)S(1)} %collective-permute-done.8.refs_3_, ...), custom_call_target="tpu_custom_call" | custom-call | flops 2415919104 | bytes 9437184 | tf_op jit(solution)/shard_map/pallas_call | solution.py:472
  28.6 0.0 slice-start.5
  28.6 0.1 collective-permute-start.10
  28.7 0.0 collective-permute-done.6.refs_1_
  28.7 0.0 copy-start
  28.7 4.1 %shard_map.137.z_ref = f32[256,1536]{1,0:T(8,128)S(1)} custom-call(s32[6]{0:T(128)S(1)} %stack.20.pos_ref.refs_0_, f32[512,384]{1,0:T(8,128)S(1)} %get-tuple-element.34.refs_0_, f32[512,384]{1,0:T(8,128)S(1)} %get-tuple-element.36.refs_1_, f32[512,384]{1,0:T(8,128)S(1)} %collective-permute-done.7.refs_2_, f32[512,384]{1,0:T(8,128)S(1)} %collective-permute-done.8.refs_3_, ...), custom_call_target="tpu_custom_call" | custom-call | flops 2415919104 | bytes 9437184 | tf_op jit(solution)/shard_map/pallas_call | solution.py:472
  32.9 0.5 %collective-permute-start.9 = (f32[256,1536]{1,0:T(8,128)S(1)}, f32[256,1536]{1,0:T(8,128)S(1)}, u32[]{:S(2)}, u32[]{:S(2)}) collective-permute-start(f32[256,1536]{1,0:T(8,128)S(1)} %shard_map.137.z_ref), channel_id=1, source_target_pairs={{0,1},{1,0},{2,3},{3,2},{4,5},{5,4},{6,7},{7,6},{8,9},{9,8},{10,11... | collective-permute-start | bytes 4718600 | tf_op jit(solution)/shard_map/ppermute | solution.py:360
  33.4 1.6 %collective-permute-start.15 = (bf16[256,256]{1,0:T(8,128)(2,1)S(1)}, bf16[256,256]{1,0:T(8,128)(2,1)S(1)}, u32[]{:S(2)}, u32[]{:S(2)}) collective-permute-start(bf16[256,256]{1,0:T(8,128)(2,1)S(1)} %shard_map.143), channel_id=1, source_target_pairs={{0,8},{8,0},{16,24},{24,16},{1,9},{9,1},{17,25},{25,17},{2,10},{10... | collective-permute-start | bytes 393224 | tf_op jit(solution)/shard_map/ppermute | solution.py:360
  35.1 0.0 collective-permute-done.10.other_ref
  35.1 1.0 %shard_map.138.first_ref = bf16[256,1024]{1,0:T(8,128)(2,1)S(1)} custom-call(f32[256,1536]{1,0:T(8,128)S(1)} %shard_map.136.z_ref, f32[256,1536]{1,0:T(8,128)S(1)} %collective-permute-done.10.other_ref, bf16[1536,1024]{1,0:T(8,128)(2,1)S(1)} %copy-done), custom_call_target="tpu_custom_call" | custom-call | flops 805306368 | bytes 3145728 | tf_op jit(solution)/shard_map/pallas_call | solution.py:487
  36.1 0.9 %shard_map.139.hot_ref = bf16[576,512]{1,0:T(8,128)(2,1)S(1)} custom-call(s32[6]{0:T(128)S(1)} %stack.20.pos_ref.refs_0_, bf16[160,384]{1,0:T(8,128)(2,1)S(1)} %get-tuple-element.37.refs_0_, bf16[160,384]{1,0:T(8,128)(2,1)S(1)} %collective-permute-done.refs_1_, bf16[160,384]{1,0:T(8,128)(2,1)S(1)} %collective-permute-done.1.refs_2_, ...), custom_call_target="tpu_custom_call" | custom-call | flops 100000000 | bytes 1000000 | tf_op jit(solution)/shard_map/pallas_call | solution.py:496
  36.9 0.0 copy-start.5
  36.9 0.0 copy-start.6
  36.9 0.0 collective-permute-done.9.other_ref
  37.0 0.0 slice-done.4
  37.0 2.9 %shard_map.140.a_ref = f32[64,256]{1,0:T(8,128)S(1)} custom-call(f32[256,1536]{1,0:T(8,128)S(1)} %shard_map.137.z_ref, f32[256,1536]{1,0:T(8,128)S(1)} %collective-permute-done.9.other_ref, bf16[256,1024]{1,0:T(8,128)(2,1)S(1)} %shard_map.138.first_ref, bf16[1536,1024]{1,0:T(8,128)(2,1)S(1)} %copy-done, bf16[9,1024,256]{2,1,0:T(8,128)(2,1)S(1)} %bitcast.18, ...), custom_call_target="tpu_custom_call" | custom-call | flops 2013265920 | bytes 6291456 | tf_op jit(solution)/shard_map/pallas_call | solution.py:505
  39.9 0.0 collective-permute-done.15.refs_2_
  39.9 0.1 collective-permute-start.16
  40.0 0.5 collective-permute-start.11
  40.5 1.0 %shard_map.142 = (bf16[64,256]{1,0:T(8,128)(2,1)S(1)}, f32[64,128]{1,0:T(8,128)S(1)}) custom-call(s32[6]{0:T(128)S(1)} %stack.20.pos_ref.refs_0_, bf16[160,384]{1,0:T(8,128)(2,1)S(1)} %get-tuple-element.37.refs_0_, bf16[160,384]{1,0:T(8,128)(2,1)S(1)} %collective-permute-done.refs_1_, bf16[160,384]{1,0:T(8,128)(2,1)S(1)} %collective-permute-done.1.refs_2_, ...), custom_call_target="tpu_custom_call" | custom-call | flops 100000000 | bytes 1000000 | tf_op jit(solution)/shard_map/pallas_call | solution.py:517
  41.4 0.1 collective-permute-done.11.b_ref
  41.6 2.6 %collective-permute-start.12 = (bf16[64,256]{1,0:T(8,128)(2,1)S(1)}, bf16[64,256]{1,0:T(8,128)(2,1)S(1)}, u32[]{:S(2)}, u32[]{:S(2)}) collective-permute-start(bf16[64,256]{1,0:T(8,128)(2,1)S(1)} %get-tuple-element.47), channel_id=1, source_target_pairs={{0,6},{2,4},{4,2},{6,0},{1,7},{3,5},{5,3},{7,1},{8,14},{10,12},{12... | collective-permute-start | bytes 98312 | tf_op jit(solution)/shard_map/ppermute | solution.py:360
  44.2 0.5 %collective-permute-start.13 = (bf16[64,256]{1,0:T(8,128)(2,1)S(1)}, bf16[64,256]{1,0:T(8,128)(2,1)S(1)}, u32[]{:S(2)}, u32[]{:S(2)}) collective-permute-start(bf16[64,256]{1,0:T(8,128)(2,1)S(1)} %get-tuple-element.47), channel_id=1, source_target_pairs={{0,2},{2,0},{4,6},{6,4},{1,3},{3,1},{5,7},{7,5},{8,10},{10,8},{12,... | collective-permute-start | bytes 98312 | tf_op jit(solution)/shard_map/ppermute | solution.py:360
  44.7 0.4 collective-permute-start.14
  45.2 0.0 collective-permute-done.16.refs_3_
  45.2 0.2 shard_map.145
  45.4 1.1 %collective-permute-done.12.refs_2_ = bf16[64,256]{1,0:T(8,128)(2,1)S(1)} collective-permute-done((bf16[64,256]{1,0:T(8,128)(2,1)S(1)}, bf16[64,256]{1,0:T(8,128)(2,1)S(1)}, u32[]{:S(2)}, u32[]{:S(2)}) %collective-permute-start.12) | collective-permute-done | bytes 32800 | tf_op jit(solution)/shard_map/ppermute | solution.py:360
  46.5 1.6 %collective-permute-done.13.refs_3_ = bf16[64,256]{1,0:T(8,128)(2,1)S(1)} collective-permute-done((bf16[64,256]{1,0:T(8,128)(2,1)S(1)}, bf16[64,256]{1,0:T(8,128)(2,1)S(1)}, u32[]{:S(2)}, u32[]{:S(2)}) %collective-permute-start.13) | collective-permute-done | bytes 32800 | tf_op jit(solution)/shard_map/ppermute | solution.py:360
  48.1 0.5 %collective-permute-done.14.refs_4_ = bf16[64,256]{1,0:T(8,128)(2,1)S(1)} collective-permute-done((bf16[64,256]{1,0:T(8,128)(2,1)S(1)}, bf16[64,256]{1,0:T(8,128)(2,1)S(1)}, u32[]{:S(2)}, u32[]{:S(2)}) %collective-permute-start.14) | collective-permute-done | bytes 32800 | tf_op jit(solution)/shard_map/ppermute | solution.py:360
  48.6 1.8 %shard_map.146 = (f32[64,256]{1,0:T(8,128)}, f32[1,64]{1,0:T(1,128)}) custom-call(s32[6]{0:T(128)S(1)} %stack.20.pos_ref.refs_0_, f32[64,256]{1,0:T(8,128)S(1)} %get-tuple-element.46.refs_1_, bf16[64,256]{1,0:T(8,128)(2,1)S(1)} %collective-permute-done.12.refs_2_, bf16[64,256]{1,0:T(8,128)(2,1)S(1)} %collective-permute-done.13.refs_3_, ...), custom_call_target="tpu_custom_call" | custom-call | flops 100000000 | bytes 1000000 | tf_op jit(solution)/shard_map/pallas_call | solution.py:549
  (20 shorter events, 0.1 us)
Async XLA Ops:
  2.1 5.2 %copy-start.1 = (bf16[64,256]{1,0:T(8,128)(2,1)S(1)}, bf16[64,256]{1,0:T(8,128)(2,1)}, u32[]{:S(2)}) copy-start(bf16[64,256]{1,0:T(8,128)(2,1)} %key_ref.1) | copy-start | bytes 98308
  2.1 5.2 %copy-start.4 = (s32[4,4,32]{2,1,0:T(4,128)S(1)}, s32[4,4,32]{2,1,0:T(4,128)}, u32[]{:S(2)}) copy-start(s32[4,4,32]{2,1,0:T(4,128)} %ids_ref.1) | copy-start | bytes 6148
  2.1 11.8 %copy-start.7 = (bf16[7,7,1536]{2,1,0:T(8,128)(2,1)S(1)}, bf16[7,7,1536]{2,1,0:T(8,128)(2,1)}, u32[]{:S(2)}) copy-start(bf16[7,7,1536]{2,1,0:T(8,128)(2,1)} %refs_4_.4) | copy-start | bytes 451588
  2.6 8.7 %collective-permute-start.3 = (bf16[128,384]{1,0:T(8,128)(2,1)S(1)}, bf16[128,384]{1,0:T(8,128)(2,1)S(1)}, u32[]{:S(2)}, u32[]{:S(2)}) collective-permute-start(bf16[128,384]{1,0:T(8,128)(2,1)S(1)} %bitcast.26), channel_id=1, source_target_pairs={{0,6},{2,4},{4,2},{6,0},{1,7},{3,5},{5,3},{7,1},{8,14},{10,12},{12... | collective-permute-start | bytes 294920 | tf_op jit(solution)/shard_map/ppermute | solution.py:360
  6.6 6.1 %collective-permute-start.4 = (bf16[128,384]{1,0:T(8,128)(2,1)S(1)}, bf16[128,384]{1,0:T(8,128)(2,1)S(1)}, u32[]{:S(2)}, u32[]{:S(2)}) collective-permute-start(bf16[128,384]{1,0:T(8,128)(2,1)S(1)} %bitcast.25), channel_id=1, source_target_pairs={{0,2},{2,0},{4,6},{6,4},{1,3},{3,1},{5,7},{7,5},{8,10},{10,8},{12,... | collective-permute-start | bytes 294920 | tf_op jit(solution)/shard_map/ppermute | solution.py:360
  7.1 6.7 %collective-permute-start.5 = (bf16[128,384]{1,0:T(8,128)(2,1)S(1)}, bf16[128,384]{1,0:T(8,128)(2,1)S(1)}, u32[]{:S(2)}, u32[]{:S(2)}) collective-permute-start(bf16[128,384]{1,0:T(8,128)(2,1)S(1)} %bitcast.24), channel_id=1, source_target_pairs={{0,4},{2,6},{4,0},{6,2},{1,5},{3,7},{5,1},{7,3},{8,12},{10,14},{12... | collective-permute-start | bytes 294920 | tf_op jit(solution)/shard_map/ppermute | solution.py:360
  7.8 16.6 %slice-start.2 = ((s8[4718592]{0:T(1024)(128)(4,1)}), s8[524288]{0:T(1024)(128)(4,1)S(1)}, s32[]{:S(2)}) async-start(s8[4718592]{0:T(1024)(128)(4,1)} %bitcast.15), calls=%async_computation.2 | async-start | bytes 1048576
  7.9 9.6 %collective-permute-start = (bf16[160,384]{1,0:T(8,128)(2,1)S(1)}, bf16[160,384]{1,0:T(8,128)(2,1)S(1)}, u32[]{:S(2)}, u32[]{:S(2)}) collective-permute-start(bf16[160,384]{1,0:T(8,128)(2,1)S(1)} %get-tuple-element.65), channel_id=1, source_target_pairs={{0,6},{2,4},{4,2},{6,0},{1,7},{3,5},{5,3},{7,1},{8,14},{10,12},{12... | collective-permute-start | bytes 368648 | tf_op jit(solution)/shard_map/ppermute | solution.py:360
  10.8 6.7 %collective-permute-start.1 = (bf16[160,384]{1,0:T(8,128)(2,1)S(1)}, bf16[160,384]{1,0:T(8,128)(2,1)S(1)}, u32[]{:S(2)}, u32[]{:S(2)}) collective-permute-start(bf16[160,384]{1,0:T(8,128)(2,1)S(1)} %get-tuple-element.66), channel_id=1, source_target_pairs={{0,2},{2,0},{4,6},{6,4},{1,3},{3,1},{5,7},{7,5},{8,10},{10,8},{12,... | collective-permute-start | bytes 368648 | tf_op jit(solution)/shard_map/ppermute | solution.py:360
  11.3 13.1 %slice-start.3 = ((s8[4718592]{0:T(1024)(128)(4,1)}), s8[4194304]{0:T(1024)(128)(4,1)S(1)}, s32[]{:S(2)}) async-start(s8[4718592]{0:T(1024)(128)(4,1)} %bitcast.15), calls=%async_computation.3 | async-start | bytes 8388608
  11.3 6.1 %collective-permute-start.2 = (bf16[160,384]{1,0:T(8,128)(2,1)S(1)}, bf16[160,384]{1,0:T(8,128)(2,1)S(1)}, u32[]{:S(2)}, u32[]{:S(2)}) collective-permute-start(bf16[160,384]{1,0:T(8,128)(2,1)S(1)} %get-tuple-element.64), channel_id=1, source_target_pairs={{0,4},{2,6},{4,0},{6,2},{1,5},{3,7},{5,1},{7,3},{8,12},{10,14},{12... | collective-permute-start | bytes 368648 | tf_op jit(solution)/shard_map/ppermute | solution.py:360
  13.9 10.5 %slice-start = ((s8[4718592]{0:T(1024)(128)(4,1)}), s8[4194304]{0:T(1024)(128)(4,1)S(1)}, s32[]{:S(2)}) async-start(s8[4718592]{0:T(1024)(128)(4,1)} %bitcast.13), calls=%async_computation | async-start | bytes 8388608
  17.4 7.0 %collective-permute-start.7 = (f32[512,384]{1,0:T(8,128)S(1)}, f32[512,384]{1,0:T(8,128)S(1)}, u32[]{:S(2)}, u32[]{:S(2)}) collective-permute-start(f32[512,384]{1,0:T(8,128)S(1)} %get-tuple-element.34.refs_0_), channel_id=1, source_target_pairs={{0,1},{1,0},{2,3},{3,2},{4,5},{5,4},{6,7},{7,6},{8,9},{9,8},{10,11... | collective-permute-start | bytes 2359304 | tf_op jit(solution)/shard_map/ppermute | solution.py:360
  17.5 6.9 %slice-start.1 = ((s8[4718592]{0:T(1024)(128)(4,1)}), s8[524288]{0:T(1024)(128)(4,1)S(1)}, s32[]{:S(2)}) async-start(s8[4718592]{0:T(1024)(128)(4,1)} %bitcast.13), calls=%async_computation.1 | async-start | bytes 1048576
  17.5 6.9 %copy-start.2 = (bf16[1536]{0:T(1024)(128)(2,1)S(1)}, bf16[1536]{0:T(1024)(128)(2,1)}, u32[]{:S(2)}) copy-start(bf16[1536]{0:T(1024)(128)(2,1)} %refs_6_.3) | copy-start | bytes 9220
  17.5 6.9 %copy-start.3 = (bf16[1536]{0:T(1024)(128)(2,1)S(1)}, bf16[1536]{0:T(1024)(128)(2,1)}, u32[]{:S(2)}) copy-start(bf16[1536]{0:T(1024)(128)(2,1)} %refs_7_.3) | copy-start | bytes 9220
  21.0 3.4 %collective-permute-start.8 = (f32[512,384]{1,0:T(8,128)S(1)}, f32[512,384]{1,0:T(8,128)S(1)}, u32[]{:S(2)}, u32[]{:S(2)}) collective-permute-start(f32[512,384]{1,0:T(8,128)S(1)} %get-tuple-element.36.refs_1_), channel_id=1, source_target_pairs={{0,1},{1,0},{2,3},{3,2},{4,5},{5,4},{6,7},{7,6},{8,9},{9,8},{10,11... | collective-permute-start | bytes 2359304 | tf_op jit(solution)/shard_map/ppermute | solution.py:360
  21.5 7.2 %collective-permute-start.6 = (bf16[128,256]{1,0:T(8,128)(2,1)S(1)}, bf16[128,256]{1,0:T(8,128)(2,1)S(1)}, u32[]{:S(2)}, u32[]{:S(2)}) collective-permute-start(bf16[128,256]{1,0:T(8,128)(2,1)S(1)} %shard_map.135.refs_0_), channel_id=1, source_target_pairs={{0,16},{8,24},{16,0},{24,8},{1,17},{9,25},{17,1},{25,9},{2,18},{10... | collective-permute-start | bytes 196616 | tf_op jit(solution)/shard_map/ppermute | solution.py:360
  24.4 12.5 %slice-start.4 = ((s8[4718592]{0:T(1024)(128)(4,1)}), s8[4194304]{0:T(1024)(128)(4,1)S(1)}, s32[]{:S(2)}) async-start(s8[4718592]{0:T(1024)(128)(4,1)} %bitcast.17), calls=%async_computation.4 | async-start | bytes 8388608
  28.6 8.4 %slice-start.5 = ((s8[4718592]{0:T(1024)(128)(4,1)}), s8[524288]{0:T(1024)(128)(4,1)S(1)}, s32[]{:S(2)}) async-start(s8[4718592]{0:T(1024)(128)(4,1)} %bitcast.17), calls=%async_computation.5 | async-start | bytes 1048576
  28.6 6.4 %collective-permute-start.10 = (f32[256,1536]{1,0:T(8,128)S(1)}, f32[256,1536]{1,0:T(8,128)S(1)}, u32[]{:S(2)}, u32[]{:S(2)}) collective-permute-start(f32[256,1536]{1,0:T(8,128)S(1)} %shard_map.136.z_ref), channel_id=1, source_target_pairs={{0,1},{1,0},{2,3},{3,2},{4,5},{5,4},{6,7},{7,6},{8,9},{9,8},{10,11... | collective-permute-start | bytes 4718600 | tf_op jit(solution)/shard_map/ppermute | solution.py:360
  28.7 6.4 %copy-start = (bf16[1536,1024]{1,0:T(8,128)(2,1)S(1)}, bf16[1536,1024]{1,0:T(8,128)(2,1)}, u32[]{:S(2)}) copy-start(bf16[1536,1024]{1,0:T(8,128)(2,1)} %pe_ref.3) | copy-start | bytes 9437188
  32.9 4.1 %collective-permute-start.9 = (f32[256,1536]{1,0:T(8,128)S(1)}, f32[256,1536]{1,0:T(8,128)S(1)}, u32[]{:S(2)}, u32[]{:S(2)}) collective-permute-start(f32[256,1536]{1,0:T(8,128)S(1)} %shard_map.137.z_ref), channel_id=1, source_target_pairs={{0,1},{1,0},{2,3},{3,2},{4,5},{5,4},{6,7},{7,6},{8,9},{9,8},{10,11... | collective-permute-start | bytes 4718600 | tf_op jit(solution)/shard_map/ppermute | solution.py:360
  33.4 6.4 %collective-permute-start.15 = (bf16[256,256]{1,0:T(8,128)(2,1)S(1)}, bf16[256,256]{1,0:T(8,128)(2,1)S(1)}, u32[]{:S(2)}, u32[]{:S(2)}) collective-permute-start(bf16[256,256]{1,0:T(8,128)(2,1)S(1)} %shard_map.143), channel_id=1, source_target_pairs={{0,8},{8,0},{16,24},{24,16},{1,9},{9,1},{17,25},{25,17},{2,10},{10... | collective-permute-start | bytes 393224 | tf_op jit(solution)/shard_map/ppermute | solution.py:360
  36.9 3.5 %copy-start.5 = (s32[4,64]{1,0:T(4,128)S(1)}, s32[4,64]{1,0:T(4,128)}, u32[]{:S(2)}) copy-start(s32[4,64]{1,0:T(4,128)} %refs_5_.1) | copy-start | bytes 3076
  36.9 3.5 %copy-start.6 = (s32[1,256]{1,0:T(1,128)S(1)}, s32[1,256]{1,0:T(1,128)}, u32[]{:S(2)}) copy-start(s32[1,256]{1,0:T(1,128)} %refs_4_.5) | copy-start | bytes 3076
  39.9 5.3 %collective-permute-start.16 = (bf16[512,256]{1,0:T(8,128)(2,1)S(1)}, bf16[512,256]{1,0:T(8,128)(2,1)S(1)}, u32[]{:S(2)}, u32[]{:S(2)}) collective-permute-start(bf16[512,256]{1,0:T(8,128)(2,1)S(1)} %shard_map.144), channel_id=1, source_target_pairs={{0,1},{1,0},{2,3},{3,2},{4,5},{5,4},{6,7},{7,6},{8,9},{9,8},{10,11... | collective-permute-start | bytes 786440 | tf_op jit(solution)/shard_map/ppermute | solution.py:360
  40.0 1.6 %collective-permute-start.11 = (f32[64,256]{1,0:T(8,128)S(1)}, f32[64,256]{1,0:T(8,128)S(1)}, u32[]{:S(2)}, u32[]{:S(2)}) collective-permute-start(f32[64,256]{1,0:T(8,128)S(1)} %shard_map.140.a_ref), channel_id=1, source_target_pairs={{0,1},{1,0},{2,3},{3,2},{4,5},{5,4},{6,7},{7,6},{8,9},{9,8},{10,11... | collective-permute-start | bytes 196616 | tf_op jit(solution)/shard_map/ppermute | solution.py:360
  41.6 4.9 %collective-permute-start.12 = (bf16[64,256]{1,0:T(8,128)(2,1)S(1)}, bf16[64,256]{1,0:T(8,128)(2,1)S(1)}, u32[]{:S(2)}, u32[]{:S(2)}) collective-permute-start(bf16[64,256]{1,0:T(8,128)(2,1)S(1)} %get-tuple-element.47), channel_id=1, source_target_pairs={{0,6},{2,4},{4,2},{6,0},{1,7},{3,5},{5,3},{7,1},{8,14},{10,12},{12... | collective-permute-start | bytes 98312 | tf_op jit(solution)/shard_map/ppermute | solution.py:360
  44.2 3.9 %collective-permute-start.13 = (bf16[64,256]{1,0:T(8,128)(2,1)S(1)}, bf16[64,256]{1,0:T(8,128)(2,1)S(1)}, u32[]{:S(2)}, u32[]{:S(2)}) collective-permute-start(bf16[64,256]{1,0:T(8,128)(2,1)S(1)} %get-tuple-element.47), channel_id=1, source_target_pairs={{0,2},{2,0},{4,6},{6,4},{1,3},{3,1},{5,7},{7,5},{8,10},{10,8},{12,... | collective-permute-start | bytes 98312 | tf_op jit(solution)/shard_map/ppermute | solution.py:360
  44.7 3.9 %collective-permute-start.14 = (bf16[64,256]{1,0:T(8,128)(2,1)S(1)}, bf16[64,256]{1,0:T(8,128)(2,1)S(1)}, u32[]{:S(2)}, u32[]{:S(2)}) collective-permute-start(bf16[64,256]{1,0:T(8,128)(2,1)S(1)} %get-tuple-element.47), channel_id=1, source_target_pairs={{0,4},{2,6},{4,0},{6,2},{1,5},{3,7},{5,1},{7,3},{8,12},{10,14},{12... | collective-permute-start | bytes 98312 | tf_op jit(solution)/shard_map/ppermute | solution.py:360
